TPU v7x, 256 devices: a whole 4x4x8 slice. The times are simulated.
256 devices in a mesh: dp: 16 (over x, y_hi, core), seq: 16 (over z, y_lo).
Axes of the slice: x: 4, y: 4 (y_hi: 2, y_lo: 2; y = y_hi * 2 + y_lo), z: 8, core: 2. Of those that a mesh axis runs over, the one named last changes fastest.
Arguments:
- normed_input: bfloat16 [32768, 4096], P(('dp', 'seq')), may hold values from -6 to 6
- queries: bfloat16 [32768, 2048], P(('dp', 'seq')), may hold values from -22 to 22
- rotated_key_rows: bfloat16 [32768, 2048], P(('dp', 'seq')), may hold values from -22 to 22
- frozen_value_rows: bfloat16 [32768, 2048], P(('dp', 'seq')), may hold values from -6 to 6
- cotangent: bfloat16 [32768, 2048], P(('dp', 'seq')), may hold values from -24 to 24
- adapter_down_weight: bfloat16 [4096, 128], replicated, may hold values from -0.09375 to 0.09375
- adapter_up_weight: bfloat16 [128, 2048], replicated, may hold values from -0.5 to 0.5
- document_lengths: int32 [16, 16], P('dp'), may hold values from 1 to 256, 2048 in all within a row
- versions: int32 [16, 16], P('dp'), may hold values from 0 to 3
Outputs:
- query_gradient: bfloat16 [32768, 2048], P(('dp', 'seq'))
- key_gradient: bfloat16 [32768, 2048], P(('dp', 'seq'))
- value_gradient: bfloat16 [32768, 2048], P(('dp', 'seq'))
- down_weight_gradient: float32 [4096, 128], P('dp')
- up_weight_gradient: float32 [128, 2048], P(None, 'dp')
Inputs may be any that keep to these rules, and one draw needn't show every extreme that they name: `document_lengths`: each row sums to 2048, and every row has a document of exactly 256 tokens.
All inputs are finite; a program needn't handle non-finite values.
Results may differ from a plain program's by a relative error of at most 0.02.
Values may be sent and summed in bfloat16 or wider, within the bound.
No kernel may reach another device: no remote copies, remote signals or barrier semaphores. Data moves between devices by JAX's collectives and lax.ppermute only.
A program may use at most 128 MiB of HBM per device.

v0:
```python
import math

import jax
import jax.numpy as jnp
from jax import lax
from jax.sharding import PartitionSpec as P

HEAD_DIM = 128
VERSIONS = 4


adapter_scale = 0.5
masked_score = -1e30


def passed_along(block, axis, distance):
    devices = range(lax.axis_size(axis))
    route = [(i - distance, i) for i in devices if i - distance in devices]
    return lax.ppermute(block, axis, route)


def document_ids(lengths, positions):
    doc_ends = jnp.cumsum(lengths)
    inside = (positions >= 0) & (positions < doc_ends[-1])
    doc_index = jnp.sum((positions[:, None] >= doc_ends[None, :]).astype(jnp.int32), axis=1)
    return jnp.where(inside, doc_index, -1)


def token_weights(doc_index, doc_versions):
    doc_weight = jnp.exp2((doc_versions - (VERSIONS - 1)).astype(jnp.float32))
    choose = doc_index[:, None] == jnp.arange(doc_versions.shape[0], dtype=jnp.int32)[None, :]
    return jnp.sum(jnp.where(choose, doc_weight[None, :], jnp.float32(0.0)), axis=1)


def attend(query_block, key_window, value_window, grad_block, query_doc, key_doc):
    total_row_count = query_block.shape[0]
    width = query_block.shape[1]
    head_count = width // HEAD_DIM
    score_scale = 1.0 / math.sqrt(HEAD_DIM)
    query_heads = query_block.reshape(total_row_count, head_count, HEAD_DIM)
    key_heads = key_window.reshape(-1, head_count, HEAD_DIM)
    value_heads = value_window.reshape(-1, head_count, HEAD_DIM)
    grad_heads = grad_block.reshape(total_row_count, head_count, HEAD_DIM)
    scores = (
        jnp.einsum("qhd,khd->hqk", query_heads, key_heads, preferred_element_type=jnp.float32)
        * score_scale
    )
    same_doc = (query_doc[:, None] == key_doc[None, :])[None]
    scores = jnp.where(same_doc, scores, masked_score)
    row_max = jnp.max(scores, axis=-1, keepdims=True)
    exponent = jnp.exp(scores - row_max)
    prob = (exponent / jnp.sum(exponent, axis=-1, keepdims=True)).astype(jnp.bfloat16)
    attended = jnp.einsum("hqk,khd->qhd", prob, value_heads, preferred_element_type=jnp.float32)
    dprob = jnp.einsum("qhd,khd->hqk", grad_heads, value_heads, preferred_element_type=jnp.float32)
    row_delta = jnp.einsum("qhd,qhd->hq", grad_heads.astype(jnp.float32), attended)
    dscore = (prob.astype(jnp.float32) * (dprob - row_delta[:, :, None]) * score_scale).astype(
        jnp.bfloat16
    )
    gradient_row_block = jnp.einsum(
        "hqk,khd->qhd", dscore, key_heads, preferred_element_type=jnp.float32
    ).reshape(total_row_count, width)
    grad_keys = jnp.einsum(
        "hqk,qhd->khd", dscore, query_heads, preferred_element_type=jnp.float32
    ).reshape(-1, width)
    grad_values = jnp.einsum(
        "hqk,qhd->khd", prob, grad_heads, preferred_element_type=jnp.float32
    ).reshape(-1, width)
    return (gradient_row_block, grad_keys.astype(jnp.bfloat16), grad_values.astype(jnp.bfloat16))


def per_device(
    normed_input,
    queries,
    rotated_key_rows,
    frozen_value_rows,
    cotangent,
    adapter_down_weight,
    adapter_up_weight,
    document_lengths,
    versions,
):
    total_row_count = queries.shape[0]
    sequence_count = lax.axis_size("seq")
    replica_count = lax.axis_size("dp")
    shard_index = lax.axis_index("seq")
    window_reach = max(1, sequence_count // 8)
    window_rows = (2 * window_reach + 1) * total_row_count
    lengths = document_lengths[0]
    adapter_value = jnp.dot(
        normed_input, adapter_down_weight, preferred_element_type=jnp.float32
    ).astype(jnp.bfloat16)
    adapted_values = (
        frozen_value_rows.astype(jnp.float32)
        + adapter_scale
        * jnp.dot(adapter_value, adapter_up_weight, preferred_element_type=jnp.float32)
    ).astype(jnp.bfloat16)
    paired = jnp.stack([rotated_key_rows, adapted_values])
    blocks = []
    for offset in range(-window_reach, window_reach + 1):
        if offset == 0:
            blocks.append(paired)
        else:
            blocks.append(passed_along(paired, "seq", -offset))
    window = jnp.concatenate(blocks, axis=1)
    query_pos = shard_index * total_row_count + jnp.arange(total_row_count, dtype=jnp.int32)
    key_pos = (shard_index - window_reach) * total_row_count + jnp.arange(
        window_rows, dtype=jnp.int32
    )
    query_doc = document_ids(lengths, query_pos)
    key_doc = document_ids(lengths, key_pos)
    weights = token_weights(query_doc, versions[0])
    scaled = (weights[:, None] * cotangent.astype(jnp.float32)).astype(jnp.bfloat16)
    gradient_row_block, grad_keys, grad_values = attend(
        queries, window[0], window[1], scaled, query_doc, key_doc
    )
    grad_stack = jnp.stack([grad_keys, grad_values])
    own_start = window_reach * total_row_count
    summed = grad_stack[:, own_start : own_start + total_row_count].astype(jnp.float32)
    for offset in range(-window_reach, window_reach + 1):
        if offset != 0:
            block_start = (offset + window_reach) * total_row_count
            block = grad_stack[:, block_start : block_start + total_row_count]
            summed = summed + passed_along(block, "seq", offset).astype(jnp.float32)
    key_gradient = summed[0].astype(jnp.bfloat16)
    value_gradient = summed[1].astype(jnp.bfloat16)
    gradient_norm_value = adapter_scale * (
        1.0 / math.sqrt(total_row_count * sequence_count * replica_count)
    )
    returned_rows = jnp.dot(
        value_gradient, adapter_up_weight.T, preferred_element_type=jnp.float32
    ).astype(jnp.bfloat16)
    contract_rows = (((0,), (0,)), ((), ()))
    part_a = (
        lax.dot_general(
            normed_input, returned_rows, contract_rows, preferred_element_type=jnp.float32
        )
        * gradient_norm_value
    )
    part_b = (
        lax.dot_general(
            adapter_value, value_gradient, contract_rows, preferred_element_type=jnp.float32
        )
        * gradient_norm_value
    )
    down_gradient_total, up_gradient_total = lax.psum((part_a, part_b), ("dp", "seq"))
    replica_index = lax.axis_index("dp")
    down_gradient_share = part_a.shape[0] // replica_count
    up_gradient_share = part_b.shape[1] // replica_count
    down_weight_gradient = lax.dynamic_slice_in_dim(
        down_gradient_total, replica_index * down_gradient_share, down_gradient_share, 0
    )
    up_weight_gradient = lax.dynamic_slice_in_dim(
        up_gradient_total, replica_index * up_gradient_share, up_gradient_share, 1
    )
    return (
        gradient_row_block.astype(jnp.bfloat16),
        key_gradient,
        value_gradient,
        down_weight_gradient,
        up_weight_gradient,
    )


def solution(mesh):
    in_specs = (
        P(("dp", "seq"), None),
        P(("dp", "seq"), None),
        P(("dp", "seq"), None),
        P(("dp", "seq"), None),
        P(("dp", "seq"), None),
        P(),
        P(),
        P("dp", None),
        P("dp", None),
    )
    out_specs = (
        P(("dp", "seq"), None),
        P(("dp", "seq"), None),
        P(("dp", "seq"), None),
        P("dp", None),
        P(None, "dp"),
    )
    return jax.shard_map(
        per_device, mesh=mesh, in_specs=in_specs, out_specs=out_specs, check_vma=False
    )
```

profile of v0, /device:TPU:2, one launch (start us, length us, event | category | flops | bytes accessed | tf_op | source)
XLA Modules:
  0.0 449.1 jit_solution(10838808331830134251)
XLA Ops:
  7.3 1.1 copy-done
  8.4 1.6 convolution_convert_fusion.4
  10.0 1.5 fusion.8
  11.6 1.1 pad_maximum_fusion.1
  12.6 4.8 %collective-permute-start = (bf16[2,128,2048]{2,1,0:T(8,128)(2,1)}, bf16[2,128,2048]{2,1,0:T(8,128)(2,1)}, u32[]{:S(2)}, u32[]{:S(2)}) collective-permute-start(bf16[2,128,2048]{2,1,0:T(8,128)(2,1)} %pad_maximum_fusion.1), channel_id=1, source_target_pairs={{0,2},{1,3},{2,4},{3,5},{4,6},{5,7},{6,8},{7,9},{8,10},{9,11},{10,... | collective-permute-start | bytes 3145736 | tf_op jit(solution)/shard_map/ppermute | solution.py:19
  17.4 4.5 collective-permute-start.1
  21.9 1.3 collective-permute-start.2
  23.2 1.3 collective-permute-start.3
  25.3 0.7 and_select_fusion.1
  26.6 0.7 and_select_fusion
  27.4 2.0 copy.76
  29.5 1.4 copy.71
  31.3 7.8 %collective-permute-done = bf16[2,128,2048]{2,1,0:T(8,128)(2,1)} collective-permute-done((bf16[2,128,2048]{2,1,0:T(8,128)(2,1)}, bf16[2,128,2048]{2,1,0:T(8,128)(2,1)}, u32[]{:S(2)}, u32[]{:S(2)}) %collective-permute-start) | collective-permute-done | bytes 1048608 | tf_op jit(solution)/shard_map/ppermute | solution.py:19
  39.1 1.3 constant_dynamic-update-slice_fusion.4
  40.5 25.3 %collective-permute-done.1 = bf16[2,128,2048]{2,1,0:T(8,128)(2,1)} collective-permute-done((bf16[2,128,2048]{2,1,0:T(8,128)(2,1)}, bf16[2,128,2048]{2,1,0:T(8,128)(2,1)}, u32[]{:S(2)}, u32[]{:S(2)}) %collective-permute-start.1) | collective-permute-done | bytes 1048608 | tf_op jit(solution)/shard_map/ppermute | solution.py:19
  65.8 1.3 constant_dynamic-update-slice_fusion.3
  67.2 1.3 constant_dynamic-update-slice_fusion.1
  68.6 1.7 collective-permute-done.3
  70.2 1.3 constant_dynamic-update-slice_fusion
  71.6 2.9 fusion.20
  74.5 4.4 copy.75
  78.9 4.5 copy.77
  83.4 6.1 %fusion.21 = (f32[16,128]{1,0:T(8,128)S(1)}, f32[16,128,640]{1,2,0:T(8,128)}) fusion(pred[128,640]{0,1:T(8,128)(4,1)S(1)} %broadcast_compare_fusion, bf16[640,16,128]{0,2,1:T(8,128)(2,1)} %bitcast.75, bf16[128,16,128]{0,2,1:T(8,128)(2,1)S(1)} %bitcast.82), kind=kOutput, calls=%fused_computation.65 | convolution fusion | flops 340787840 | bytes 8478720 | tf_op jit(solution)/shard_map/sub | solution.py:51
  89.5 3.1 divide_convert_fusion
  92.6 2.6 convolution_convert_fusion
  95.2 0.9 fusion.10
  96.1 1.5 multiply_convert_fusion
  97.6 2.6 convolution_convert_fusion.1
  100.2 4.5 %copy.60 = bf16[1,640,2048]{2,1,0:T(8,128)(2,1)} copy(bf16[1,640,2048]{1,2,0:T(8,128)(2,1)} %bitcast.78) | data formatting | bytes 5242880 | tf_op jit(solution)/shard_map/convert_element_type | solution.py:68
  104.7 4.5 %copy.61 = bf16[1,640,2048]{2,1,0:T(8,128)(2,1)} copy(bf16[1,640,2048]{1,2,0:T(8,128)(2,1)} %bitcast.77) | data formatting | bytes 5242880 | tf_op jit(solution)/shard_map/convert_element_type | solution.py:68
  109.2 2.5 fusion.13
  111.7 4.2 collective-permute-start.7
  115.8 1.7 collective-permute-start.6
  117.5 1.3 collective-permute-start.5
  118.8 1.6 collective-permute-start.4
  120.5 16.3 %collective-permute-done.7 = bf16[2,128,2048]{2,1,0:T(8,128)(2,1)S(1)} collective-permute-done((bf16[2,128,2048]{2,1,0:T(8,128)(2,1)S(1)}, bf16[2,128,2048]{2,1,0:T(8,128)(2,1)S(1)}, u32[]{:S(2)}, u32[]{:S(2)}) %collective-permute-start.7) | collective-permute-done | bytes 1048608 | tf_op jit(solution)/shard_map/ppermute | solution.py:19
  136.7 24.1 %collective-permute-done.6 = bf16[2,128,2048]{2,1,0:T(8,128)(2,1)S(1)} collective-permute-done((bf16[2,128,2048]{2,1,0:T(8,128)(2,1)S(1)}, bf16[2,128,2048]{2,1,0:T(8,128)(2,1)S(1)}, u32[]{:S(2)}, u32[]{:S(2)}) %collective-permute-start.6) | collective-permute-done | bytes 1048608 | tf_op jit(solution)/shard_map/ppermute | solution.py:19
  160.9 8.4 %collective-permute-done.4 = bf16[2,128,2048]{2,1,0:T(8,128)(2,1)S(1)} collective-permute-done((bf16[2,128,2048]{2,1,0:T(8,128)(2,1)S(1)}, bf16[2,128,2048]{2,1,0:T(8,128)(2,1)S(1)}, u32[]{:S(2)}, u32[]{:S(2)}) %collective-permute-start.4) | collective-permute-done | bytes 1048608 | tf_op jit(solution)/shard_map/ppermute | solution.py:19
  169.3 1.0 add_convert_fusion
  170.3 0.9 slice_bitcast_fusion
  171.2 2.4 fusion.1
  173.6 1.3 convolution_multiply_fusion.1
  174.9 3.4 convolution_convert_fusion.2
  178.3 1.0 copy.62
  179.3 259.8 %all-reduce.3.cloned.1.call-done = (f32[4096,128]{0,1:T(8,128)}, f32[128,2048]{1,0:T(8,128)}) async-done(((f32[4096,128]{0,1:T(8,128)}, f32[128,2048]{1,0:T(8,128)}), (f32[4096,128]{0,1:T(8,128)}, f32[128,2048]{1,0:T(8,128)})) %all-reduce.3.cloned.1.call-update) | async-done | bytes 3145744 | tf_op jit(solution)/shard_map/psum | solution.py:145
  439.1 0.9 constant_dynamic-slice_fusion.1
  440.0 0.8 copy.63
  440.8 1.5 constant_dynamic-slice_fusion
  (47 shorter events, 2.2 us)
Async XLA Ops:
  7.2 1.2 copy-start
  7.2 4.4 copy-start.7
  7.2 17.3 %copy-start.12 = (s32[1,16]{1,0:T(1,128)S(1)}, s32[1,16]{1,0:T(1,128)}, u32[]{:S(2)}) copy-start(s32[1,16]{1,0:T(1,128)} %param.16) | copy-start | bytes 196
  7.2 18.0 %copy-start.13 = (s32[1,16]{1,0:T(1,128)S(1)}, s32[1,16]{1,0:T(1,128)}, u32[]{:S(2)}) copy-start(s32[1,16]{1,0:T(1,128)} %param.17) | copy-start | bytes 196
  7.2 18.9 %copy-start.11 = (bf16[128,2048]{1,0:T(8,128)(2,1)S(1)}, bf16[128,2048]{1,0:T(8,128)(2,1)}, u32[]{:S(2)}) copy-start(bf16[128,2048]{1,0:T(8,128)(2,1)} %param.13) | copy-start | bytes 1572868
  7.2 431.9 %all-reduce.3.cloned.1.call-start = ((), (), s32[]{:S(2)}) async-start(), calls=%async_computation | async-start | bytes 6291456 | tf_op jit(solution)/shard_map/psum | solution.py:145
  12.6 26.5 %collective-permute-start = (bf16[2,128,2048]{2,1,0:T(8,128)(2,1)}, bf16[2,128,2048]{2,1,0:T(8,128)(2,1)}, u32[]{:S(2)}, u32[]{:S(2)}) collective-permute-start(bf16[2,128,2048]{2,1,0:T(8,128)(2,1)} %pad_maximum_fusion.1), channel_id=1, source_target_pairs={{0,2},{1,3},{2,4},{3,5},{4,6},{5,7},{6,8},{7,9},{8,10},{9,11},{10,... | collective-permute-start | bytes 3145736 | tf_op jit(solution)/shard_map/ppermute | solution.py:19
  17.4 48.4 %collective-permute-start.1 = (bf16[2,128,2048]{2,1,0:T(8,128)(2,1)}, bf16[2,128,2048]{2,1,0:T(8,128)(2,1)}, u32[]{:S(2)}, u32[]{:S(2)}) collective-permute-start(bf16[2,128,2048]{2,1,0:T(8,128)(2,1)} %pad_maximum_fusion.1), channel_id=1, source_target_pairs={{0,1},{1,2},{2,3},{3,4},{4,5},{5,6},{6,7},{7,8},{8,9},{9,10},{10,1... | collective-permute-start | bytes 3145736 | tf_op jit(solution)/shard_map/ppermute | solution.py:19
  21.9 45.3 %collective-permute-start.2 = (bf16[2,128,2048]{2,1,0:T(8,128)(2,1)}, bf16[2,128,2048]{2,1,0:T(8,128)(2,1)}, u32[]{:S(2)}, u32[]{:S(2)}) collective-permute-start(bf16[2,128,2048]{2,1,0:T(8,128)(2,1)} %pad_maximum_fusion.1), channel_id=1, source_target_pairs={{1,0},{2,1},{3,2},{4,3},{5,4},{6,5},{7,6},{8,7},{9,8},{10,9},{11,1... | collective-permute-start | bytes 3145736 | tf_op jit(solution)/shard_map/ppermute | solution.py:19
  23.2 47.1 %collective-permute-start.3 = (bf16[2,128,2048]{2,1,0:T(8,128)(2,1)}, bf16[2,128,2048]{2,1,0:T(8,128)(2,1)}, u32[]{:S(2)}, u32[]{:S(2)}) collective-permute-start(bf16[2,128,2048]{2,1,0:T(8,128)(2,1)} %pad_maximum_fusion.1), channel_id=1, source_target_pairs={{2,0},{3,1},{4,2},{5,3},{6,4},{7,5},{8,6},{9,7},{10,8},{11,9},{12,... | collective-permute-start | bytes 3145736 | tf_op jit(solution)/shard_map/ppermute | solution.py:19
  30.9 36.3 %copy-start.8 = (bf16[128,2048]{1,0:T(8,128)(2,1)S(1)}, bf16[128,2048]{1,0:T(8,128)(2,1)}, u32[]{:S(2)}) copy-start(bf16[128,2048]{1,0:T(8,128)(2,1)} %param.11) | copy-start | bytes 1572868
  78.9 4.5 copy-start.10
  92.6 2.6 copy-start.4
  92.6 2.6 copy-start.6
  97.6 2.6 copy-start.3
  109.2 60.1 %copy-start.1 = (bf16[1,640,2048]{2,1,0:T(8,128)(2,1)S(1)}, bf16[1,640,2048]{2,1,0:T(8,128)(2,1)}, u32[]{:S(2)}) copy-start(bf16[1,640,2048]{2,1,0:T(8,128)(2,1)} %copy.60) | copy-start | bytes 7864324
  109.2 60.1 %copy-start.2 = (bf16[1,640,2048]{2,1,0:T(8,128)(2,1)S(1)}, bf16[1,640,2048]{2,1,0:T(8,128)(2,1)}, u32[]{:S(2)}) copy-start(bf16[1,640,2048]{2,1,0:T(8,128)(2,1)} %copy.61) | copy-start | bytes 7864324
  111.7 25.1 %collective-permute-start.7 = (bf16[2,128,2048]{2,1,0:T(8,128)(2,1)S(1)}, bf16[2,128,2048]{2,1,0:T(8,128)(2,1)S(1)}, u32[]{:S(2)}, u32[]{:S(2)}) collective-permute-start(bf16[2,128,2048]{2,1,0:T(8,128)(2,1)S(1)} %get-tuple-element.24), channel_id=1, source_target_pairs={{0,2},{1,3},{2,4},{3,5},{4,6},{5,7},{6,8},{7,9},{8,10},{9,11},{10,... | collective-permute-start | bytes 3145736 | tf_op jit(solution)/shard_map/ppermute | solution.py:19
  115.8 45.0 %collective-permute-start.6 = (bf16[2,128,2048]{2,1,0:T(8,128)(2,1)S(1)}, bf16[2,128,2048]{2,1,0:T(8,128)(2,1)S(1)}, u32[]{:S(2)}, u32[]{:S(2)}) collective-permute-start(bf16[2,128,2048]{2,1,0:T(8,128)(2,1)S(1)} %get-tuple-element.25), channel_id=1, source_target_pairs={{0,1},{1,2},{2,3},{3,4},{4,5},{5,6},{6,7},{7,8},{8,9},{9,10},{10,1... | collective-permute-start | bytes 3145736 | tf_op jit(solution)/shard_map/ppermute | solution.py:19
  117.5 43.3 %collective-permute-start.5 = (bf16[2,128,2048]{2,1,0:T(8,128)(2,1)S(1)}, bf16[2,128,2048]{2,1,0:T(8,128)(2,1)S(1)}, u32[]{:S(2)}, u32[]{:S(2)}) collective-permute-start(bf16[2,128,2048]{2,1,0:T(8,128)(2,1)S(1)} %get-tuple-element.23), channel_id=1, source_target_pairs={{1,0},{2,1},{3,2},{4,3},{5,4},{6,5},{7,6},{8,7},{9,8},{10,9},{11,1... | collective-permute-start | bytes 3145736 | tf_op jit(solution)/shard_map/ppermute | solution.py:19
  118.8 52.3 %copy-start.9 = (bf16[128,2048]{1,0:T(8,128)(2,1)S(1)}, bf16[128,2048]{1,0:T(8,128)(2,1)}, u32[]{:S(2)}) copy-start(bf16[128,2048]{1,0:T(8,128)(2,1)} %param.15) | copy-start | bytes 1572868
  118.8 50.4 %collective-permute-start.4 = (bf16[2,128,2048]{2,1,0:T(8,128)(2,1)S(1)}, bf16[2,128,2048]{2,1,0:T(8,128)(2,1)S(1)}, u32[]{:S(2)}, u32[]{:S(2)}) collective-permute-start(bf16[2,128,2048]{2,1,0:T(8,128)(2,1)S(1)} %get-tuple-element.22), channel_id=1, source_target_pairs={{2,0},{3,1},{4,2},{5,3},{6,4},{7,5},{8,6},{9,7},{10,8},{11,9},{12,... | collective-permute-start | bytes 3145736 | tf_op jit(solution)/shard_map/ppermute | solution.py:19
  171.1 3.7 copy-start.5
Sparse Core Ops, SparseCore 0:
  175.0 264.0 all-reduce.2
where the time goes:
time: 450 us; the launch traced here: 449 us
  waiting for transfers between devices  343 us (76%)
  local copies, waits for them, and re-layouts  37 us (8%)
  matrix products  23.8 us (5%)
  starting transfers between devices  20.6 us (5%)
  between operations  14.4 us (3%)
  other arithmetic  9.88 us (2%)
    psum x1, waiting for transfers between devices, per_device(): lax.psum((part_a, part_b), ('dp', 'seq'))  260 us
    ppermute x8, waiting for transfers between devices, passed_along(): return lax.ppermute(block, axis, route)  83.6 us
    ppermute x8, starting transfers between devices, passed_along(): return lax.ppermute(block, axis, route)  20.6 us
  transfers between devices with their start and end apart: 9, of which 7 were waited for; matrix products, arithmetic and copies ran while one was open for 3% of the time, Pallas kernels for 0%

commit v1 on v0

v1 whole, which is shorter than its diff:
```python
import functools
import math

import jax
import jax.numpy as jnp
from jax import lax
from jax.experimental import pallas as pl
from jax.experimental.pallas import tpu as pltpu
from jax.sharding import PartitionSpec as P

HEAD_DIM = 128
VERSIONS = 4

adapter_scale = 0.5
masked_score = -1e30
VMEM_LIMIT = 48 * 1024 * 1024
HEADS_PER_STEP = 2


def contract(a, b, dim_a, dim_b):
    return lax.dot_general(
        a, b, (((dim_a,), (dim_b,)), ((), ())), preferred_element_type=jnp.float32
    )


def shifted(block, axis, target):
    count = lax.axis_size(axis)
    route = [(i, target(i)) for i in range(count) if 0 <= target(i) < count]
    return lax.ppermute(block, axis, route)


def prepare_kernel(place, x, down, up, frozen, keys, queries, grads, pair_out, ring_out, query_out, value_own, low_out, x_out):
    half = keys.shape[1] // 2
    y = place[0]
    own = pl.multiple_of(y * half, half)
    other = pl.multiple_of((1 - y) * half, half)
    low = contract(x[...], down[...], 1, 0).astype(jnp.bfloat16)
    low_out[...] = low
    pair_out[:, :half] = keys[:, pl.ds(other, half)]
    ring_out[:, :half] = keys[:, pl.ds(own, half)]
    query_out[:, :half] = queries[:, pl.ds(other, half)]
    query_out[:, half:] = grads[:, pl.ds(other, half)]
    share = x.shape[1] // x_out.shape[0]
    for i in range(x_out.shape[0]):
        x_out[i] = x[:, i * share : (i + 1) * share]

    def values(start):
        lifted = contract(low, up[:, pl.ds(start, half)], 1, 0)
        base = frozen[:, pl.ds(start, half)].astype(jnp.float32)
        return (base + adapter_scale * lifted).astype(jnp.bfloat16)

    pair_out[:, half : 2 * half] = values(other)
    pair_out[:, 2 * half :] = low
    mine = values(own)
    ring_out[:, half:] = mine
    value_own[...] = mine


def prepare(place, x, down, up, frozen, keys, queries, grads, replicas):
    rows, width = keys.shape
    rank = down.shape[1]
    half = width // 2
    kind = jnp.bfloat16
    shapes = [
        (rows, width + rank),
        (rows, width),
        (rows, width),
        (rows, half),
        (rows, rank),
        (replicas, rows, x.shape[1] // replicas),
    ]
    vmem = pl.BlockSpec(memory_space=pltpu.VMEM)
    return pl.pallas_call(
        prepare_kernel,
        out_shape=[jax.ShapeDtypeStruct(s, kind) for s in shapes],
        in_specs=[pl.BlockSpec(memory_space=pltpu.SMEM)] + [vmem] * 7,
        out_specs=[vmem] * 6,
        compiler_params=pltpu.CompilerParams(vmem_limit_bytes=VMEM_LIMIT),
    )(place, x, down, up, frozen, keys, queries, grads)


def attend_kernel(
    place, lengths, versions,
    q_own, q_pair, g_own, g_pair,
    k_own, k_pair, k_prev, k_prev2, k_next, k_next2,
    v_own, v_pair, v_prev, v_prev2, v_next, v_next2,
    l_own, l_pair, l_prev, l_prev2, l_next, l_next2,
    up,
    dq_own, dq_pair, mid, prev, nxt, back, up_part,
    bias, weight, low,
):
    rows = q_own.shape[0]
    documents = lengths.shape[1]
    step = pl.program_id(0)
    y, z = place[0], place[1]
    own_base = (2 * z + y) * rows
    pair_base = (2 * z + 1 - y) * rows
    bases = [own_base, pair_base]
    for shift in (-2 * rows, 2 * rows):
        bases += [own_base + shift, pair_base + shift]

    @pl.when(step == 0)
    def _():
        ends, total = [], jnp.int32(0)
        for j in range(documents):
            total = total + lengths[0, j]
            ends.append(total)
        for b in range(2):
            pos = lax.broadcasted_iota(jnp.int32, (8, rows), 1) + bases[b]
            first = jnp.zeros_like(pos)
            last = jnp.zeros_like(pos)
            for j in range(documents):
                first = jnp.where(pos >= ends[j], ends[j], first)
            for j in reversed(range(documents)):
                last = jnp.where(pos < ends[j], ends[j], last)
            first, last = first[:1], last[:1]
            for c in range(6):
                key_pos = lax.broadcasted_iota(jnp.int32, (rows, rows), 0) + bases[c]
                inside = (key_pos >= first) & (key_pos < last)
                bias[c * rows : (c + 1) * rows, b * rows : (b + 1) * rows] = jnp.where(
                    inside, jnp.float32(0.0), jnp.float32(masked_score)
                )
            row_pos = lax.broadcasted_iota(jnp.int32, (rows, HEAD_DIM), 0) + bases[b]
            scale = jnp.zeros((rows, HEAD_DIM), jnp.float32)
            for j in range(documents):
                level = lax.shift_left(jnp.int32(1), versions[0, j]).astype(jnp.float32)
                level = level * (2.0 ** (1 - VERSIONS))
                begin = ends[j - 1] if j > 0 else 0
                scale = jnp.where(row_pos >= begin, level, scale)
            weight[b * rows : (b + 1) * rows, :] = scale
        for c, ref in enumerate((l_own, l_pair, l_prev, l_prev2, l_next, l_next2)):
            low[c * rows : (c + 1) * rows, :] = ref[...]
        back[...] = jnp.zeros_like(back)

    score_scale = 1.0 / math.sqrt(HEAD_DIM)
    log2e = 1.4426950408889634
    for h in range(HEADS_PER_STEP):
        cols = slice(h * HEAD_DIM, (h + 1) * HEAD_DIM)
        gather = lambda *refs: jnp.concatenate([r[:, cols] for r in refs], axis=0)
        q = gather(q_own, q_pair)
        k = gather(k_own, k_pair, k_prev, k_prev2, k_next, k_next2)
        v = gather(v_own, v_pair, v_prev, v_prev2, v_next, v_next2)
        g = (weight[...] * gather(g_own, g_pair).astype(jnp.float32)).astype(jnp.bfloat16)
        s = contract(k, q, 1, 1) * (score_scale * log2e) + bias[...]
        e = jnp.exp2(s - jnp.max(s, axis=0, keepdims=True))
        p = (e * (1.0 / jnp.sum(e, axis=0, keepdims=True))).astype(jnp.bfloat16)
        dv = contract(p, g, 1, 0)
        mid[1, :, cols] = dv[: 2 * rows]
        dv_small = dv.astype(jnp.bfloat16)
        prev[1, :, cols] = dv_small[2 * rows : 4 * rows]
        nxt[1, :, cols] = dv_small[4 * rows :]
        back[...] += contract(dv_small, up[:, cols], 1, 1)
        up_part[h] = contract(low[...], dv_small, 0, 0)
        dp = contract(v, g, 1, 1)
        wide = p.astype(jnp.float32)
        delta = jnp.sum(wide * dp, axis=0, keepdims=True)
        ds = (wide * (dp - delta) * score_scale).astype(jnp.bfloat16)
        dk = contract(ds, q, 1, 0)
        mid[0, :, cols] = dk[: 2 * rows]
        prev[0, :, cols] = dk[2 * rows : 4 * rows].astype(jnp.bfloat16)
        nxt[0, :, cols] = dk[4 * rows :].astype(jnp.bfloat16)
        dq = contract(ds, k, 0, 0).astype(jnp.bfloat16)
        dq_own[:, cols] = dq[:rows]
        dq_pair[:, cols] = dq[rows:]


def attend(place, lengths, versions, queries, grads, keys, value_own, low, up, pair, pair_q, prev, prev2, nxt, nxt2):
    rows, width = queries.shape
    rank = low.shape[1]
    half = width // 2
    heads = half // HEAD_DIM
    block = HEADS_PER_STEP * HEAD_DIM
    steps = heads // HEADS_PER_STEP
    whole = lambda h, pc, *_: (0, pc[0] * steps + h)
    at = lambda first: pl.BlockSpec((rows, block), lambda h, *_: (0, first + h))
    mine = pl.BlockSpec((rows, block), whole)
    low_at = lambda b: pl.BlockSpec((rows, rank), lambda h, *_: (0, b))
    tail = width // rank
    kind = jnp.bfloat16
    in_specs = [
        mine, at(0), mine, at(steps),
        mine, at(0), at(0), at(0), at(0), at(0),
        at(0), at(steps), at(steps), at(steps), at(steps), at(steps),
        low_at(0), low_at(tail), low_at(tail), low_at(tail + 1), low_at(tail), low_at(tail + 1),
        pl.BlockSpec((rank, block), whole),
    ]
    operands = (
        queries, pair_q, grads, pair_q,
        keys, pair, prev, prev2, nxt, nxt2,
        value_own, pair, prev, prev2, nxt, nxt2,
        low, pair, prev2, prev2, nxt2, nxt2,
        up,
    )
    out_shape = [
        jax.ShapeDtypeStruct((rows, half), kind),
        jax.ShapeDtypeStruct((rows, half), kind),
        jax.ShapeDtypeStruct((2, 2 * rows, half), jnp.float32),
        jax.ShapeDtypeStruct((2, 2 * rows, half), kind),
        jax.ShapeDtypeStruct((2, 2 * rows, half), kind),
        jax.ShapeDtypeStruct((6 * rows, rank), jnp.float32),
        jax.ShapeDtypeStruct((heads, rank, HEAD_DIM), jnp.float32),
    ]
    triple = pl.BlockSpec((2, 2 * rows, block), lambda h, *_: (0, 0, h))
    out_specs = [
        at(0), at(0), triple, triple, triple,
        pl.BlockSpec((6 * rows, rank), lambda h, *_: (0, 0)),
        pl.BlockSpec((HEADS_PER_STEP, rank, HEAD_DIM), lambda h, *_: (h, 0, 0)),
    ]
    pairs = 12 * rows * rows * heads
    return pl.pallas_call(
        attend_kernel,
        grid_spec=pltpu.PrefetchScalarGridSpec(
            num_scalar_prefetch=3,
            grid=(steps,),
            in_specs=in_specs,
            out_specs=out_specs,
            scratch_shapes=[
                pltpu.VMEM((6 * rows, 2 * rows), jnp.float32),
                pltpu.VMEM((2 * rows, HEAD_DIM), jnp.float32),
                pltpu.VMEM((6 * rows, rank), kind),
            ],
        ),
        out_shape=out_shape,
        compiler_params=pltpu.CompilerParams(
            vmem_limit_bytes=VMEM_LIMIT, dimension_semantics=("arbitrary",)
        ),
        cost_estimate=pl.CostEstimate(
            flops=10 * pairs * HEAD_DIM, bytes_accessed=12 << 20, transcendentals=pairs
        ),
    )(place, lengths, versions, *operands)


def per_device(
    normed_input, queries, rotated_key_rows, frozen_value_rows, cotangent,
    adapter_down_weight, adapter_up_weight, document_lengths, versions,
):
    rows, width = queries.shape
    half = width // 2
    rank = adapter_down_weight.shape[1]
    sequence_count = lax.axis_size("seq")
    replicas = lax.axis_size("dp")
    shard = lax.axis_index("seq")
    replica = lax.axis_index("dp")
    y, z = shard % 2, shard // 2
    place = jnp.stack([y, z]).astype(jnp.int32)

    pair_send, ring_send, query_send, value_own, low, x_send = prepare(
        place, normed_input, adapter_down_weight, adapter_up_weight, frozen_value_rows,
        rotated_key_rows, queries, cotangent, replicas,
    )
    to_pair = lambda a: shifted(a, "seq", lambda i: i ^ 1)
    to_next = lambda a: shifted(a, "seq", lambda i: i + 2)
    to_prev = lambda a: shifted(a, "seq", lambda i: i - 2)
    pair = to_pair(pair_send)
    prev, nxt = to_next(ring_send), to_prev(ring_send)
    pair_q = to_pair(query_send)
    second = jnp.concatenate([pair[:, :width], low, pair[:, width:]], axis=1)
    prev2, nxt2 = to_next(second), to_prev(second)

    dq_own, dq_pair, mid, out_prev, out_next, back, up_part = attend(
        place, document_lengths, versions, queries, cotangent, rotated_key_rows, value_own, low,
        adapter_up_weight, pair, pair_q, prev, prev2, nxt, nxt2,
    )
    x_cols = lax.all_to_all(x_send, "dp", 0, 0, tiled=True)

    blocks = [back[i * rows : (i + 1) * rows] for i in range(6)]
    arrived = blocks[0] + to_pair(blocks[1])
    arrived = arrived + to_prev(blocks[2]) + to_next(blocks[4])
    arrived = arrived + shifted(blocks[3], "seq", lambda i: i - 1 if i % 2 == 0 else i - 3)
    arrived = arrived + shifted(blocks[5], "seq", lambda i: i + 3 if i % 2 == 0 else i + 1)
    returned_rows = arrived.astype(jnp.bfloat16)
    spread = jnp.broadcast_to(returned_rows[None], (replicas,) + returned_rows.shape)
    rows_all = lax.all_to_all(spread, "dp", 0, 0, tiled=True)

    empty = jnp.zeros_like(up_part)
    up_send = jnp.where(
        y == 0,
        jnp.concatenate([up_part, empty], axis=0),
        jnp.concatenate([empty, up_part], axis=0),
    ).astype(jnp.bfloat16)
    up_all = lax.all_to_all(up_send, "dp", 0, 0, tiled=True)
    up_mine = jnp.sum(up_all.astype(jnp.float32), axis=0)
    norm = adapter_scale / math.sqrt(rows * sequence_count * replicas)
    down_mine = lax.dot_general(
        x_cols, rows_all, (((0, 1), (0, 1)), ((), ())), preferred_element_type=jnp.float32
    )
    joined = jnp.concatenate([down_mine, up_mine], axis=0) * norm
    share = joined.shape[0] // sequence_count
    parts = lax.all_to_all(joined.reshape(sequence_count, share, rank), "seq", 0, 0, tiled=True)
    reduced = jnp.sum(parts, axis=0)
    spread = jnp.broadcast_to(reduced[None], (sequence_count, share, rank))
    final = lax.all_to_all(spread, "seq", 0, 0, tiled=True).reshape(sequence_count * share, rank)
    down_rows = adapter_down_weight.shape[0] // replicas
    down_weight_gradient = final[:down_rows]
    up_weight_gradient = final[down_rows:]

    total = mid + to_prev(out_prev).astype(jnp.float32) + to_next(out_next).astype(jnp.float32)
    total = total.astype(jnp.bfloat16)
    send = jnp.concatenate([total[:, rows:], dq_pair[None]], axis=0)
    came = to_pair(send)
    kept = jnp.concatenate([total[:, :rows], dq_own[None]], axis=0)
    whole = jnp.where(
        y == 0, jnp.concatenate([kept, came], axis=2), jnp.concatenate([came, kept], axis=2)
    )
    return (whole[2], whole[0], whole[1], down_weight_gradient, up_weight_gradient)


def solution(mesh):
    tokens = P(("dp", "seq"), None)
    in_specs = (tokens,) * 5 + (P(), P(), P("dp", None), P("dp", None))
    out_specs = (tokens,) * 3 + (P("dp", None), P(None, "dp"))
    return jax.shard_map(
        per_device, mesh=mesh, in_specs=in_specs, out_specs=out_specs, check_vma=False
    )
```

time: 450 us -> 187 us (0.42)
  waiting for transfers between devices: 343 us -> 44.1 us
  blocking collectives: 0 us -> 42.3 us
  starting transfers between devices: 20.6 us -> 58.1 us
  local copies, waits for them, and re-layouts: 37 us -> 12.8 us
  matrix products: 23.8 us -> 1.7 us
  Pallas kernels: 0 us -> 20.3 us
  between operations: 14.4 us -> 0.95 us
  other arithmetic: 9.88 us -> 5.26 us
    psum x1 -> x0, waiting for transfers between devices: 260 us -> none  [per_device(): lax.psum((part_a, part_b), ('dp', 'seq'))]
    ppermute x8 -> x14, waiting for transfers between devices: 83.6 us -> 34.9 us  [shifted(): return lax.ppermute(block, axis, route)]
    all_to_all x0 -> x2, blocking collectives: none -> 42.3 us  [the longest x1 22.6 us: per_device(): lax.all_to_all(joined.reshape(sequence_count, share, rank), 'seq', 0, 0,...]
    all_to_all x0 -> x3, starting transfers between devices: none -> 23.1 us  [the longest x1 8.53 us: per_device(): rows_all = lax.all_to_all(spread, 'dp', 0, 0, tiled=True)]
    pallas_call x0 -> x2, Pallas kernels: none -> 20.3 us  [the longest x1 16.9 us: attend(): pl.pallas_call(attend_kernel, grid_spec=pltpu.PrefetchScalarGridSpec(num_...]
    dot_general x9 -> x1, matrix products: 17.7 us -> 1.7 us  [per_device(): lax.dot_general(x_cols, rows_all, (((0, 1), (0, 1)), ((), ())), preferred...]
    ppermute x8 -> x14, starting transfers between devices: 20.6 us -> 35 us  [shifted(): return lax.ppermute(block, axis, route)]
    convert_element_type x3 -> x0, local copies, waits for them, and re-layouts: 9.89 us -> none  [the longest x1 4.5 us: attend(): grad_values.astype(jnp.bfloat16)]
  transfers between devices with their start and end apart: 9 -> 17, of which waited for: 7 -> 8; matrix products, arithmetic and copies ran while one was open for 3% -> 3% of each run, Pallas kernels for 0% -> 9%
where the time goes in v1:
time: 187 us; the launch traced here: 186 us
  starting transfers between devices  58.1 us (31%)
  waiting for transfers between devices  44.1 us (24%)
  blocking collectives  42.3 us (23%)
  Pallas kernels  20.3 us (11%)
  local copies, waits for them, and re-layouts  12.8 us (7%)
  other arithmetic  5.26 us (3%)
    ppermute x14, starting transfers between devices, shifted(): return lax.ppermute(block, axis, route)  35 us
    ppermute x14, waiting for transfers between devices, shifted(): return lax.ppermute(block, axis, route)  34.9 us
    all_to_all x1, blocking collectives, per_device(): lax.all_to_all(joined.reshape(sequence_count, share, rank), 'seq', 0, 0,...  22.6 us
    all_to_all x1, blocking collectives, per_device(): lax.all_to_all(spread, 'seq', 0, 0, tiled=True)  19.7 us
    pallas_call x1, Pallas kernels, attend(): pl.pallas_call(attend_kernel, grid_spec=pltpu.PrefetchScalarGridSpec(num_...  16.9 us
    all_to_all x1, waiting for transfers between devices, per_device(): rows_all = lax.all_to_all(spread, 'dp', 0, 0, tiled=True)  9.29 us
    unnamed x40, local copies, waits for them, and re-layouts  9.25 us
    all_to_all x1, starting transfers between devices, per_device(): rows_all = lax.all_to_all(spread, 'dp', 0, 0, tiled=True)  8.53 us
  transfers between devices with their start and end apart: 17, of which 8 were waited for; matrix products, arithmetic and copies ran while one was open for 3% of the time, Pallas kernels for 9%

profile of v1, /device:TPU:2, one launch (start us, length us, event | category | flops | bytes accessed | tf_op | source)
XLA Modules:
  0.0 185.5 jit_solution(17054527201285341680)
XLA Ops:
  0.7 1.0 copy-done
  1.8 1.0 copy-done.2
  2.8 1.0 copy-done.4
  3.9 1.0 copy-done.6
  4.9 1.0 copy-done.9
  5.9 3.3 %shard_map.128 = (bf16[128,2176]{1,0:T(8,128)(2,1)}, bf16[128,2048]{1,0:T(8,128)(2,1)}, bf16[128,2048]{1,0:T(8,128)(2,1)}, bf16[128,1024]{1,0:T(8,128)(2,1)S(1)}...) custom-call(s32[2]{0:T(128)S(1)} %pad_add_fusion.place, bf16[128,4096]{1,0:T(8,128)(2,1)} %x.5, ...), custom_call_target="tpu_custom_call" | custom-call | tf_op jit(solution)/shard_map/pallas_call | solution.py:73
  9.3 1.0 copy-done.8
  10.3 1.6 collective-permute-start.1
  11.9 7.3 %all-to-all-start = ((bf16[16,128,256]{2,1,0:T(8,128)(2,1)}), bf16[16,128,256]{2,1,0:T(8,128)(2,1)}, u32[]{:S(2)}, u32[]{:S(2)}) async-start(bf16[16,128,256]{2,1,0:T(8,128)(2,1)} %copy-done.8), calls=%async_computation | async-start | bytes 2097152 | tf_op jit(solution)/shard_map/all_to_all | solution.py:264
  19.2 15.2 %collective-permute-done.1.k_pair.v_pair.l_pair = bf16[128,2176]{1,0:T(8,128)(2,1)S(1)} collective-permute-done((bf16[128,2176]{1,0:T(8,128)(2,1)}, bf16[128,2176]{1,0:T(8,128)(2,1)S(1)}, u32[]{:S(2)}, u32[]{:S(2)}) %collective-permute-start.1) | collective-permute-done | bytes 557088 | tf_op jit(solution)/shard_map/ppermute | solution.py:29
  34.5 0.9 pad_maximum_fusion.1
  35.3 1.3 collective-permute-start.5
  36.6 5.4 %collective-permute-start.3 = (bf16[128,2304]{1,0:T(8,128)(2,1)}, bf16[128,2304]{1,0:T(8,128)(2,1)}, u32[]{:S(2)}, u32[]{:S(2)}) collective-permute-start(bf16[128,2304]{1,0:T(8,128)(2,1)} %pad_maximum_fusion.1), channel_id=1, source_target_pairs={{0,2},{1,3},{2,4},{3,5},{4,6},{5,7},{6,8},{7,9},{8,10},{9,11},{10,... | collective-permute-start | bytes 1769480 | tf_op jit(solution)/shard_map/ppermute | solution.py:29
  42.0 1.6 collective-permute-start
  43.6 1.3 collective-permute-start.4
  44.9 5.4 %collective-permute-start.2 = (bf16[128,2048]{1,0:T(8,128)(2,1)}, bf16[128,2048]{1,0:T(8,128)(2,1)}, u32[]{:S(2)}, u32[]{:S(2)}) collective-permute-start(bf16[128,2048]{1,0:T(8,128)(2,1)} %get-tuple-element.20), channel_id=1, source_target_pairs={{0,2},{1,3},{2,4},{3,5},{4,6},{5,7},{6,8},{7,9},{8,10},{9,11},{10,... | collective-permute-start | bytes 1572872 | tf_op jit(solution)/shard_map/ppermute | solution.py:29
  50.3 1.6 collective-permute-done.q_pair.g_pair
  51.8 8.5 %collective-permute-done.4.k_next.v_next = bf16[128,2048]{1,0:T(8,128)(2,1)} collective-permute-done((bf16[128,2048]{1,0:T(8,128)(2,1)}, bf16[128,2048]{1,0:T(8,128)(2,1)}, u32[]{:S(2)}, u32[]{:S(2)}) %collective-permute-start.4) | collective-permute-done | bytes 524320 | tf_op jit(solution)/shard_map/ppermute | solution.py:29
  60.4 1.2 collective-permute-done.2.k_prev.v_prev
  61.6 16.9 %shard_map.129 = (bf16[128,1024]{1,0:T(8,128)(2,1)S(1)}, bf16[128,1024]{1,0:T(8,128)(2,1)S(1)}, f32[2,256,1024]{2,1,0:T(8,128)}, bf16[2,256,1024]{2,1,0:T(8,128)...) custom-call(s32[2]{0:T(128)S(1)} %pad_add_fusion.place, ...), custom_call_target="tpu_custom_call" | custom-call | flops 2013265920 | bytes 12582912 | tf_op jit(solution)/shard_map/pallas_call | solution.py:210
  78.6 0.7 copy-done.10
  79.3 0.7 copy-done.12
  80.0 0.7 copy-done.14
  80.7 1.4 collective-permute-start.6
  82.1 6.0 %collective-permute-start.7 = (bf16[2,256,1024]{2,1,0:T(8,128)(2,1)}, bf16[2,256,1024]{2,1,0:T(8,128)(2,1)}, u32[]{:S(2)}, u32[]{:S(2)}) collective-permute-start(bf16[2,256,1024]{2,1,0:T(8,128)(2,1)} %get-tuple-element.25), channel_id=1, source_target_pairs={{0,2},{1,3},{2,4},{3,5},{4,6},{5,7},{6,8},{7,9},{8,10},{9,11},{10,... | collective-permute-start | bytes 3145736 | tf_op jit(solution)/shard_map/ppermute | solution.py:29
  88.1 0.8 select_convert_fusion
  89.0 7.3 %all-to-all-start.2 = ((bf16[16,128,128]{2,1,0:T(8,128)(2,1)}), bf16[16,128,128]{2,1,0:T(8,128)(2,1)S(1)}, u32[]{:S(2)}, u32[]{:S(2)}) async-start(bf16[16,128,128]{2,1,0:T(8,128)(2,1)} %select_convert_fusion), calls=%async_computation.2 | async-start | bytes 1048576 | tf_op jit(solution)/shard_map/all_to_all | solution.py:281
  96.3 0.8 collective-permute-start.9
  97.0 3.7 %collective-permute-start.13 = (f32[128,128]{1,0:T(8,128)S(1)}, f32[128,128]{1,0:T(8,128)S(1)}, u32[]{:S(2)}, u32[]{:S(2)}) collective-permute-start(f32[128,128]{1,0:T(8,128)S(1)} %get-tuple-element.37), channel_id=1, source_target_pairs={{0,3},{1,2},{2,5},{3,4},{4,7},{5,6},{6,9},{7,8},{8,11},{9,10},{10,... | collective-permute-start | bytes 196616 | tf_op jit(solution)/shard_map/ppermute | solution.py:29
  100.8 1.3 collective-permute-start.12
  102.1 3.1 %collective-permute-done.9 = f32[128,128]{1,0:T(8,128)S(1)} collective-permute-done((f32[128,128]{1,0:T(8,128)S(1)}, f32[128,128]{1,0:T(8,128)S(1)}, u32[]{:S(2)}, u32[]{:S(2)}) %collective-permute-start.9) | collective-permute-done | bytes 65568 | tf_op jit(solution)/shard_map/ppermute | solution.py:29
  105.1 3.7 %collective-permute-start.11 = (f32[128,128]{1,0:T(8,128)S(1)}, f32[128,128]{1,0:T(8,128)S(1)}, u32[]{:S(2)}, u32[]{:S(2)}) collective-permute-start(f32[128,128]{1,0:T(8,128)S(1)} %get-tuple-element.39), channel_id=1, source_target_pairs={{0,2},{1,3},{2,4},{3,5},{4,6},{5,7},{6,8},{7,9},{8,10},{9,11},{10,... | collective-permute-start | bytes 196616 | tf_op jit(solution)/shard_map/ppermute | solution.py:29
  108.8 1.4 collective-permute-start.10
  110.3 0.4 collective-permute-done.11
  110.7 4.9 %collective-permute-done.10 = f32[128,128]{1,0:T(8,128)S(1)} collective-permute-done((f32[128,128]{1,0:T(8,128)S(1)}, f32[128,128]{1,0:T(8,128)S(1)}, u32[]{:S(2)}, u32[]{:S(2)}) %collective-permute-start.10) | collective-permute-done | bytes 65568 | tf_op jit(solution)/shard_map/ppermute | solution.py:29
  115.6 0.9 broadcast_in_dim.10
  116.5 8.5 %all-to-all-start.1 = ((bf16[16,128,128]{2,1,0:T(8,128)(2,1)}), bf16[16,128,128]{2,1,0:T(8,128)(2,1)S(1)}, u32[]{:S(2)}, u32[]{:S(2)}) async-start(bf16[16,128,128]{2,1,0:T(8,128)(2,1)} %broadcast_in_dim.10), calls=%async_computation.1 | async-start | bytes 1048576 | tf_op jit(solution)/shard_map/all_to_all | solution.py:273
  125.0 0.7 convert_reduce_fusion
  125.7 9.3 %all-to-all-done.1 = bf16[16,128,128]{2,1,0:T(8,128)(2,1)S(1)} async-done(((bf16[16,128,128]{2,1,0:T(8,128)(2,1)}), bf16[16,128,128]{2,1,0:T(8,128)(2,1)S(1)}, u32[]{:S(2)}, u32[]{:S(2)}) %all-to-all-start.1) | async-done | bytes 524320 | tf_op jit(solution)/shard_map/all_to_all | solution.py:273
  135.0 1.7 convolution_bitcast_fusion
  136.8 2.0 %add_convert_fusion = bf16[2,256,1024]{2,1,0:T(8,128)(2,1)S(1)} fusion(bf16[2,256,1024]{2,1,0:T(8,128)(2,1)} %collective-permute-done.7, f32[2,256,1024]{2,1,0:T(8,128)S(1)} %copy-done.18, bf16[2,256,1024]{2,1,0:T(8,128)(2,1)} %collective-permute-done.6), kind=kLoop, calls=%fused_computation | loop fusion | flops 2621440 | bytes 5242880 | tf_op jit(solution)/shard_map/convert_element_type | solution.py:298
  138.9 0.8 copy-done.13
  140.1 22.6 %all_to_all.25 = f32[16,24,128]{2,1,0:T(8,128)S(1)} all-to-all(f32[16,24,128]{2,1,0:T(8,128)S(1)} %bitcast.18), channel_id=1, replica_groups=mesh['dp'=16,'seq'=16] {'seq'}, dimensions={0} | all-to-all | bytes 393216 | tf_op jit(solution)/shard_map/all_to_all | solution.py:289
  162.7 19.7 %all_to_all.26 = f32[16,24,128]{2,1,0:T(8,128)S(1)} all-to-all(f32[16,24,128]{2,1,0:T(8,128)S(1)} %broadcast_in_dim.22), channel_id=1, replica_groups=mesh['dp'=16,'seq'=16] {'seq'}, dimensions={0} | all-to-all | bytes 393216 | tf_op jit(solution)/shard_map/all_to_all | solution.py:292
  182.4 0.6 slice.68
  183.1 0.7 slice.67
  183.7 0.6 maximum_select_fusion
  184.3 1.2 slice_bitcast_fusion
  (50 shorter events, 0.7 us)
Async XLA Ops:
  0.7 1.0 copy-start
  1.8 1.0 copy-start.2
  2.8 1.0 copy-start.4
  3.9 1.0 copy-start.6
  4.9 1.0 copy-start.9
  9.3 1.0 copy-start.8
  10.3 24.1 %collective-permute-start.1 = (bf16[128,2176]{1,0:T(8,128)(2,1)}, bf16[128,2176]{1,0:T(8,128)(2,1)S(1)}, u32[]{:S(2)}, u32[]{:S(2)}) collective-permute-start(bf16[128,2176]{1,0:T(8,128)(2,1)} %get-tuple-element.19), channel_id=1, source_target_pairs={{0,1},{1,0},{2,3},{3,2},{4,5},{5,4},{6,7},{7,6},{8,9},{9,8},{10,11... | collective-permute-start | bytes 1671176 | tf_op jit(solution)/shard_map/ppermute | solution.py:29
  11.8 49.7 %copy-start.1 = (bf16[128,2048]{1,0:T(8,128)(2,1)S(1)}, bf16[128,2048]{1,0:T(8,128)(2,1)}, u32[]{:S(2)}) copy-start(bf16[128,2048]{1,0:T(8,128)(2,1)} %q_own.1) | copy-start | bytes 1572868
  11.8 49.7 %copy-start.3 = (bf16[128,2048]{1,0:T(8,128)(2,1)S(1)}, bf16[128,2048]{1,0:T(8,128)(2,1)}, u32[]{:S(2)}) copy-start(bf16[128,2048]{1,0:T(8,128)(2,1)} %up.3) | copy-start | bytes 1572868
  11.8 49.7 %copy-start.5 = (bf16[128,2048]{1,0:T(8,128)(2,1)S(1)}, bf16[128,2048]{1,0:T(8,128)(2,1)}, u32[]{:S(2)}) copy-start(bf16[128,2048]{1,0:T(8,128)(2,1)} %k_own.1) | copy-start | bytes 1572868
  11.9 49.7 %copy-start.7 = (bf16[128,2048]{1,0:T(8,128)(2,1)S(1)}, bf16[128,2048]{1,0:T(8,128)(2,1)}, u32[]{:S(2)}) copy-start(bf16[128,2048]{1,0:T(8,128)(2,1)} %g_own.1) | copy-start | bytes 1572868
  11.9 49.7 %copy-start.16 = (s32[1,16]{1,0:T(1,128)S(1)}, s32[1,16]{1,0:T(1,128)}, u32[]{:S(2)}) copy-start(s32[1,16]{1,0:T(1,128)} %lengths.1) | copy-start | bytes 196
  11.9 49.7 %copy-start.17 = (s32[1,16]{1,0:T(1,128)S(1)}, s32[1,16]{1,0:T(1,128)}, u32[]{:S(2)}) copy-start(s32[1,16]{1,0:T(1,128)} %versions.1) | copy-start | bytes 196
  11.9 77.1 %all-to-all-start = ((bf16[16,128,256]{2,1,0:T(8,128)(2,1)}), bf16[16,128,256]{2,1,0:T(8,128)(2,1)}, u32[]{:S(2)}, u32[]{:S(2)}) async-start(bf16[16,128,256]{2,1,0:T(8,128)(2,1)} %copy-done.8), calls=%async_computation | async-start | bytes 2097152 | tf_op jit(solution)/shard_map/all_to_all | solution.py:264
  35.3 26.2 %collective-permute-start.5 = (bf16[128,2304]{1,0:T(8,128)(2,1)}, bf16[128,2304]{1,0:T(8,128)(2,1)}, u32[]{:S(2)}, u32[]{:S(2)}) collective-permute-start(bf16[128,2304]{1,0:T(8,128)(2,1)} %pad_maximum_fusion.1), channel_id=1, source_target_pairs={{2,0},{3,1},{4,2},{5,3},{6,4},{7,5},{8,6},{9,7},{10,8},{11,9},{12,... | collective-permute-start | bytes 1769480 | tf_op jit(solution)/shard_map/ppermute | solution.py:29
  36.6 24.9 %collective-permute-start.3 = (bf16[128,2304]{1,0:T(8,128)(2,1)}, bf16[128,2304]{1,0:T(8,128)(2,1)}, u32[]{:S(2)}, u32[]{:S(2)}) collective-permute-start(bf16[128,2304]{1,0:T(8,128)(2,1)} %pad_maximum_fusion.1), channel_id=1, source_target_pairs={{0,2},{1,3},{2,4},{3,5},{4,6},{5,7},{6,8},{7,9},{8,10},{9,11},{10,... | collective-permute-start | bytes 1769480 | tf_op jit(solution)/shard_map/ppermute | solution.py:29
  42.0 9.8 %collective-permute-start = (bf16[128,2048]{1,0:T(8,128)(2,1)}, bf16[128,2048]{1,0:T(8,128)(2,1)S(1)}, u32[]{:S(2)}, u32[]{:S(2)}) collective-permute-start(bf16[128,2048]{1,0:T(8,128)(2,1)} %get-tuple-element.18), channel_id=1, source_target_pairs={{0,1},{1,0},{2,3},{3,2},{4,5},{5,4},{6,7},{7,6},{8,9},{9,8},{10,11... | collective-permute-start | bytes 1572872 | tf_op jit(solution)/shard_map/ppermute | solution.py:29
  43.6 16.8 %collective-permute-start.4 = (bf16[128,2048]{1,0:T(8,128)(2,1)}, bf16[128,2048]{1,0:T(8,128)(2,1)}, u32[]{:S(2)}, u32[]{:S(2)}) collective-permute-start(bf16[128,2048]{1,0:T(8,128)(2,1)} %get-tuple-element.20), channel_id=1, source_target_pairs={{2,0},{3,1},{4,2},{5,3},{6,4},{7,5},{8,6},{9,7},{10,8},{11,9},{12,... | collective-permute-start | bytes 1572872 | tf_op jit(solution)/shard_map/ppermute | solution.py:29
  44.9 16.7 %collective-permute-start.2 = (bf16[128,2048]{1,0:T(8,128)(2,1)}, bf16[128,2048]{1,0:T(8,128)(2,1)}, u32[]{:S(2)}, u32[]{:S(2)}) collective-permute-start(bf16[128,2048]{1,0:T(8,128)(2,1)} %get-tuple-element.20), channel_id=1, source_target_pairs={{0,2},{1,3},{2,4},{3,5},{4,6},{5,7},{6,8},{7,9},{8,10},{9,11},{10,... | collective-permute-start | bytes 1572872 | tf_op jit(solution)/shard_map/ppermute | solution.py:29
  78.5 0.7 copy-start.10
  79.3 0.7 copy-start.12
  80.0 0.7 copy-start.14
  80.7 15.5 %copy-start.11 = (f32[768,128]{1,0:T(8,128)S(1)}, f32[768,128]{1,0:T(8,128)}, u32[]{:S(2)}) copy-start(f32[768,128]{1,0:T(8,128)} %copy-done.10) | copy-start | bytes 1179652
  80.7 56.0 %collective-permute-start.6 = (bf16[2,256,1024]{2,1,0:T(8,128)(2,1)}, bf16[2,256,1024]{2,1,0:T(8,128)(2,1)}, u32[]{:S(2)}, u32[]{:S(2)}) collective-permute-start(bf16[2,256,1024]{2,1,0:T(8,128)(2,1)} %get-tuple-element.24), channel_id=1, source_target_pairs={{2,0},{3,1},{4,2},{5,3},{6,4},{7,5},{8,6},{9,7},{10,8},{11,9},{12,... | collective-permute-start | bytes 3145736 | tf_op jit(solution)/shard_map/ppermute | solution.py:29
  82.1 54.6 %collective-permute-start.7 = (bf16[2,256,1024]{2,1,0:T(8,128)(2,1)}, bf16[2,256,1024]{2,1,0:T(8,128)(2,1)}, u32[]{:S(2)}, u32[]{:S(2)}) collective-permute-start(bf16[2,256,1024]{2,1,0:T(8,128)(2,1)} %get-tuple-element.25), channel_id=1, source_target_pairs={{0,2},{1,3},{2,4},{3,5},{4,6},{5,7},{6,8},{7,9},{8,10},{9,11},{10,... | collective-permute-start | bytes 3145736 | tf_op jit(solution)/shard_map/ppermute | solution.py:29
  89.0 26.6 %all-to-all-start.2 = ((bf16[16,128,128]{2,1,0:T(8,128)(2,1)}), bf16[16,128,128]{2,1,0:T(8,128)(2,1)S(1)}, u32[]{:S(2)}, u32[]{:S(2)}) async-start(bf16[16,128,128]{2,1,0:T(8,128)(2,1)} %select_convert_fusion), calls=%async_computation.2 | async-start | bytes 1048576 | tf_op jit(solution)/shard_map/all_to_all | solution.py:281
  96.3 8.9 %collective-permute-start.9 = (f32[128,128]{1,0:T(8,128)S(1)}, f32[128,128]{1,0:T(8,128)S(1)}, u32[]{:S(2)}, u32[]{:S(2)}) collective-permute-start(f32[128,128]{1,0:T(8,128)S(1)} %get-tuple-element.36), channel_id=1, source_target_pairs={{0,1},{1,0},{2,3},{3,2},{4,5},{5,4},{6,7},{7,6},{8,9},{9,8},{10,11... | collective-permute-start | bytes 196616 | tf_op jit(solution)/shard_map/ppermute | solution.py:29
  97.0 11.8 %collective-permute-start.13 = (f32[128,128]{1,0:T(8,128)S(1)}, f32[128,128]{1,0:T(8,128)S(1)}, u32[]{:S(2)}, u32[]{:S(2)}) collective-permute-start(f32[128,128]{1,0:T(8,128)S(1)} %get-tuple-element.37), channel_id=1, source_target_pairs={{0,3},{1,2},{2,5},{3,4},{4,7},{5,6},{6,9},{7,8},{8,11},{9,10},{10,... | collective-permute-start | bytes 196616 | tf_op jit(solution)/shard_map/ppermute | solution.py:29
  100.8 9.5 %collective-permute-start.12 = (f32[128,128]{1,0:T(8,128)S(1)}, f32[128,128]{1,0:T(8,128)S(1)}, u32[]{:S(2)}, u32[]{:S(2)}) collective-permute-start(f32[128,128]{1,0:T(8,128)S(1)} %get-tuple-element.38), channel_id=1, source_target_pairs={{2,1},{3,0},{4,3},{5,2},{6,5},{7,4},{8,7},{9,6},{10,9},{11,8},{12,... | collective-permute-start | bytes 196616 | tf_op jit(solution)/shard_map/ppermute | solution.py:29
  105.1 5.5 %collective-permute-start.11 = (f32[128,128]{1,0:T(8,128)S(1)}, f32[128,128]{1,0:T(8,128)S(1)}, u32[]{:S(2)}, u32[]{:S(2)}) collective-permute-start(f32[128,128]{1,0:T(8,128)S(1)} %get-tuple-element.39), channel_id=1, source_target_pairs={{0,2},{1,3},{2,4},{3,5},{4,6},{5,7},{6,8},{7,9},{8,10},{9,11},{10,... | collective-permute-start | bytes 196616 | tf_op jit(solution)/shard_map/ppermute | solution.py:29
  108.8 27.9 %copy-start.18 = (f32[2,256,1024]{2,1,0:T(8,128)S(1)}, f32[2,256,1024]{2,1,0:T(8,128)}, u32[]{:S(2)}) copy-start(f32[2,256,1024]{2,1,0:T(8,128)} %get-tuple-element.23) | copy-start | bytes 6291460
  108.8 6.7 %collective-permute-start.10 = (f32[128,128]{1,0:T(8,128)S(1)}, f32[128,128]{1,0:T(8,128)S(1)}, u32[]{:S(2)}, u32[]{:S(2)}) collective-permute-start(f32[128,128]{1,0:T(8,128)S(1)} %get-tuple-element.40), channel_id=1, source_target_pairs={{2,0},{3,1},{4,2},{5,3},{6,4},{7,5},{8,6},{9,7},{10,8},{11,9},{12,... | collective-permute-start | bytes 196616 | tf_op jit(solution)/shard_map/ppermute | solution.py:29
  116.5 18.5 %all-to-all-start.1 = ((bf16[16,128,128]{2,1,0:T(8,128)(2,1)}), bf16[16,128,128]{2,1,0:T(8,128)(2,1)S(1)}, u32[]{:S(2)}, u32[]{:S(2)}) async-start(bf16[16,128,128]{2,1,0:T(8,128)(2,1)} %broadcast_in_dim.10), calls=%async_computation.1 | async-start | bytes 1048576 | tf_op jit(solution)/shard_map/all_to_all | solution.py:273
  138.8 1.0 copy-start.13
  138.8 1.2 copy-start.19
  138.9 44.8 %copy-start.15 = (bf16[128,1024]{1,0:T(8,128)(2,1)S(1)}, bf16[128,1024]{1,0:T(8,128)(2,1)}, u32[]{:S(2)}) copy-start(bf16[128,1024]{1,0:T(8,128)(2,1)} %copy-done.14) | copy-start | bytes 786436
  139.8 43.9 %collective-permute-start.8 = (bf16[3,128,1024]{2,1,0:T(8,128)(2,1)S(1)}, bf16[3,128,1024]{2,1,0:T(8,128)(2,1)S(1)}, u32[]{:S(2)}, u32[]{:S(2)}) collective-permute-start(bf16[3,128,1024]{2,1,0:T(8,128)(2,1)S(1)} %pad_maximum_fusion), channel_id=1, source_target_pairs={{0,1},{1,0},{2,3},{3,2},{4,5},{5,4},{6,7},{7,6},{8,9},{9,8},{10,11... | collective-permute-start | bytes 2359304 | tf_op jit(solution)/shard_map/ppermute | solution.py:29

commit v2 on v1

v2 whole, which is shorter than its diff:
```python
import functools
import math

import jax
import jax.numpy as jnp
from jax import lax
from jax.experimental import pallas as pl
from jax.experimental.pallas import tpu as pltpu
from jax.sharding import PartitionSpec as P

HEAD_DIM = 128
VERSIONS = 4

adapter_scale = 0.5
masked_score = -1e30
VMEM_LIMIT = 60 * 1024 * 1024
HEADS_PER_STEP = 4


def contract(a, b, dim_a, dim_b):
    return lax.dot_general(
        a, b, (((dim_a,), (dim_b,)), ((), ())), preferred_element_type=jnp.float32
    )


def shifted(block, axis, target):
    count = lax.axis_size(axis)
    route = [(i, target(i)) for i in range(count) if 0 <= target(i) < count]
    return lax.ppermute(block, axis, route)


def prepare_kernel(
    place, x, down, up, frozen, keys, queries, grads,
    pair_out, ring_out, query_out,
    x_in, down_in, up_in, frozen_in, moved, values_v, low_v, sems,
):
    rows, rank = low_v.shape
    half = values_v.shape[2]
    y = place[0]
    own = pl.multiple_of(y * half, half)
    other = pl.multiple_of((1 - y) * half, half)
    used = []

    def copy(src, dst):
        done = pltpu.make_async_copy(src, dst, sems.at[len(used)])
        used.append(done)
        done.start()
        return done

    chunks = 4
    size = x.shape[1] // chunks
    parts = []
    for c in range(chunks):
        span = pl.ds(c * size, size)
        parts.append((copy(x.at[:, span], x_in.at[:, span]), copy(down.at[span], down_in.at[span])))
    left, right = pl.ds(0, half), pl.ds(half, half)
    route = [
        (keys, other, pair_out.at[:, left]),
        (keys, own, ring_out.at[:, left]),
        (queries, other, query_out.at[:, left]),
        (grads, other, query_out.at[:, right]),
    ]
    arriving = [copy(src.at[:, pl.ds(at, half)], moved.at[i]) for i, (src, at, _) in enumerate(route)]
    up_done = copy(up, up_in)
    frozen_done = copy(frozen, frozen_in)
    low = jnp.zeros((rows, rank), jnp.float32)
    for c, (a, b) in enumerate(parts):
        a.wait()
        b.wait()
        low += contract(x_in[:, c * size : (c + 1) * size], down_in[c * size : (c + 1) * size, :], 1, 0)
    low = low.astype(jnp.bfloat16)
    low_v[...] = low
    rest = []
    for target in (pair_out.at[:, pl.ds(2 * half, rank)], ring_out.at[:, pl.ds(2 * half, rank)]):
        rest.append(copy(low_v, target))
    for i, done in enumerate(arriving):
        done.wait()
        rest.append(copy(moved.at[i], route[i][2]))
    up_done.wait()
    frozen_done.wait()
    for i, (start, target) in enumerate(((other, pair_out.at[:, right]), (own, ring_out.at[:, right]))):
        lifted = contract(low, up_in[:, pl.ds(start, half)], 1, 0)
        base = frozen_in[:, pl.ds(start, half)].astype(jnp.float32)
        values_v[i] = (base + adapter_scale * lifted).astype(jnp.bfloat16)
        rest.append(copy(values_v.at[i], target))
    for done in rest:
        done.wait()


def prepare(place, x, down, up, frozen, keys, queries, grads):
    rows, width = keys.shape
    rank = down.shape[1]
    half = width // 2
    kind = jnp.bfloat16
    shapes = [(rows, width + rank), (rows, width + rank), (rows, width)]
    anywhere = pl.BlockSpec(memory_space=pl.ANY)
    return pl.pallas_call(
        prepare_kernel,
        out_shape=[jax.ShapeDtypeStruct(s, kind) for s in shapes],
        in_specs=[pl.BlockSpec(memory_space=pltpu.SMEM)] + [anywhere] * 7,
        out_specs=[anywhere] * 3,
        scratch_shapes=[
            pltpu.VMEM(x.shape, kind),
            pltpu.VMEM(down.shape, kind),
            pltpu.VMEM(up.shape, kind),
            pltpu.VMEM(frozen.shape, kind),
            pltpu.VMEM((4, rows, half), kind),
            pltpu.VMEM((2, rows, half), kind),
            pltpu.VMEM((rows, rank), kind),
            pltpu.SemaphoreType.DMA((22,)),
        ],
        compiler_params=pltpu.CompilerParams(vmem_limit_bytes=VMEM_LIMIT),
    )(place, x, down, up, frozen, keys, queries, grads)


def gather(refs, cols):
    return jnp.concatenate([r[:, cols] for r in refs], axis=0)


def against(main, far_a, far_b, other):
    rows = far_a.shape[0]
    far = jnp.concatenate(
        [contract(far_a, other[:rows], 1, 1), contract(far_b, other[rows:], 1, 1)], axis=1
    )
    return jnp.concatenate([contract(main, other, 1, 1), far], axis=0)


def onto(grid, other):
    rows = other.shape[0] // 2
    near = 4 * rows
    return (
        contract(grid[:near], other, 1, 0),
        contract(grid[near:, :rows], other[:rows], 1, 0),
        contract(grid[near:, rows:], other[rows:], 1, 0),
    )


def ordered(order, own, pair, prev, prev2, nxt, nxt2):
    pick = lambda a, b: (a, b) if order == 0 else (b, a)
    mid0, mid1 = pick(own, pair)
    far_prev, near_prev = pick(prev, prev2)
    near_next, far_next = pick(nxt, nxt2)
    return (near_prev, mid0, mid1, near_next), far_prev, far_next


def scatter(order, mid, prev, nxt, cols, main, far_a, far_b):
    rows = far_a.shape[0]
    first, second = (0, rows) if order == 0 else (rows, 0)

    def put(ref, at, val):
        ref[at : at + rows, cols] = val

    put(prev, second, main[:rows])
    put(mid, first, main[rows : 2 * rows])
    put(mid, second, main[2 * rows : 3 * rows])
    put(nxt, first, main[3 * rows :])
    put(prev, first, far_a)
    put(nxt, second, far_b)


def attend_kernel(
    place, lengths, versions,
    q_own, q_pair, g_own, g_pair,
    k_own, k_pair, k_prev, k_prev2, k_next, k_next2,
    v_own, v_pair, v_prev, v_prev2, v_next, v_next2,
    l_own, l_pair, l_prev, l_prev2, l_next, l_next2,
    up,
    dq_own, dq_pair, mid, prev, nxt, back_mid, back_prev, back_next, up_send,
    bias, weight, dvs,
):
    rows = q_own.shape[0]
    documents = lengths.shape[1]
    step = pl.program_id(0)
    y, z = place[0], place[1]
    base = 2 * z * rows
    heads = dvs.shape[1] // HEAD_DIM

    @pl.when(step == 0)
    def _():
        ends, total = [], jnp.int32(0)
        for j in range(documents):
            total = total + lengths[0, j]
            ends.append(total)
        for b in range(2):
            pos = lax.broadcasted_iota(jnp.int32, (8, rows), 1) + base + b * rows
            first = jnp.zeros_like(pos)
            last = jnp.zeros_like(pos)
            for j in range(documents):
                first = jnp.where(pos >= ends[j], ends[j], first)
            for j in reversed(range(documents)):
                last = jnp.where(pos < ends[j], ends[j], last)
            first, last = first[:1], last[:1]
            for c, shift in enumerate((-1, 0, 1, 2, -2 if b == 0 else 3)):
                key_pos = lax.broadcasted_iota(jnp.int32, (rows, rows), 0) + base + shift * rows
                inside = (key_pos >= first) & (key_pos < last)
                bias[c * rows : (c + 1) * rows, b * rows : (b + 1) * rows] = jnp.where(
                    inside, jnp.float32(0.0), jnp.float32(masked_score)
                )
            row_pos = lax.broadcasted_iota(jnp.int32, (rows, HEAD_DIM), 0) + base + b * rows
            scale = jnp.zeros((rows, HEAD_DIM), jnp.float32)
            for j in range(documents):
                level = lax.shift_left(jnp.int32(1), versions[0, j]).astype(jnp.float32)
                level = level * (2.0 ** (1 - VERSIONS))
                begin = ends[j - 1] if j > 0 else 0
                scale = jnp.where(row_pos >= begin, level, scale)
            weight[b * rows : (b + 1) * rows, :] = scale

    score_scale = 1.0 / math.sqrt(HEAD_DIM)
    factor = math.log2(math.e) * score_scale
    near = 4 * rows

    def work(order):
        pick = lambda own, pair: (own, pair) if order == 0 else (pair, own)
        ks, k_fp, k_fn = ordered(order, k_own, k_pair, k_prev, k_prev2, k_next, k_next2)
        vs, v_fp, v_fn = ordered(order, v_own, v_pair, v_prev, v_prev2, v_next, v_next2)
        dq0, dq1 = pick(dq_own, dq_pair)
        for h in range(HEADS_PER_STEP):
            cols = slice(h * HEAD_DIM, (h + 1) * HEAD_DIM)
            q = gather(pick(q_own, q_pair), cols)
            g = weight[...] * gather(pick(g_own, g_pair), cols).astype(jnp.float32)
            g = g.astype(jnp.bfloat16)
            k = gather(ks, cols)
            s = against(k, k_fp[:, cols], k_fn[:, cols], q) * factor + bias[...]
            e = jnp.exp2(s - jnp.max(s, axis=0, keepdims=True))
            wide = e * (1.0 / jnp.sum(e, axis=0, keepdims=True))
            p = wide.astype(jnp.bfloat16)
            small = [a.astype(jnp.bfloat16) for a in onto(p, g)]
            scatter(order, mid.at[1], prev.at[1], nxt.at[1], cols, *small)
            at = step * (HEADS_PER_STEP * HEAD_DIM)
            at = pl.ds(pl.multiple_of(at, HEAD_DIM) + h * HEAD_DIM, HEAD_DIM)
            dvs[:near, at] = small[0]
            dvs[near : near + rows, at] = small[1]
            dvs[near + rows :, at] = small[2]
            dp = against(gather(vs, cols), v_fp[:, cols], v_fn[:, cols], g)
            delta = jnp.sum(wide * dp, axis=0, keepdims=True)
            ds = (wide * (dp - delta)).astype(jnp.bfloat16)
            small = [(score_scale * a).astype(jnp.bfloat16) for a in onto(ds, q)]
            scatter(order, mid.at[0], prev.at[0], nxt.at[0], cols, *small)
            far = jnp.concatenate(
                [
                    contract(ds[near:, :rows], k_fp[:, cols], 0, 0),
                    contract(ds[near:, rows:], k_fn[:, cols], 0, 0),
                ],
                axis=0,
            )
            dq = contract(ds[:near], k, 0, 0) + far
            dq = (dq * score_scale).astype(jnp.bfloat16)
            dq0[:, cols] = dq[:rows]
            dq1[:, cols] = dq[rows:]

        @pl.when(step == pl.num_programs(0) - 1)
        def _():
            ls, l_fp, l_fn = ordered(order, l_own, l_pair, l_prev, l_prev2, l_next, l_next2)
            low = jnp.concatenate([r[...] for r in (*ls, l_fp, l_fn)], axis=0)
            part = contract(low, dvs[...], 0, 0).astype(jnp.bfloat16)
            for h in range(heads):
                up_send[order * heads + h] = part[:, h * HEAD_DIM : (h + 1) * HEAD_DIM]
                up_send[(1 - order) * heads + h] = jnp.zeros((part.shape[0], HEAD_DIM), jnp.bfloat16)
            full = contract(dvs[...], up[...], 1, 1)
            a, b = (0, rows) if order == 0 else (rows, 0)
            places = (
                (back_prev, b), (back_mid, a), (back_mid, b), (back_next, a), (back_prev, a), (back_next, b),
            )
            for c, (ref, at) in enumerate(places):
                ref[at : at + rows, :] = full[c * rows : (c + 1) * rows]

    for order in range(2):
        pl.when(y == order)(functools.partial(work, order))


def attend(place, lengths, versions, queries, grads, keys, ring, up, pair_q, pair, prev, prev2, nxt, nxt2):
    rows, width = queries.shape
    rank = up.shape[0]
    half = width // 2
    heads = half // HEAD_DIM
    block = HEADS_PER_STEP * HEAD_DIM
    steps = heads // HEADS_PER_STEP
    at = lambda first: pl.BlockSpec((rows, block), lambda h, *_: (0, first + h))
    mine = pl.BlockSpec((rows, block), lambda h, pc, *_: (0, pc[0] * steps + h))
    low_at = lambda b: pl.BlockSpec((rows, rank), lambda h, *_: (0, b))
    kind = jnp.bfloat16
    last = half // rank
    in_specs = [
        mine, at(0), mine, at(steps),
        mine, at(0), at(0), at(0), at(0), at(0),
    ] + [at(steps)] * 6 + [low_at(2 * last)] * 6 + [
        pl.BlockSpec((rank, half), lambda h, pc, *_: (0, pc[0])),
    ]
    operands = (
        queries, pair_q, grads, pair_q,
        keys, pair, prev, prev2, nxt, nxt2,
        ring, pair, prev, prev2, nxt, nxt2,
        ring, pair, prev, prev2, nxt, nxt2,
        up,
    )
    single = jax.ShapeDtypeStruct((rows, half), kind)
    double = jax.ShapeDtypeStruct((2, 2 * rows, half), kind)
    back = jax.ShapeDtypeStruct((2 * rows, rank), jnp.float32)
    double_spec = pl.BlockSpec((2, 2 * rows, block), lambda h, *_: (0, 0, h))
    back_spec = pl.BlockSpec((2 * rows, rank), lambda h, *_: (0, 0))
    out_shape = [
        single, single, double, double, double,
        back, back, back,
        jax.ShapeDtypeStruct((2 * heads, rank, HEAD_DIM), kind),
    ]
    out_specs = [
        at(0), at(0), double_spec, double_spec, double_spec,
        back_spec, back_spec, back_spec,
        pl.BlockSpec((2 * heads, rank, HEAD_DIM), lambda h, *_: (0, 0, 0)),
    ]
    pairs = 10 * rows * rows * heads
    return pl.pallas_call(
        attend_kernel,
        grid_spec=pltpu.PrefetchScalarGridSpec(
            num_scalar_prefetch=3,
            grid=(steps,),
            in_specs=in_specs,
            out_specs=out_specs,
            scratch_shapes=[
                pltpu.VMEM((5 * rows, 2 * rows), jnp.float32),
                pltpu.VMEM((2 * rows, HEAD_DIM), jnp.float32),
                pltpu.VMEM((6 * rows, half), kind),
            ],
        ),
        out_shape=out_shape,
        compiler_params=pltpu.CompilerParams(
            vmem_limit_bytes=VMEM_LIMIT, dimension_semantics=("arbitrary",)
        ),
        cost_estimate=pl.CostEstimate(
            flops=10 * pairs * HEAD_DIM, bytes_accessed=12 << 20, transcendentals=pairs
        ),
    )(place, lengths, versions, *operands)


def spread_kernel(mine, from_next, from_prev, theirs, x, up_send, out):
    rows, rank = theirs.shape
    share = out.shape[2] - rank
    back_rows = mine[:rows] + from_next[:rows] + from_prev[:rows] + theirs[...]
    back_rows = back_rows.astype(jnp.bfloat16)
    part = contract(back_rows, x[...], 0, 0).astype(jnp.bfloat16)
    for i in range(out.shape[0]):
        out[i, :, :share] = part[:, i * share : (i + 1) * share]
        out[i, :, share:] = up_send[i]


def spread(mine, from_next, from_prev, theirs, x, up_send):
    rows, rank = theirs.shape
    replicas = up_send.shape[0]
    share = x.shape[1] // replicas
    steps = 1
    each = replicas // steps
    full = lambda a: pl.BlockSpec(a.shape, lambda i: (0, 0))
    return pl.pallas_call(
        spread_kernel,
        grid=(steps,),
        out_shape=jax.ShapeDtypeStruct((replicas, rank, share + HEAD_DIM), jnp.bfloat16),
        in_specs=[
            full(mine), full(from_next), full(from_prev), full(theirs),
            pl.BlockSpec((rows, each * share), lambda i: (0, i)),
            pl.BlockSpec((each, rank, HEAD_DIM), lambda i: (i, 0, 0)),
        ],
        out_specs=pl.BlockSpec((each, rank, share + HEAD_DIM), lambda i: (i, 0, 0)),
        compiler_params=pltpu.CompilerParams(vmem_limit_bytes=VMEM_LIMIT),
    )(mine, from_next, from_prev, theirs, x, up_send)


def fold_kernel(place, parts, keep, send, *, norm):
    rank = parts.shape[1]
    total = parts[0].astype(jnp.float32)
    for i in range(1, parts.shape[0]):
        total = total + parts[i].astype(jnp.float32)
    total = total * norm
    share = total.shape[1] - HEAD_DIM
    down, up = total[:, :share].T, total[:, share:]
    cut = share // 2

    def write(first, second):
        first[:cut] = down[:cut]
        first[cut:] = up[: rank // 2]
        second[:cut] = down[cut:]
        second[cut:] = up[rank // 2 :]

    pl.when(place[0] == 0)(lambda: write(keep, send))
    pl.when(place[0] == 1)(lambda: write(send, keep))


def assemble_kernel(place, both, dq, pair_both, pair_dq, dk_out, dv_out, dq_out):
    rows, half = dq.shape

    def write(own, other):
        dk_out[:, own] = both[0, :rows]
        dv_out[:, own] = both[1, :rows]
        dq_out[:, own] = dq[...]
        dk_out[:, other] = pair_both[0]
        dv_out[:, other] = pair_both[1]
        dq_out[:, other] = pair_dq[...]

    left, right = slice(0, half), slice(half, 2 * half)
    pl.when(place[0] == 0)(lambda: write(left, right))
    pl.when(place[0] == 1)(lambda: write(right, left))


def simple(kernel, out_shape, place, *operands):
    smem, spec = pl.BlockSpec(memory_space=pltpu.SMEM), pl.BlockSpec(memory_space=pltpu.VMEM)
    return pl.pallas_call(
        kernel,
        out_shape=out_shape,
        in_specs=[smem] + [spec] * len(operands),
        out_specs=[spec] * len(out_shape),
        compiler_params=pltpu.CompilerParams(vmem_limit_bytes=VMEM_LIMIT),
    )(place, *operands)


def per_device(
    normed_input, queries, rotated_key_rows, frozen_value_rows, cotangent,
    adapter_down_weight, adapter_up_weight, document_lengths, versions,
):
    rows, width = queries.shape
    half = width // 2
    rank = adapter_down_weight.shape[1]
    sequence_count = lax.axis_size("seq")
    replicas = lax.axis_size("dp")
    shard = lax.axis_index("seq")
    y, z = shard % 2, shard // 2
    place = jnp.stack([y, z]).astype(jnp.int32)
    to_pair = lambda a: shifted(a, "seq", lambda i: i ^ 1)
    to_next = lambda a: shifted(a, "seq", lambda i: i + 2)
    to_prev = lambda a: shifted(a, "seq", lambda i: i - 2)
    after = lambda *a: lax.optimization_barrier(a)
    shape = jax.ShapeDtypeStruct
    wide, narrow = jnp.float32, jnp.bfloat16

    pair_send, ring, q_send = prepare(
        place, normed_input, adapter_down_weight, adapter_up_weight, frozen_value_rows,
        rotated_key_rows, queries, cotangent,
    )
    pair, prev, nxt = to_pair(pair_send), to_next(ring), to_prev(ring)
    pair, q_send = after(pair, q_send)
    prev2, nxt2 = to_next(pair), to_prev(pair)
    q_pair = to_pair(q_send)

    dq, dq_send, mid, out_prev, out_next, back, back_prev, back_next, up_send = attend(
        place, document_lengths, versions, queries, cotangent, rotated_key_rows, ring,
        adapter_up_weight, q_pair, pair, prev, prev2, nxt, nxt2,
    )
    from_next, from_prev = to_prev(back_prev), to_next(back_next)
    from_next, from_prev, dq_send, out_prev, out_next = after(
        from_next, from_prev, dq_send, out_prev, out_next
    )
    theirs = to_pair(back[rows:] + from_next[rows:] + from_prev[rows:])
    payload = spread(back, from_next, from_prev, theirs, normed_input, up_send)
    parts = lax.all_to_all(payload, "dp", 0, 0, tiled=True)
    dq_came = to_pair(dq_send)
    total = mid.astype(wide) + to_prev(out_prev).astype(wide) + to_next(out_next).astype(wide)
    total = total.astype(narrow)

    norm = adapter_scale / math.sqrt(rows * sequence_count * replicas)
    piece = shape(((parts.shape[2] - HEAD_DIM + rank) // 2, rank), wide)
    keep, give = simple(functools.partial(fold_kernel, norm=norm), [piece, piece], place, parts)
    given = to_pair(give)
    given, total_send = after(given, total[:, rows:])
    came = to_pair(total_send)
    count = sequence_count // 2
    columns = [list(range(c, sequence_count, 2)) for c in range(2)]
    copies = jnp.broadcast_to((keep + given).astype(narrow)[None], (count,) + keep.shape)
    sums = lax.all_to_all(copies, "seq", 0, 0, tiled=True, axis_index_groups=columns)
    mine = jnp.sum(sums.astype(wide), axis=0)
    other = to_pair(mine)
    whole = shape((rows, width), narrow)
    dk, dv, dq = simple(assemble_kernel, [whole] * 3, place, total, dq, came, dq_came)
    halves = [jnp.where(y == 0, mine, other), jnp.where(y == 0, other, mine)]
    cut = mine.shape[0] - rank // 2
    down_gradient = jnp.concatenate([a[:cut] for a in halves], axis=0)
    up_gradient = jnp.concatenate([a[cut:] for a in halves], axis=0)
    return dq, dk, dv, down_gradient, up_gradient


def solution(mesh):
    tokens = P(("dp", "seq"), None)
    in_specs = (tokens,) * 5 + (P(), P(), P("dp", None), P("dp", None))
    out_specs = (tokens,) * 3 + (P("dp", None), P(None, "dp"))
    return jax.shard_map(
        per_device, mesh=mesh, in_specs=in_specs, out_specs=out_specs, check_vma=False
    )
```

time: 187 us -> 150 us (0.80)
  blocking collectives: 42.3 us -> 0 us
  waiting for transfers between devices: 44.1 us -> 58.2 us
  local copies, waits for them, and re-layouts: 12.8 us -> 5.33 us
  Pallas kernels: 20.3 us -> 26 us
  starting transfers between devices: 58.1 us -> 53.6 us
    all_to_all x2 -> x0, blocking collectives: 42.3 us -> none  [the longest x1 22.6 us: per_device(): lax.all_to_all(joined.reshape(sequence_count, share, rank), 'seq', 0, 0,...]
    all_to_all x3 -> x2, waiting for transfers between devices: 9.29 us -> 26.8 us  [the longest x1 14.6 us: per_device(): parts = lax.all_to_all(payload, 'dp', 0, 0, tiled=True)]
    pallas_call x0 -> x3, Pallas kernels: none -> 8.32 us  [the longest x2 5.08 us: simple(): pl.pallas_call(kernel, out_shape=out_shape, in_specs=[smem] + [spec] * le...]
    unnamed x40 -> x32, local copies, waits for them, and re-layouts: 9.25 us -> 4.48 us
    ppermute x14 -> x15, waiting for transfers between devices: 34.9 us -> 31.5 us  [shifted(): return lax.ppermute(block, axis, route)]
    pallas_call x1, Pallas kernels: 16.9 us -> 13.7 us  [attend(): pl.pallas_call(attend_kernel, grid_spec=pltpu.PrefetchScalarGridSpec(num_...]
    all_to_all x3 -> x2, starting transfers between devices: 23.1 us -> 20.1 us  [the longest x1 12.6 us: per_device(): lax.all_to_all(copies, 'seq', 0, 0, tiled=True, axis_index_groups=columns)]
    ppermute x14 -> x15, starting transfers between devices: 35 us -> 33.5 us  [shifted(): return lax.ppermute(block, axis, route)]
  transfers between devices with their start and end apart: 17 -> 17, of which waited for: 8 -> 10; matrix products, arithmetic and copies ran while one was open for 3% -> 2% of each run, Pallas kernels for 9% -> 3%
where the time goes in v2:
time: 150 us; the launch traced here: 149 us
  waiting for transfers between devices  58.2 us (39%)
  starting transfers between devices  53.6 us (36%)
  Pallas kernels  26 us (17%)
  local copies, waits for them, and re-layouts  5.33 us (4%)
  other arithmetic  5.13 us (3%)
    ppermute x15, starting transfers between devices, shifted(): return lax.ppermute(block, axis, route)  33.5 us
    ppermute x15, waiting for transfers between devices, shifted(): return lax.ppermute(block, axis, route)  31.5 us
    all_to_all x1, waiting for transfers between devices, per_device(): parts = lax.all_to_all(payload, 'dp', 0, 0, tiled=True)  14.6 us
    pallas_call x1, Pallas kernels, attend(): pl.pallas_call(attend_kernel, grid_spec=pltpu.PrefetchScalarGridSpec(num_...  13.7 us
    all_to_all x1, starting transfers between devices, per_device(): lax.all_to_all(copies, 'seq', 0, 0, tiled=True, axis_index_groups=columns)  12.6 us
    all_to_all x1, waiting for transfers between devices, per_device(): lax.all_to_all(copies, 'seq', 0, 0, tiled=True, axis_index_groups=columns)  12.1 us
    all_to_all x1, starting transfers between devices, per_device(): parts = lax.all_to_all(payload, 'dp', 0, 0, tiled=True)  7.48 us
    pallas_call x2, Pallas kernels, simple(): pl.pallas_call(kernel, out_shape=out_shape, in_specs=[smem] + [spec] * le...  5.08 us
  transfers between devices with their start and end apart: 17, of which 10 were waited for; matrix products, arithmetic and copies ran while one was open for 2% of the time, Pallas kernels for 3%

profile of v2, /device:TPU:2, one launch (start us, length us, event | category | flops | bytes accessed | tf_op | source)
XLA Modules:
  0.0 149.2 jit_solution(4122342799858913043)
XLA Ops:
  0.6 0.7 pad_add_fusion.place
  1.3 4.0 %shard_map.128 = (bf16[128,2176]{1,0:T(8,128)(2,1)}, bf16[128,2176]{1,0:T(8,128)(2,1)}, bf16[128,2048]{1,0:T(8,128)(2,1)}) custom-call(s32[2]{0:T(128)} %pad_add_fusion.place, bf16[128,4096]{1,0:T(8,128)(2,1)} %x.3, bf16[4096,128]{1,0:T(8,128)(2,1)} %down.1, bf16[128,2048]{1,0:T(8,128)(2,1)} %up.3, bf16[128,2048]{1,0:T(8,128)(2,1)} %frozen.1, ...), custom_call_target="tpu_custom_call" | custom-call | tf_op jit(solution)/shard_map/pallas_call | solution.py:97
  5.3 1.7 %collective-permute-start = (bf16[128,2176]{1,0:T(8,128)(2,1)}, bf16[128,2176]{1,0:T(8,128)(2,1)S(1)}, u32[]{:S(2)}, u32[]{:S(2)}) collective-permute-start(bf16[128,2176]{1,0:T(8,128)(2,1)} %get-tuple-element.31), channel_id=1, source_target_pairs={{0,1},{1,0},{2,3},{3,2},{4,5},{5,4},{6,7},{7,6},{8,9},{9,8},{10,11... | collective-permute-start | bytes 1671176 | tf_op jit(solution)/shard_map/ppermute | solution.py:29
  7.0 1.3 collective-permute-start.4
  8.3 4.6 %collective-permute-start.2 = (bf16[128,2176]{1,0:T(8,128)(2,1)}, bf16[128,2176]{1,0:T(8,128)(2,1)S(1)}, u32[]{:S(2)}, u32[]{:S(2)}) collective-permute-start(bf16[128,2176]{1,0:T(8,128)(2,1)} %get-tuple-element.35.v_own.l_own), channel_id=1, source_target_pairs={{0,2},{1,3},{2,4},{3,5},{4,6},{5,7},{6,8},{7,9},{8,10},{9,11},{10,... | collective-permute-start | bytes 1671176 | tf_op jit(solution)/shard_map/ppermute | solution.py:29
  12.9 7.1 %collective-permute-done.k_pair.v_pair.l_pair = bf16[128,2176]{1,0:T(8,128)(2,1)S(1)} collective-permute-done((bf16[128,2176]{1,0:T(8,128)(2,1)}, bf16[128,2176]{1,0:T(8,128)(2,1)S(1)}, u32[]{:S(2)}, u32[]{:S(2)}) %collective-permute-start) | collective-permute-done | bytes 557088 | tf_op jit(solution)/shard_map/ppermute | solution.py:29
  20.0 1.3 collective-permute-start.5
  21.3 4.6 %collective-permute-start.3 = (bf16[128,2176]{1,0:T(8,128)(2,1)S(1)}, bf16[128,2176]{1,0:T(8,128)(2,1)S(1)}, u32[]{:S(2)}, u32[]{:S(2)}) collective-permute-start(bf16[128,2176]{1,0:T(8,128)(2,1)S(1)} %collective-permute-done.k_pair.v_pair.l_pair), channel_id=1, source_target_pairs={{0,2},{1,3},{2,4},{3,5},{4,6},{5,7},{6,8},{7,9},{8,10},{9,11},{10,... | collective-permute-start | bytes 1671176 | tf_op jit(solution)/shard_map/ppermute | solution.py:29
  25.9 1.8 %collective-permute-start.1 = (bf16[128,2048]{1,0:T(8,128)(2,1)}, bf16[128,2048]{1,0:T(8,128)(2,1)S(1)}, u32[]{:S(2)}, u32[]{:S(2)}) collective-permute-start(bf16[128,2048]{1,0:T(8,128)(2,1)} %get-tuple-element.33), channel_id=1, source_target_pairs={{0,1},{1,0},{2,3},{3,2},{4,5},{5,4},{6,7},{7,6},{8,9},{9,8},{10,11... | collective-permute-start | bytes 1572872 | tf_op jit(solution)/shard_map/ppermute | solution.py:29
  27.7 0.0 collective-permute-done.4.k_next.v_next.l_next
  27.7 11.0 %collective-permute-done.1.q_pair.g_pair = bf16[128,2048]{1,0:T(8,128)(2,1)S(1)} collective-permute-done((bf16[128,2048]{1,0:T(8,128)(2,1)}, bf16[128,2048]{1,0:T(8,128)(2,1)S(1)}, u32[]{:S(2)}, u32[]{:S(2)}) %collective-permute-start.1) | collective-permute-done | bytes 524320 | tf_op jit(solution)/shard_map/ppermute | solution.py:29
  38.8 0.7 copy-done.7
  39.6 0.2 copy-done.5
  39.8 0.8 copy-done.6
  40.6 13.7 %shard_map.129 = (bf16[128,1024]{1,0:T(8,128)(2,1)}, bf16[128,1024]{1,0:T(8,128)(2,1)}, bf16[2,256,1024]{2,1,0:T(8,128)(2,1)}, bf16[2,256,1024]{2,1,0:T(8,128)(2...) custom-call(s32[2]{0:T(128)} %pad_add_fusion.place, ...), custom_call_target="tpu_custom_call" | custom-call | flops 1677721600 | bytes 12582912 | tf_op jit(solution)/shard_map/pallas_call | solution.py:312
  54.3 1.3 collective-permute-start.6
  55.6 4.6 %collective-permute-start.7 = (f32[256,128]{1,0:T(8,128)}, f32[256,128]{1,0:T(8,128)S(1)}, u32[]{:S(2)}, u32[]{:S(2)}) collective-permute-start(f32[256,128]{1,0:T(8,128)} %get-tuple-element.38), channel_id=1, source_target_pairs={{0,2},{1,3},{2,4},{3,5},{4,6},{5,7},{6,8},{7,9},{8,10},{9,11},{10,... | collective-permute-start | bytes 393224 | tf_op jit(solution)/shard_map/ppermute | solution.py:29
  60.1 1.2 collective-permute-done.6.from_next
  61.3 1.6 %collective-permute-done.7.from_prev = f32[256,128]{1,0:T(8,128)S(1)} collective-permute-done((f32[256,128]{1,0:T(8,128)}, f32[256,128]{1,0:T(8,128)S(1)}, u32[]{:S(2)}, u32[]{:S(2)}) %collective-permute-start.7) | collective-permute-done | bytes 131104 | tf_op jit(solution)/shard_map/ppermute | solution.py:29
  63.0 0.9 slice_add_fusion
  63.9 1.7 %collective-permute-start.10 = (f32[128,128]{1,0:T(8,128)S(1)}, f32[128,128]{1,0:T(8,128)S(1)}, u32[]{:S(2)}, u32[]{:S(2)}) collective-permute-start(f32[128,128]{1,0:T(8,128)S(1)} %slice_add_fusion), channel_id=1, source_target_pairs={{0,1},{1,0},{2,3},{3,2},{4,5},{5,4},{6,7},{7,6},{8,9},{9,8},{10,11... | collective-permute-start | bytes 196616 | tf_op jit(solution)/shard_map/ppermute | solution.py:29
  65.5 2.7 %collective-permute-done.10.theirs = f32[128,128]{1,0:T(8,128)S(1)} collective-permute-done((f32[128,128]{1,0:T(8,128)S(1)}, f32[128,128]{1,0:T(8,128)S(1)}, u32[]{:S(2)}, u32[]{:S(2)}) %collective-permute-start.10) | collective-permute-done | bytes 65568 | tf_op jit(solution)/shard_map/ppermute | solution.py:29
  68.2 0.6 copy-done.14
  68.8 3.2 %shard_map.130 = bf16[16,128,384]{2,1,0:T(8,128)(2,1)} custom-call(f32[256,128]{1,0:T(8,128)} %get-tuple-element.45.mine, f32[256,128]{1,0:T(8,128)} %copy-done.10, f32[256,128]{1,0:T(8,128)} %copy-done.11, f32[128,128]{1,0:T(8,128)} %copy-done.14, bf16[128,4096]{1,0:T(8,128)(2,1)} %x.3, bf16[16,128,128]{2,1,0:T(8,128)(2,1)} %get-tuple-element.48.up_send), custom_call_target="tpu_custom_call" | custom-call | tf_op jit(solution)/shard_map/pallas_call | solution.py:353
  72.1 7.5 %all-to-all-start = ((bf16[16,128,384]{2,1,0:T(8,128)(2,1)}), bf16[16,128,384]{2,1,0:T(8,128)(2,1)S(1)}, u32[]{:S(2)}, u32[]{:S(2)}) async-start(bf16[16,128,384]{2,1,0:T(8,128)(2,1)} %shard_map.130), calls=%async_computation | async-start | bytes 3145728 | tf_op jit(solution)/shard_map/all_to_all | solution.py:452
  79.6 1.4 collective-permute-start.8
  81.0 5.9 %collective-permute-start.9 = (bf16[2,256,1024]{2,1,0:T(8,128)(2,1)}, bf16[2,256,1024]{2,1,0:T(8,128)(2,1)}, u32[]{:S(2)}, u32[]{:S(2)}) collective-permute-start(bf16[2,256,1024]{2,1,0:T(8,128)(2,1)} %get-tuple-element.43), channel_id=1, source_target_pairs={{0,2},{1,3},{2,4},{3,5},{4,6},{5,7},{6,8},{7,9},{8,10},{9,11},{10,... | collective-permute-start | bytes 3145736 | tf_op jit(solution)/shard_map/ppermute | solution.py:29
  86.9 14.6 %all-to-all-done.parts = bf16[16,128,384]{2,1,0:T(8,128)(2,1)S(1)} async-done(((bf16[16,128,384]{2,1,0:T(8,128)(2,1)}), bf16[16,128,384]{2,1,0:T(8,128)(2,1)S(1)}, u32[]{:S(2)}, u32[]{:S(2)}) %all-to-all-start) | async-done | bytes 1572896 | tf_op jit(solution)/shard_map/all_to_all | solution.py:452
  101.5 1.2 copy-done.1
  102.6 2.3 %shard_map.131 = (f32[192,128]{1,0:T(8,128)}, f32[192,128]{1,0:T(8,128)}) custom-call(s32[2]{0:T(128)} %pad_add_fusion.place, bf16[16,128,384]{2,1,0:T(8,128)(2,1)} %copy-done.1), custom_call_target="tpu_custom_call" | custom-call | tf_op jit(solution)/shard_map/pallas_call | solution.py:405
  105.0 0.7 collective-permute-start.11
  105.6 2.1 %collective-permute-done.8 = bf16[2,256,1024]{2,1,0:T(8,128)(2,1)} collective-permute-done((bf16[2,256,1024]{2,1,0:T(8,128)(2,1)}, bf16[2,256,1024]{2,1,0:T(8,128)(2,1)}, u32[]{:S(2)}, u32[]{:S(2)}) %collective-permute-start.8) | collective-permute-done | bytes 1048608 | tf_op jit(solution)/shard_map/ppermute | solution.py:29
  107.7 1.2 collective-permute-done.9
  108.9 2.2 %add_convert_fusion.both = bf16[2,256,1024]{2,1,0:T(8,128)(2,1)S(1)} fusion(bf16[2,256,1024]{2,1,0:T(8,128)(2,1)} %collective-permute-done.9, bf16[2,256,1024]{2,1,0:T(8,128)(2,1)} %collective-permute-done.8, bf16[2,256,1024]{2,1,0:T(8,128)(2,1)S(1)} %copy-done.8), kind=kLoop, calls=%fused_computation | loop fusion | flops 3145728 | bytes 4194304 | tf_op jit(solution)/shard_map/convert_element_type | solution.py:455
  111.1 0.0 copy-start.15
  111.2 0.8 broadcast_in_dim.2
  112.0 12.6 %all-to-all-start.1 = ((bf16[8,192,128]{2,1,0:T(8,128)(2,1)}), bf16[8,192,128]{2,1,0:T(8,128)(2,1)S(1)}, u32[]{:S(2)}, u32[]{:S(2)}) async-start(bf16[8,192,128]{2,1,0:T(8,128)(2,1)} %broadcast_in_dim.2), calls=%async_computation.1 | async-start | bytes 786432 | tf_op jit(solution)/shard_map/all_to_all | solution.py:466
  124.7 0.7 collective-permute-start.12
  125.3 1.3 collective-permute-start.13
  126.7 12.1 %all-to-all-done.1 = bf16[8,192,128]{2,1,0:T(8,128)(2,1)S(1)} async-done(((bf16[8,192,128]{2,1,0:T(8,128)(2,1)}), bf16[8,192,128]{2,1,0:T(8,128)(2,1)S(1)}, u32[]{:S(2)}, u32[]{:S(2)}) %all-to-all-start.1) | async-done | bytes 393248 | tf_op jit(solution)/shard_map/all_to_all | solution.py:466
  138.8 0.1 convert_reduce_fusion
  138.9 0.8 collective-permute-start.14
  139.7 4.5 %collective-permute-done.13.pair_dq = bf16[128,1024]{1,0:T(8,128)(2,1)S(1)} collective-permute-done((bf16[128,1024]{1,0:T(8,128)(2,1)S(1)}, bf16[128,1024]{1,0:T(8,128)(2,1)S(1)}, u32[]{:S(2)}, u32[]{:S(2)}) %collective-permute-start.13) | collective-permute-done | bytes 262176 | tf_op jit(solution)/shard_map/ppermute | solution.py:29
  144.2 0.7 copy-done.12
  144.9 0.2 copy-done.9
  145.1 2.8 %shard_map.132 = (bf16[128,2048]{1,0:T(8,128)(2,1)}, bf16[128,2048]{1,0:T(8,128)(2,1)}, bf16[128,2048]{1,0:T(8,128)(2,1)}) custom-call(s32[2]{0:T(128)} %pad_add_fusion.place, bf16[2,256,1024]{2,1,0:T(8,128)(2,1)} %copy-done, bf16[128,1024]{1,0:T(8,128)(2,1)} %get-tuple-element.44.dq, bf16[2,128,1024]{2,1,0:T(8,128)(2,1)} %copy-done.9, ...), custom_call_target="tpu_custom_call" | custom-call | tf_op jit(solution)/shard_map/pallas_call | solution.py:405
  147.9 0.7 pad_maximum_fusion
  148.6 0.6 pad_maximum_fusion.1
  (37 shorter events, 0.1 us)
Async XLA Ops:
  5.3 14.7 %collective-permute-start = (bf16[128,2176]{1,0:T(8,128)(2,1)}, bf16[128,2176]{1,0:T(8,128)(2,1)S(1)}, u32[]{:S(2)}, u32[]{:S(2)}) collective-permute-start(bf16[128,2176]{1,0:T(8,128)(2,1)} %get-tuple-element.31), channel_id=1, source_target_pairs={{0,1},{1,0},{2,3},{3,2},{4,5},{5,4},{6,7},{7,6},{8,9},{9,8},{10,11... | collective-permute-start | bytes 1671176 | tf_op jit(solution)/shard_map/ppermute | solution.py:29
  7.0 20.7 %collective-permute-start.4 = (bf16[128,2176]{1,0:T(8,128)(2,1)}, bf16[128,2176]{1,0:T(8,128)(2,1)S(1)}, u32[]{:S(2)}, u32[]{:S(2)}) collective-permute-start(bf16[128,2176]{1,0:T(8,128)(2,1)} %get-tuple-element.35.v_own.l_own), channel_id=1, source_target_pairs={{2,0},{3,1},{4,2},{5,3},{6,4},{7,5},{8,6},{9,7},{10,8},{11,9},{12,... | collective-permute-start | bytes 1671176 | tf_op jit(solution)/shard_map/ppermute | solution.py:29
  8.3 19.4 %collective-permute-start.2 = (bf16[128,2176]{1,0:T(8,128)(2,1)}, bf16[128,2176]{1,0:T(8,128)(2,1)S(1)}, u32[]{:S(2)}, u32[]{:S(2)}) collective-permute-start(bf16[128,2176]{1,0:T(8,128)(2,1)} %get-tuple-element.35.v_own.l_own), channel_id=1, source_target_pairs={{0,2},{1,3},{2,4},{3,5},{4,6},{5,7},{6,8},{7,9},{8,10},{9,11},{10,... | collective-permute-start | bytes 1671176 | tf_op jit(solution)/shard_map/ppermute | solution.py:29
  20.0 18.8 %copy-start.2 = (bf16[128,2176]{1,0:T(8,128)(2,1)}, bf16[128,2176]{1,0:T(8,128)(2,1)S(1)}, u32[]{:S(2)}) copy-start(bf16[128,2176]{1,0:T(8,128)(2,1)S(1)} %collective-permute-done.k_pair.v_pair.l_pair) | copy-start | bytes 1671172
  20.0 18.8 %collective-permute-start.5 = (bf16[128,2176]{1,0:T(8,128)(2,1)S(1)}, bf16[128,2176]{1,0:T(8,128)(2,1)S(1)}, u32[]{:S(2)}, u32[]{:S(2)}) collective-permute-start(bf16[128,2176]{1,0:T(8,128)(2,1)S(1)} %collective-permute-done.k_pair.v_pair.l_pair), channel_id=1, source_target_pairs={{2,0},{3,1},{4,2},{5,3},{6,4},{7,5},{8,6},{9,7},{10,8},{11,9},{12,... | collective-permute-start | bytes 1671176 | tf_op jit(solution)/shard_map/ppermute | solution.py:29
  21.3 17.5 %collective-permute-start.3 = (bf16[128,2176]{1,0:T(8,128)(2,1)S(1)}, bf16[128,2176]{1,0:T(8,128)(2,1)S(1)}, u32[]{:S(2)}, u32[]{:S(2)}) collective-permute-start(bf16[128,2176]{1,0:T(8,128)(2,1)S(1)} %collective-permute-done.k_pair.v_pair.l_pair), channel_id=1, source_target_pairs={{0,2},{1,3},{2,4},{3,5},{4,6},{5,7},{6,8},{7,9},{8,10},{9,11},{10,... | collective-permute-start | bytes 1671176 | tf_op jit(solution)/shard_map/ppermute | solution.py:29
  25.9 12.9 %collective-permute-start.1 = (bf16[128,2048]{1,0:T(8,128)(2,1)}, bf16[128,2048]{1,0:T(8,128)(2,1)S(1)}, u32[]{:S(2)}, u32[]{:S(2)}) collective-permute-start(bf16[128,2048]{1,0:T(8,128)(2,1)} %get-tuple-element.33), channel_id=1, source_target_pairs={{0,1},{1,0},{2,3},{3,2},{4,5},{5,4},{6,7},{7,6},{8,9},{9,8},{10,11... | collective-permute-start | bytes 1572872 | tf_op jit(solution)/shard_map/ppermute | solution.py:29
  27.7 11.1 %copy-start.3 = (bf16[128,2176]{1,0:T(8,128)(2,1)}, bf16[128,2176]{1,0:T(8,128)(2,1)S(1)}, u32[]{:S(2)}) copy-start(bf16[128,2176]{1,0:T(8,128)(2,1)S(1)} %collective-permute-done.4.k_next.v_next.l_next) | copy-start | bytes 1671172
  27.7 11.1 %copy-start.4 = (bf16[128,2176]{1,0:T(8,128)(2,1)}, bf16[128,2176]{1,0:T(8,128)(2,1)S(1)}, u32[]{:S(2)}) copy-start(bf16[128,2176]{1,0:T(8,128)(2,1)S(1)} %collective-permute-done.2.k_prev.v_prev.l_prev) | copy-start | bytes 1671172
  38.8 0.8 copy-start.7
  38.8 1.0 copy-start.5
  39.8 0.8 copy-start.6
  54.3 7.1 %collective-permute-start.6 = (f32[256,128]{1,0:T(8,128)}, f32[256,128]{1,0:T(8,128)S(1)}, u32[]{:S(2)}, u32[]{:S(2)}) collective-permute-start(f32[256,128]{1,0:T(8,128)} %get-tuple-element.37), channel_id=1, source_target_pairs={{2,0},{3,1},{4,2},{5,3},{6,4},{7,5},{8,6},{9,7},{10,8},{11,9},{12,... | collective-permute-start | bytes 393224 | tf_op jit(solution)/shard_map/ppermute | solution.py:29
  55.6 7.4 %collective-permute-start.7 = (f32[256,128]{1,0:T(8,128)}, f32[256,128]{1,0:T(8,128)S(1)}, u32[]{:S(2)}, u32[]{:S(2)}) collective-permute-start(f32[256,128]{1,0:T(8,128)} %get-tuple-element.38), channel_id=1, source_target_pairs={{0,2},{1,3},{2,4},{3,5},{4,6},{5,7},{6,8},{7,9},{8,10},{9,11},{10,... | collective-permute-start | bytes 393224 | tf_op jit(solution)/shard_map/ppermute | solution.py:29
  61.3 6.9 %copy-start.10 = (f32[256,128]{1,0:T(8,128)}, f32[256,128]{1,0:T(8,128)S(1)}, u32[]{:S(2)}) copy-start(f32[256,128]{1,0:T(8,128)S(1)} %collective-permute-done.6.from_next) | copy-start | bytes 393220
  62.9 5.3 %copy-start.11 = (f32[256,128]{1,0:T(8,128)}, f32[256,128]{1,0:T(8,128)S(1)}, u32[]{:S(2)}) copy-start(f32[256,128]{1,0:T(8,128)S(1)} %collective-permute-done.7.from_prev) | copy-start | bytes 393220
  63.9 4.4 %collective-permute-start.10 = (f32[128,128]{1,0:T(8,128)S(1)}, f32[128,128]{1,0:T(8,128)S(1)}, u32[]{:S(2)}, u32[]{:S(2)}) collective-permute-start(f32[128,128]{1,0:T(8,128)S(1)} %slice_add_fusion), channel_id=1, source_target_pairs={{0,1},{1,0},{2,3},{3,2},{4,5},{5,4},{6,7},{7,6},{8,9},{9,8},{10,11... | collective-permute-start | bytes 196616 | tf_op jit(solution)/shard_map/ppermute | solution.py:29
  68.2 0.6 copy-start.14
  72.1 29.4 %all-to-all-start = ((bf16[16,128,384]{2,1,0:T(8,128)(2,1)}), bf16[16,128,384]{2,1,0:T(8,128)(2,1)S(1)}, u32[]{:S(2)}, u32[]{:S(2)}) async-start(bf16[16,128,384]{2,1,0:T(8,128)(2,1)} %shard_map.130), calls=%async_computation | async-start | bytes 3145728 | tf_op jit(solution)/shard_map/all_to_all | solution.py:452
  79.6 29.3 %copy-start.8 = (bf16[2,256,1024]{2,1,0:T(8,128)(2,1)S(1)}, bf16[2,256,1024]{2,1,0:T(8,128)(2,1)}, u32[]{:S(2)}) copy-start(bf16[2,256,1024]{2,1,0:T(8,128)(2,1)} %get-tuple-element.36) | copy-start | bytes 3145732
  79.6 28.2 %collective-permute-start.8 = (bf16[2,256,1024]{2,1,0:T(8,128)(2,1)}, bf16[2,256,1024]{2,1,0:T(8,128)(2,1)}, u32[]{:S(2)}, u32[]{:S(2)}) collective-permute-start(bf16[2,256,1024]{2,1,0:T(8,128)(2,1)} %get-tuple-element.42), channel_id=1, source_target_pairs={{2,0},{3,1},{4,2},{5,3},{6,4},{7,5},{8,6},{9,7},{10,8},{11,9},{12,... | collective-permute-start | bytes 3145736 | tf_op jit(solution)/shard_map/ppermute | solution.py:29
  81.0 27.9 %collective-permute-start.9 = (bf16[2,256,1024]{2,1,0:T(8,128)(2,1)}, bf16[2,256,1024]{2,1,0:T(8,128)(2,1)}, u32[]{:S(2)}, u32[]{:S(2)}) collective-permute-start(bf16[2,256,1024]{2,1,0:T(8,128)(2,1)} %get-tuple-element.43), channel_id=1, source_target_pairs={{0,2},{1,3},{2,4},{3,5},{4,6},{5,7},{6,8},{7,9},{8,10},{9,11},{10,... | collective-permute-start | bytes 3145736 | tf_op jit(solution)/shard_map/ppermute | solution.py:29
  101.5 1.2 copy-start.1
  105.0 6.2 %collective-permute-start.11 = (f32[192,128]{1,0:T(8,128)}, f32[192,128]{1,0:T(8,128)S(1)}, u32[]{:S(2)}, u32[]{:S(2)}) collective-permute-start(f32[192,128]{1,0:T(8,128)} %get-tuple-element.49), channel_id=1, source_target_pairs={{0,1},{1,0},{2,3},{3,2},{4,5},{5,4},{6,7},{7,6},{8,9},{9,8},{10,11... | collective-permute-start | bytes 294920 | tf_op jit(solution)/shard_map/ppermute | solution.py:29
  108.9 2.3 %copy-start.13 = (f32[192,128]{1,0:T(8,128)S(1)}, f32[192,128]{1,0:T(8,128)}, u32[]{:S(2)}) copy-start(f32[192,128]{1,0:T(8,128)} %get-tuple-element.55) | copy-start | bytes 294916
  111.1 33.1 %copy-start = (bf16[2,256,1024]{2,1,0:T(8,128)(2,1)}, bf16[2,256,1024]{2,1,0:T(8,128)(2,1)S(1)}, u32[]{:S(2)}) copy-start(bf16[2,256,1024]{2,1,0:T(8,128)(2,1)S(1)} %add_convert_fusion.both) | copy-start | bytes 3145732
  111.1 14.2 %copy-start.15 = (bf16[128,1024]{1,0:T(8,128)(2,1)S(1)}, bf16[128,1024]{1,0:T(8,128)(2,1)}, u32[]{:S(2)}) copy-start(bf16[128,1024]{1,0:T(8,128)(2,1)} %get-tuple-element.51) | copy-start | bytes 786436
  112.0 26.8 %all-to-all-start.1 = ((bf16[8,192,128]{2,1,0:T(8,128)(2,1)}), bf16[8,192,128]{2,1,0:T(8,128)(2,1)S(1)}, u32[]{:S(2)}, u32[]{:S(2)}) async-start(bf16[8,192,128]{2,1,0:T(8,128)(2,1)} %broadcast_in_dim.2), calls=%async_computation.1 | async-start | bytes 786432 | tf_op jit(solution)/shard_map/all_to_all | solution.py:466
  124.7 19.5 %collective-permute-start.12 = (bf16[2,128,1024]{2,1,0:T(8,128)(2,1)S(1)}, bf16[2,128,1024]{2,1,0:T(8,128)(2,1)S(1)}, u32[]{:S(2)}, u32[]{:S(2)}) collective-permute-start(bf16[2,128,1024]{2,1,0:T(8,128)(2,1)S(1)} %slice.32), channel_id=1, source_target_pairs={{0,1},{1,0},{2,3},{3,2},{4,5},{5,4},{6,7},{7,6},{8,9},{9,8},{10,11... | collective-permute-start | bytes 1572872 | tf_op jit(solution)/shard_map/ppermute | solution.py:29
  125.3 18.9 %collective-permute-start.13 = (bf16[128,1024]{1,0:T(8,128)(2,1)S(1)}, bf16[128,1024]{1,0:T(8,128)(2,1)S(1)}, u32[]{:S(2)}, u32[]{:S(2)}) collective-permute-start(bf16[128,1024]{1,0:T(8,128)(2,1)S(1)} %copy-done.15), channel_id=1, source_target_pairs={{0,1},{1,0},{2,3},{3,2},{4,5},{5,4},{6,7},{7,6},{8,9},{9,8},{10,11... | collective-permute-start | bytes 786440 | tf_op jit(solution)/shard_map/ppermute | solution.py:29
  138.9 9.0 %collective-permute-start.14 = (f32[192,128]{1,0:T(8,128)S(1)}, f32[192,128]{1,0:T(8,128)S(1)}, u32[]{:S(2)}, u32[]{:S(2)}) collective-permute-start(f32[192,128]{1,0:T(8,128)S(1)} %convert_reduce_fusion), channel_id=1, source_target_pairs={{0,1},{1,0},{2,3},{3,2},{4,5},{5,4},{6,7},{7,6},{8,9},{9,8},{10,11... | collective-permute-start | bytes 294920 | tf_op jit(solution)/shard_map/ppermute | solution.py:29
  144.2 0.7 copy-start.12
  144.2 0.9 copy-start.9

commit v3 on v2

v3 whole, which is shorter than its diff:
```python
import functools
import math

import jax
import jax.numpy as jnp
from jax import lax
from jax.experimental import pallas as pl
from jax.experimental.pallas import tpu as pltpu
from jax.sharding import PartitionSpec as P

HEAD_DIM = 128
VERSIONS = 4

adapter_scale = 0.5
masked_score = -1e30
VMEM_LIMIT = 60 * 1024 * 1024
HEADS_PER_STEP = 4


def contract(a, b, dim_a, dim_b):
    return lax.dot_general(
        a, b, (((dim_a,), (dim_b,)), ((), ())), preferred_element_type=jnp.float32
    )


def shifted(block, axis, target):
    count = lax.axis_size(axis)
    route = [(i, target(i) % count) for i in range(count)]
    return lax.ppermute(block, axis, route)


def prepare_kernel(
    place, x, down, up, frozen, keys, queries, grads,
    pair_out, ring_out, query_out, value_out, x_out,
    x_in, down_in, up_in, frozen_in, moved, values_v, low_v, sems,
):
    rows, rank = low_v.shape
    half = values_v.shape[2]
    y = place[0]
    own = pl.multiple_of(y * half, half)
    other = pl.multiple_of((1 - y) * half, half)
    used = []

    def copy(src, dst):
        done = pltpu.make_async_copy(src, dst, sems.at[len(used)])
        used.append(done)
        done.start()
        return done

    chunks = 4
    size = x.shape[1] // chunks
    parts = []
    for c in range(chunks):
        span = pl.ds(c * size, size)
        parts.append((copy(x.at[:, span], x_in.at[:, span]), copy(down.at[span], down_in.at[span])))
    left, right = pl.ds(0, half), pl.ds(half, half)
    route = [
        (keys, other, pair_out.at[:, left]),
        (keys, own, ring_out.at[:, left]),
        (queries, other, query_out.at[:, left]),
        (grads, other, query_out.at[:, right]),
    ]
    arriving = [copy(src.at[:, pl.ds(at, half)], moved.at[i]) for i, (src, at, _) in enumerate(route)]
    up_done = copy(up, up_in)
    frozen_done = copy(frozen, frozen_in)
    low = jnp.zeros((rows, rank), jnp.float32)
    for c, (a, b) in enumerate(parts):
        a.wait()
        b.wait()
        low += contract(x_in[:, c * size : (c + 1) * size], down_in[c * size : (c + 1) * size, :], 1, 0)
    low = low.astype(jnp.bfloat16)
    low_v[...] = low
    rest = []
    members = x_out.shape[0]
    share = x.shape[1] // (2 * members)
    for p in range(members):
        for slot in range(2):
            first = (4 * (p // 2) + 2 * slot + p % 2) * share
            rest.append(copy(x_in.at[:, pl.ds(first, share)], x_out.at[p, :, pl.ds(slot * share, share)]))
    for target in (pair_out.at[:, pl.ds(half, rank)], ring_out.at[:, pl.ds(2 * half, rank)]):
        rest.append(copy(low_v, target))
    for i, done in enumerate(arriving):
        done.wait()
        rest.append(copy(moved.at[i], route[i][2]))
    up_done.wait()
    frozen_done.wait()
    for i, (start, target) in enumerate(((own, ring_out.at[:, right]), (other, value_out))):
        lifted = contract(low, up_in[:, pl.ds(start, half)], 1, 0)
        base = frozen_in[:, pl.ds(start, half)].astype(jnp.float32)
        values_v[i] = (base + adapter_scale * lifted).astype(jnp.bfloat16)
        rest.append(copy(values_v.at[i], target))
    for done in rest:
        done.wait()


def prepare(place, x, down, up, frozen, keys, queries, grads, members):
    rows, width = keys.shape
    rank = down.shape[1]
    half = width // 2
    kind = jnp.bfloat16
    shapes = [
        (rows, half + rank), (rows, width + rank), (rows, width), (rows, half),
        (members, rows, x.shape[1] // members),
    ]
    anywhere = pl.BlockSpec(memory_space=pl.ANY)
    return pl.pallas_call(
        prepare_kernel,
        out_shape=[jax.ShapeDtypeStruct(s, kind) for s in shapes],
        in_specs=[pl.BlockSpec(memory_space=pltpu.SMEM)] + [anywhere] * 7,
        out_specs=[anywhere] * 5,
        scratch_shapes=[
            pltpu.VMEM(x.shape, kind),
            pltpu.VMEM(down.shape, kind),
            pltpu.VMEM(up.shape, kind),
            pltpu.VMEM(frozen.shape, kind),
            pltpu.VMEM((4, rows, half), kind),
            pltpu.VMEM((2, rows, half), kind),
            pltpu.VMEM((rows, rank), kind),
            pltpu.SemaphoreType.DMA((22 + 2 * members,)),
        ],
        compiler_params=pltpu.CompilerParams(vmem_limit_bytes=VMEM_LIMIT),
    )(place, x, down, up, frozen, keys, queries, grads)


def gather(refs, cols):
    return jnp.concatenate([r[:, cols] for r in refs], axis=0)


def against(main, far_a, far_b, other):
    rows = far_a.shape[0]
    far = jnp.concatenate(
        [contract(far_a, other[:rows], 1, 1), contract(far_b, other[rows:], 1, 1)], axis=1
    )
    return jnp.concatenate([contract(main, other, 1, 1), far], axis=0)


def onto(grid, other):
    rows = other.shape[0] // 2
    near = 4 * rows
    return (
        contract(grid[:near], other, 1, 0),
        contract(grid[near:, :rows], other[:rows], 1, 0),
        contract(grid[near:, rows:], other[rows:], 1, 0),
    )


def ordered(order, own, pair, prev, prev2, nxt, nxt2):
    pick = lambda a, b: (a, b) if order == 0 else (b, a)
    mid0, mid1 = pick(own, pair)
    far_prev, near_prev = pick(prev, prev2)
    near_next, far_next = pick(nxt, nxt2)
    return (near_prev, mid0, mid1, near_next), far_prev, far_next


def scatter(order, mid, prev, nxt, cols, main, far_a, far_b):
    rows = far_a.shape[0]
    first, second = (0, rows) if order == 0 else (rows, 0)

    def put(ref, at, val):
        ref[at : at + rows, cols] = val

    put(prev, second, main[:rows])
    put(mid, first, main[rows : 2 * rows])
    put(mid, second, main[2 * rows : 3 * rows])
    put(nxt, first, main[3 * rows :])
    put(prev, first, far_a)
    put(nxt, second, far_b)


def forward_kernel(
    place, lengths, versions,
    q_own, q_pair, g_own, g_pair,
    k_own, k_pair, k_prev, k_prev2, k_next, k_next2,
    l_own, l_pair, l_prev, l_prev2, l_next, l_next2,
    up,
    mid, prev, nxt, back_mid, back_prev, back_next, up_send, probs, scaled,
    bias, weight, dvs,
):
    rows = q_own.shape[0]
    documents = lengths.shape[1]
    step = pl.program_id(0)
    y, z = place[0], place[1]
    base = 2 * z * rows
    heads = dvs.shape[1] // HEAD_DIM

    @pl.when(step == 0)
    def _():
        ends, total = [], jnp.int32(0)
        for j in range(documents):
            total = total + lengths[0, j]
            ends.append(total)
        for b in range(2):
            pos = lax.broadcasted_iota(jnp.int32, (8, rows), 1) + base + b * rows
            first = jnp.zeros_like(pos)
            last = jnp.zeros_like(pos)
            for j in range(documents):
                first = jnp.where(pos >= ends[j], ends[j], first)
            for j in reversed(range(documents)):
                last = jnp.where(pos < ends[j], ends[j], last)
            first, last = first[:1], last[:1]
            for c, shift in enumerate((-1, 0, 1, 2, -2 if b == 0 else 3)):
                key_pos = lax.broadcasted_iota(jnp.int32, (rows, rows), 0) + base + shift * rows
                inside = (key_pos >= first) & (key_pos < last)
                bias[c * rows : (c + 1) * rows, b * rows : (b + 1) * rows] = jnp.where(
                    inside, jnp.float32(0.0), jnp.float32(masked_score)
                )
            row_pos = lax.broadcasted_iota(jnp.int32, (rows, HEAD_DIM), 0) + base + b * rows
            scale = jnp.zeros((rows, HEAD_DIM), jnp.float32)
            for j in range(documents):
                level = lax.shift_left(jnp.int32(1), versions[0, j]).astype(jnp.float32)
                level = level * (2.0 ** (1 - VERSIONS))
                begin = ends[j - 1] if j > 0 else 0
                scale = jnp.where(row_pos >= begin, level, scale)
            weight[b * rows : (b + 1) * rows, :] = scale

    factor = math.log2(math.e) / math.sqrt(HEAD_DIM)
    near = 4 * rows

    def work(order):
        pick = lambda own, pair: (own, pair) if order == 0 else (pair, own)
        ks, k_fp, k_fn = ordered(order, k_own, k_pair, k_prev, k_prev2, k_next, k_next2)
        for h in range(HEADS_PER_STEP):
            cols = slice(h * HEAD_DIM, (h + 1) * HEAD_DIM)
            q = gather(pick(q_own, q_pair), cols)
            g = weight[...] * gather(pick(g_own, g_pair), cols).astype(jnp.float32)
            g = g.astype(jnp.bfloat16)
            scaled[:, cols] = g
            s = against(gather(ks, cols), k_fp[:, cols], k_fn[:, cols], q) * factor + bias[...]
            e = jnp.exp2(s - jnp.max(s, axis=0, keepdims=True))
            p = (e * (1.0 / jnp.sum(e, axis=0, keepdims=True))).astype(jnp.bfloat16)
            probs[h] = p
            small = [a.astype(jnp.bfloat16) for a in onto(p, g)]
            scatter(order, mid, prev, nxt, cols, *small)
            at = step * (HEADS_PER_STEP * HEAD_DIM)
            at = pl.ds(pl.multiple_of(at, HEAD_DIM) + h * HEAD_DIM, HEAD_DIM)
            dvs[:near, at] = small[0]
            dvs[near : near + rows, at] = small[1]
            dvs[near + rows :, at] = small[2]

        @pl.when(step == pl.num_programs(0) - 1)
        def _():
            ls, l_fp, l_fn = ordered(order, l_own, l_pair, l_prev, l_prev2, l_next, l_next2)
            low = jnp.concatenate([r[...] for r in (*ls, l_fp, l_fn)], axis=0)
            part = contract(low, dvs[...], 0, 0).astype(jnp.bfloat16)
            for h in range(2 * heads):
                slot = slice((1 + (h // 2) % 2) * HEAD_DIM, (2 + (h // 2) % 2) * HEAD_DIM)
                local = h - order * heads
                if 0 <= local < heads:
                    block = part[:, local * HEAD_DIM : (local + 1) * HEAD_DIM]
                else:
                    block = jnp.zeros((part.shape[0], HEAD_DIM), jnp.bfloat16)
                up_send[2 * (h // 4) + h % 2, :, slot] = block
            up_send[:, :, :HEAD_DIM] = jnp.zeros(up_send.shape[:2] + (HEAD_DIM,), jnp.bfloat16)
            full = contract(dvs[...], up[...], 1, 1)
            a, b = (0, rows) if order == 0 else (rows, 0)
            places = (
                (back_prev, b), (back_mid, a), (back_mid, b), (back_next, a), (back_prev, a), (back_next, b),
            )
            for c, (ref, at) in enumerate(places):
                ref[at : at + rows, :] = full[c * rows : (c + 1) * rows]

    for order in range(2):
        pl.when(y == order)(functools.partial(work, order))


def backward_kernel(
    place,
    q_own, q_pair, scaled, probs,
    k_own, k_pair, k_prev, k_prev2, k_next, k_next2,
    v_own, v_pair, v_prev, v_prev2, v_next, v_next2,
    dq_own, dq_pair, mid, prev, nxt,
):
    rows = q_own.shape[0]
    near = 4 * rows
    score_scale = 1.0 / math.sqrt(HEAD_DIM)

    def work(order):
        pick = lambda own, pair: (own, pair) if order == 0 else (pair, own)
        ks, k_fp, k_fn = ordered(order, k_own, k_pair, k_prev, k_prev2, k_next, k_next2)
        vs, v_fp, v_fn = ordered(order, v_own, v_pair, v_prev, v_prev2, v_next, v_next2)
        dq0, dq1 = pick(dq_own, dq_pair)
        for h in range(HEADS_PER_STEP):
            cols = slice(h * HEAD_DIM, (h + 1) * HEAD_DIM)
            q = gather(pick(q_own, q_pair), cols)
            dp = against(gather(vs, cols), v_fp[:, cols], v_fn[:, cols], scaled[:, cols])
            wide = probs[h].astype(jnp.float32)
            delta = jnp.sum(wide * dp, axis=0, keepdims=True)
            ds = (wide * (dp - delta)).astype(jnp.bfloat16)
            small = [(score_scale * a).astype(jnp.bfloat16) for a in onto(ds, q)]
            scatter(order, mid, prev, nxt, cols, *small)
            far = jnp.concatenate(
                [
                    contract(ds[near:, :rows], k_fp[:, cols], 0, 0),
                    contract(ds[near:, rows:], k_fn[:, cols], 0, 0),
                ],
                axis=0,
            )
            dq = contract(ds[:near], gather(ks, cols), 0, 0) + far
            dq = (dq * score_scale).astype(jnp.bfloat16)
            dq0[:, cols] = dq[:rows]
            dq1[:, cols] = dq[rows:]

    for order in range(2):
        pl.when(place[0] == order)(functools.partial(work, order))


def forward(place, lengths, versions, queries, grads, keys, ring, up, pair_q, pair, prev, prev2, nxt, nxt2):
    rows, width = queries.shape
    rank = up.shape[0]
    half = width // 2
    heads = half // HEAD_DIM
    block = HEADS_PER_STEP * HEAD_DIM
    steps = heads // HEADS_PER_STEP
    at = lambda first: pl.BlockSpec((rows, block), lambda h, *_: (0, first + h))
    mine = pl.BlockSpec((rows, block), lambda h, pc, *_: (0, pc[0] * steps + h))
    low_at = lambda b: pl.BlockSpec((rows, rank), lambda h, *_: (0, b))
    kind = jnp.bfloat16
    last = half // rank
    in_specs = [
        mine, at(0), mine, at(steps),
        mine, at(0), at(0), at(0), at(0), at(0),
        low_at(2 * last), low_at(last), low_at(2 * last), low_at(last), low_at(2 * last), low_at(last),
        pl.BlockSpec((rank, half), lambda h, pc, *_: (0, pc[0])),
    ]
    operands = (
        queries, pair_q, grads, pair_q,
        keys, pair, prev, prev2, nxt, nxt2,
        ring, pair, prev, prev2, nxt, nxt2,
        up,
    )
    double = jax.ShapeDtypeStruct((2 * rows, half), kind)
    back = jax.ShapeDtypeStruct((2 * rows, rank), jnp.float32)
    double_spec = pl.BlockSpec((2 * rows, block), lambda h, *_: (0, h))
    back_spec = pl.BlockSpec((2 * rows, rank), lambda h, *_: (0, 0))
    out_shape = [
        double, double, double,
        back, back, back,
        jax.ShapeDtypeStruct((heads, rank, 3 * HEAD_DIM), kind),
        jax.ShapeDtypeStruct((heads, 5 * rows, 2 * rows), kind),
        double,
    ]
    out_specs = [
        double_spec, double_spec, double_spec,
        back_spec, back_spec, back_spec,
        pl.BlockSpec((heads, rank, 3 * HEAD_DIM), lambda h, *_: (0, 0, 0)),
        pl.BlockSpec((HEADS_PER_STEP, 5 * rows, 2 * rows), lambda h, *_: (h, 0, 0)),
        double_spec,
    ]
    pairs = 10 * rows * rows * heads
    return pl.pallas_call(
        forward_kernel,
        grid_spec=pltpu.PrefetchScalarGridSpec(
            num_scalar_prefetch=3,
            grid=(steps,),
            in_specs=in_specs,
            out_specs=out_specs,
            scratch_shapes=[
                pltpu.VMEM((5 * rows, 2 * rows), jnp.float32),
                pltpu.VMEM((2 * rows, HEAD_DIM), jnp.float32),
                pltpu.VMEM((6 * rows, half), kind),
            ],
        ),
        out_shape=out_shape,
        compiler_params=pltpu.CompilerParams(
            vmem_limit_bytes=VMEM_LIMIT, dimension_semantics=("arbitrary",)
        ),
        cost_estimate=pl.CostEstimate(
            flops=10 * pairs * HEAD_DIM, bytes_accessed=12 << 20, transcendentals=pairs
        ),
    )(place, lengths, versions, *operands)


def backward(place, queries, keys, scaled, probs, pair_q, k_pair, k_prev2, k_next2, ring, v_pair, prev, v_prev2, nxt, v_next2):
    rows, width = queries.shape
    half = width // 2
    heads = half // HEAD_DIM
    block = HEADS_PER_STEP * HEAD_DIM
    steps = heads // HEADS_PER_STEP
    at = pl.BlockSpec((rows, block), lambda h, *_: (0, h))
    high = pl.BlockSpec((rows, block), lambda h, *_: (0, steps + h))
    mine = pl.BlockSpec((rows, block), lambda h, pc, *_: (0, pc[0] * steps + h))
    kind = jnp.bfloat16
    double = jax.ShapeDtypeStruct((2 * rows, half), kind)
    double_spec = pl.BlockSpec((2 * rows, block), lambda h, *_: (0, h))
    in_specs = [
        mine, at, double_spec,
        pl.BlockSpec((HEADS_PER_STEP, 5 * rows, 2 * rows), lambda h, *_: (h, 0, 0)),
        mine,
    ] + [at] * 5 + [high, at, high, at, high, at]
    single = jax.ShapeDtypeStruct((rows, half), kind)
    pairs = 10 * rows * rows * heads
    return pl.pallas_call(
        backward_kernel,
        grid_spec=pltpu.PrefetchScalarGridSpec(
            num_scalar_prefetch=1,
            grid=(steps,),
            in_specs=in_specs,
            out_specs=[at, at, double_spec, double_spec, double_spec],
        ),
        out_shape=[single, single, double, double, double],
        compiler_params=pltpu.CompilerParams(
            vmem_limit_bytes=VMEM_LIMIT, dimension_semantics=("arbitrary",)
        ),
        cost_estimate=pl.CostEstimate(
            flops=10 * pairs * HEAD_DIM, bytes_accessed=12 << 20, transcendentals=0
        ),
    )(
        place, queries, pair_q, scaled, probs,
        keys, k_pair, prev, k_prev2, nxt, k_next2, ring, v_pair, prev, v_prev2, nxt, v_next2,
    )


def finish_kernel(place, x_cols, both, own, to_low, to_high, to_both, *, norm):
    members, rows, width = x_cols.shape
    rank = both.shape[1]
    x = x_cols[...].reshape(members * rows, width)
    back_rows = both[:, :, :rank].reshape(members * rows, rank)
    down = contract(x, back_rows, 0, 0) * norm
    up = both[0, :, rank:].astype(jnp.float32)
    for i in range(1, members):
        up = up + both[i, :, rank:].astype(jnp.float32)
    up = up * norm
    cut, half = width // 4, rank // 2
    low, high = place[0], place[2]

    def write(a, b):
        refs = (own, to_low, to_high, to_both)
        for slot in range(2):
            for part in range(2):
                ref = refs[2 * (slot ^ b) + (part ^ a)]
                first = (2 * slot + part) * cut
                ref[:cut] = down[first : first + cut]
                ref[cut:] = up[part * half : (part + 1) * half, slot * HEAD_DIM : (slot + 1) * HEAD_DIM]

    for a in range(2):
        for b in range(2):
            pl.when((low == a) & (high == b))(functools.partial(write, a, b))


def simple(kernel, out_shape, place, *operands):
    smem, spec = pl.BlockSpec(memory_space=pltpu.SMEM), pl.BlockSpec(memory_space=pltpu.VMEM)
    return pl.pallas_call(
        kernel,
        out_shape=out_shape,
        in_specs=[smem] + [spec] * len(operands),
        out_specs=[spec] * len(out_shape),
        compiler_params=pltpu.CompilerParams(vmem_limit_bytes=VMEM_LIMIT),
    )(place, *operands)


def per_device(
    normed_input, queries, rotated_key_rows, frozen_value_rows, cotangent,
    adapter_down_weight, adapter_up_weight, document_lengths, versions,
):
    rows, width = queries.shape
    half = width // 2
    rank = adapter_down_weight.shape[1]
    sequence_count = lax.axis_size("seq")
    replicas = lax.axis_size("dp")
    shard = lax.axis_index("seq")
    y, z, high = shard % 2, shard // 2, (lax.axis_index("dp") // 2) % 2
    place = jnp.stack([y, z, high]).astype(jnp.int32)
    to_pair = lambda a: shifted(a, "seq", lambda i: i ^ 1)
    to_next = lambda a: shifted(a, "seq", lambda i: i + 2)
    to_prev = lambda a: shifted(a, "seq", lambda i: i - 2)
    to_high = lambda a: shifted(a, "dp", lambda i: i ^ 2)
    crossed = [
        (i * sequence_count + j, (i ^ 2) * sequence_count + (j ^ 1))
        for i in range(replicas) for j in range(sequence_count)
    ]
    to_both = lambda a: lax.ppermute(a, ("dp", "seq"), crossed)
    after = lambda *a: lax.optimization_barrier(a)
    shape = jax.ShapeDtypeStruct
    wide, narrow = jnp.float32, jnp.bfloat16
    members = replicas // 2
    flat = [[i for i in range(replicas) if (i // 2) % 2 == b] for b in range(2)]

    k_send, ring, q_send, v_send, x_send = prepare(
        place, normed_input, adapter_down_weight, adapter_up_weight, frozen_value_rows,
        rotated_key_rows, queries, cotangent, members,
    )
    k_pair, prev, nxt = to_pair(k_send), to_next(ring), to_prev(ring)
    k_pair, q_send, v_send = after(k_pair, q_send, v_send)
    k_prev2, k_next2 = to_next(k_pair), to_prev(k_pair)
    q_pair, v_pair = to_pair(q_send), to_pair(v_send)
    x_cols = lax.all_to_all(x_send, "dp", 0, 0, tiled=True, axis_index_groups=flat)
    q_pair, v_pair = after(q_pair, v_pair)

    dv_mid, dv_prev, dv_next, back, back_prev, back_next, up_send, probs, scaled = forward(
        place, document_lengths, versions, queries, cotangent, rotated_key_rows, ring,
        adapter_up_weight, q_pair, k_pair, prev, k_prev2, nxt, k_next2,
    )
    from_next, from_prev = to_prev(back_prev), to_next(back_next)
    v_prev2, v_next2 = to_next(v_pair), to_prev(v_pair)
    theirs = to_pair(back[rows:] + from_next[rows:] + from_prev[rows:])
    theirs, v_prev2, v_next2, x_cols = after(theirs, v_prev2, v_next2, x_cols)
    back_rows = (back[:rows] + from_next[:rows] + from_prev[:rows] + theirs).astype(narrow)
    payload = up_send.at[:, :, :rank].set(jnp.broadcast_to(back_rows[None], (members, rows, rank)))
    parts = lax.all_to_all(payload, "dp", 0, 0, tiled=True, axis_index_groups=flat)

    add = lambda a, b, c: (a.astype(wide) + b.astype(wide) + c.astype(wide)).astype(narrow)
    dv = add(dv_mid, to_prev(dv_prev), to_next(dv_next))
    scaled, dv = after(scaled, dv)
    dv_came = to_pair(dv[rows:])
    dq_own, dq_pair, dk_mid, dk_prev, dk_next = backward(
        place, queries, rotated_key_rows, scaled, probs, q_pair, k_pair, k_prev2, k_next2,
        ring, v_pair, prev, v_prev2, nxt, v_next2,
    )
    dk = add(dk_mid, to_prev(dk_prev), to_next(dk_next))

    norm = adapter_scale / math.sqrt(rows * sequence_count * replicas)
    down_rows = adapter_down_weight.shape[0] // replicas
    piece = shape(((down_rows + rank) // 2, rank), wide)
    parts, dk_prev, dk_next, dv_came = after(parts, dk_prev, dk_next, dv_came)
    keep, a, b, c = simple(functools.partial(finish_kernel, norm=norm), [piece] * 4, place, x_cols, parts)
    a, b, c = to_pair(a), to_high(b), to_both(c)
    dq_came, dk_came = to_pair(dq_pair), to_pair(dk[rows:])
    keep = (keep + a + b + c).astype(narrow)
    count = sequence_count // 2
    columns = [list(range(c, sequence_count, 2)) for c in range(2)]
    sums = lax.all_to_all(
        jnp.broadcast_to(keep[None], (count,) + keep.shape), "seq", 0, 0, tiled=True, axis_index_groups=columns
    )
    def joined(a, b):
        return jnp.concatenate([jnp.where(y == 0, a, b), jnp.where(y == 0, b, a)], axis=1)

    dk, dv, dq = joined(dk[:rows], dk_came), joined(dv[:rows], dv_came), joined(dq_own, dq_came)
    sums, dv, dq = after(sums, dv, dq)
    mine = jnp.sum(sums.astype(wide), axis=0)
    other = to_pair(mine)
    halves = [jnp.where(y == 0, mine, other), jnp.where(y == 0, other, mine)]
    cut = down_rows // 2
    down_gradient = jnp.concatenate([a[:cut] for a in halves], axis=0)
    up_gradient = jnp.concatenate([a[cut:] for a in halves], axis=0)
    return dq, dk, dv, down_gradient, up_gradient


def solution(mesh):
    tokens = P(("dp", "seq"), None)
    in_specs = (tokens,) * 5 + (P(), P(), P("dp", None), P("dp", None))
    out_specs = (tokens,) * 3 + (P("dp", None), P(None, "dp"))
    return jax.shard_map(
        per_device, mesh=mesh, in_specs=in_specs, out_specs=out_specs, check_vma=False
    )
```

time: 150 us -> 127 us (0.85)
  waiting for transfers between devices: 58.2 us -> 36.5 us
  starting transfers between devices: 53.6 us -> 47.7 us
  other arithmetic: 5.13 us -> 11 us
    all_to_all x2 -> x3, waiting for transfers between devices: 26.8 us -> 3.93 us  [the longest x1 3.92 us: per_device(): lax.all_to_all(jnp.broadcast_to(keep[None], (count,) + keep.shape), 'seq'...]
    all_to_all x2 -> x3, starting transfers between devices: 20.1 us -> 13.1 us  [the longest x1 4.83 us: per_device(): lax.all_to_all(x_send, 'dp', 0, 0, tiled=True, axis_index_groups=flat)]
    pallas_call x2 -> x1, Pallas kernels: 5.08 us -> 2.72 us  [simple(): pl.pallas_call(kernel, out_shape=out_shape, in_specs=[smem] + [spec] * le...]
    convert_element_type x2 -> x4, other arithmetic: 2.21 us -> 4.49 us  [the longest x2 2.62 us: per_device(): (a.astype(wide) + b.astype(wide) + c.astype(wide)).astype(narrow)]
    ppermute x0 -> x1, waiting for transfers between devices: none -> 2.19 us  [per_device(): to_both = lambda a: lax.ppermute(a, ('dp', 'seq'), crossed)]
    concatenate x0 -> x2, other arithmetic: none -> 1.88 us  [joined(): jnp.concatenate([jnp.where(y == 0, a, b), jnp.where(y == 0, b, a)], axis=1)]
    unnamed x32 -> x28, local copies, waits for them, and re-layouts: 4.48 us -> 2.96 us
    ppermute x15 -> x22, waiting for transfers between devices: 31.5 us -> 30.4 us  [shifted(): return lax.ppermute(block, axis, route)]
  transfers between devices with their start and end apart: 17 -> 26, of which waited for: 10 -> 13; matrix products, arithmetic and copies ran while one was open for 2% -> 8% of each run, Pallas kernels for 3% -> 17%
where the time goes in v3:
time: 127 us; the launch traced here: 126 us
  starting transfers between devices  47.7 us (38%)
  waiting for transfers between devices  36.5 us (29%)
  Pallas kernels  25.1 us (20%)
  other arithmetic  11 us (9%)
  local copies, waits for them, and re-layouts  4.61 us (4%)
    ppermute x22, starting transfers between devices, shifted(): return lax.ppermute(block, axis, route)  34.4 us
    ppermute x22, waiting for transfers between devices, shifted(): return lax.ppermute(block, axis, route)  30.4 us
    pallas_call x1, Pallas kernels, forward(): pl.pallas_call(forward_kernel, grid_spec=pltpu.PrefetchScalarGridSpec(num...  9.78 us
    pallas_call x1, Pallas kernels, backward(): pl.pallas_call(backward_kernel, grid_spec=pltpu.PrefetchScalarGridSpec(nu...  8.41 us
    all_to_all x1, starting transfers between devices, per_device(): lax.all_to_all(x_send, 'dp', 0, 0, tiled=True, axis_index_groups=flat)  4.83 us
    all_to_all x1, starting transfers between devices, per_device(): lax.all_to_all(payload, 'dp', 0, 0, tiled=True, axis_index_groups=flat)  4.82 us
    pallas_call x1, Pallas kernels, prepare(): pl.pallas_call(prepare_kernel, out_shape=[jax.ShapeDtypeStruct(s, kind) f...  4.19 us
    all_to_all x1, waiting for transfers between devices, per_device(): lax.all_to_all(jnp.broadcast_to(keep[None], (count,) + keep.shape), 'seq'...  3.92 us
  transfers between devices with their start and end apart: 26, of which 13 were waited for; matrix products, arithmetic and copies ran while one was open for 8% of the time, Pallas kernels for 17%

profile of v3, /device:TPU:2, one launch (start us, length us, event | category | flops | bytes accessed | tf_op | source)
XLA Modules:
  0.0 125.9 jit_solution(8016153294151281306)
XLA Ops:
  0.7 0.7 pad_add_fusion.place
  1.3 4.2 %shard_map.128 = (bf16[128,1152]{1,0:T(8,128)(2,1)}, bf16[128,2176]{1,0:T(8,128)(2,1)}, bf16[128,2048]{1,0:T(8,128)(2,1)}, bf16[128,1024]{1,0:T(8,128)(2,1)}, bf16[8,128,512]{2,1,0:T(8,128)(2,1)}) custom-call(s32[3]{0:T(128)} %pad_add_fusion.place, bf16[128,4096]{1,0:T(8,128)(2,1)} %x.1, bf16[4096,128]{1,0:T(8,128)(2,1)} %down.1, bf16[128,2048]{1,0:T(8,128)(2,1)} %up.3, ...), custom_call_target="tpu_custom_call" | custom-call | tf_op jit(solution)/shard_map/pallas_call | solution.py:106
  5.5 1.7 %collective-permute-start = (bf16[128,1152]{1,0:T(8,128)(2,1)}, bf16[128,1152]{1,0:T(8,128)(2,1)S(1)}, u32[]{:S(2)}, u32[]{:S(2)}) collective-permute-start(bf16[128,1152]{1,0:T(8,128)(2,1)} %get-tuple-element.56), channel_id=1, source_target_pairs={{0,1},{1,0},{2,3},{3,2},{4,5},{5,4},{6,7},{7,6},{8,9},{9,8},{10,11... | collective-permute-start | bytes 884744 | tf_op jit(solution)/shard_map/ppermute | solution.py:29
  7.2 5.9 %collective-permute-start.5 = (bf16[128,2176]{1,0:T(8,128)(2,1)}, bf16[128,2176]{1,0:T(8,128)(2,1)S(1)}, u32[]{:S(2)}, u32[]{:S(2)}) collective-permute-start(bf16[128,2176]{1,0:T(8,128)(2,1)} %get-tuple-element.63.l_own.v_own), channel_id=1, source_target_pairs={{0,14},{1,15},{2,0},{3,1},{4,2},{5,3},{6,4},{7,5},{8,6},{9,7},{10,... | collective-permute-start | bytes 1671176 | tf_op jit(solution)/shard_map/ppermute | solution.py:29
  13.0 1.5 %collective-permute-done.k_pair.l_pair = bf16[128,1152]{1,0:T(8,128)(2,1)S(1)} collective-permute-done((bf16[128,1152]{1,0:T(8,128)(2,1)}, bf16[128,1152]{1,0:T(8,128)(2,1)S(1)}, u32[]{:S(2)}, u32[]{:S(2)}) %collective-permute-start) | collective-permute-done | bytes 294944 | tf_op jit(solution)/shard_map/ppermute | solution.py:29
  14.6 1.6 %collective-permute-start.2 = (bf16[128,1024]{1,0:T(8,128)(2,1)}, bf16[128,1024]{1,0:T(8,128)(2,1)}, u32[]{:S(2)}, u32[]{:S(2)}) collective-permute-start(bf16[128,1024]{1,0:T(8,128)(2,1)} %get-tuple-element.60), channel_id=1, source_target_pairs={{0,1},{1,0},{2,3},{3,2},{4,5},{5,4},{6,7},{7,6},{8,9},{9,8},{10,11... | collective-permute-start | bytes 786440 | tf_op jit(solution)/shard_map/ppermute | solution.py:29
  16.6 4.8 %all-to-all-start = ((bf16[8,128,512]{2,1,0:T(8,128)(2,1)}), bf16[8,128,512]{2,1,0:T(8,128)(2,1)S(1)}, u32[]{:S(2)}, u32[]{:S(2)}) async-start(bf16[8,128,512]{2,1,0:T(8,128)(2,1)} %get-tuple-element.68), calls=%async_computation | async-start | bytes 2097152 | tf_op jit(solution)/shard_map/all_to_all | solution.py:486
  21.4 5.9 %collective-permute-start.6 = (bf16[128,1152]{1,0:T(8,128)(2,1)S(1)}, bf16[128,1152]{1,0:T(8,128)(2,1)S(1)}, u32[]{:S(2)}, u32[]{:S(2)}) collective-permute-start(bf16[128,1152]{1,0:T(8,128)(2,1)S(1)} %collective-permute-done.k_pair.l_pair), channel_id=1, source_target_pairs={{0,14},{1,15},{2,0},{3,1},{4,2},{5,3},{6,4},{7,5},{8,6},{9,7},{10,... | collective-permute-start | bytes 884744 | tf_op jit(solution)/shard_map/ppermute | solution.py:29
  27.3 5.9 %collective-permute-done.1.q_pair.g_pair = bf16[128,2048]{1,0:T(8,128)(2,1)S(1)} collective-permute-done((bf16[128,2048]{1,0:T(8,128)(2,1)}, bf16[128,2048]{1,0:T(8,128)(2,1)S(1)}, u32[]{:S(2)}, u32[]{:S(2)}) %collective-permute-start.1) | collective-permute-done | bytes 524320 | tf_op jit(solution)/shard_map/ppermute | solution.py:29
  33.2 0.6 collective-permute-done.6.k_next2.l_next2
  33.9 3.4 %collective-permute-done.4.k_prev2.l_prev2 = bf16[128,1152]{1,0:T(8,128)(2,1)S(1)} collective-permute-done((bf16[128,1152]{1,0:T(8,128)(2,1)S(1)}, bf16[128,1152]{1,0:T(8,128)(2,1)S(1)}, u32[]{:S(2)}, u32[]{:S(2)}) %collective-permute-start.4) | collective-permute-done | bytes 294944 | tf_op jit(solution)/shard_map/ppermute | solution.py:29
  37.3 0.8 copy-done.7
  38.1 9.8 %shard_map.129 = (bf16[256,1024]{1,0:T(8,128)(2,1)}, bf16[256,1024]{1,0:T(8,128)(2,1)}, bf16[256,1024]{1,0:T(8,128)(2,1)}, f32[256,128]{1,0:T(8,128)}, f32[256,1...) custom-call(s32[3]{0:T(128)} %pad_add_fusion.place, ...), custom_call_target="tpu_custom_call" | custom-call | flops 1677721600 | bytes 12582912 | tf_op jit(solution)/shard_map/pallas_call | solution.py:350
  47.9 3.3 %collective-permute-start.7 = (f32[256,128]{1,0:T(8,128)}, f32[256,128]{1,0:T(8,128)S(1)}, u32[]{:S(2)}, u32[]{:S(2)}) collective-permute-start(f32[256,128]{1,0:T(8,128)} %get-tuple-element.65), channel_id=1, source_target_pairs={{0,14},{1,15},{2,0},{3,1},{4,2},{5,3},{6,4},{7,5},{8,6},{9,7},{10,... | collective-permute-start | bytes 393224 | tf_op jit(solution)/shard_map/ppermute | solution.py:29
  51.2 3.2 %collective-permute-start.11 = (bf16[128,1024]{1,0:T(8,128)(2,1)}, bf16[128,1024]{1,0:T(8,128)(2,1)S(1)}, u32[]{:S(2)}, u32[]{:S(2)}) collective-permute-start(bf16[128,1024]{1,0:T(8,128)(2,1)} %collective-permute-done.2.v_pair), channel_id=1, source_target_pairs={{0,14},{1,15},{2,0},{3,1},{4,2},{5,3},{6,4},{7,5},{8,6},{9,7},{10,... | collective-permute-start | bytes 786440 | tf_op jit(solution)/shard_map/ppermute | solution.py:29
  54.4 1.0 collective-permute-done.7
  55.4 3.5 %collective-permute-done.8 = f32[256,128]{1,0:T(8,128)S(1)} collective-permute-done((f32[256,128]{1,0:T(8,128)}, f32[256,128]{1,0:T(8,128)S(1)}, u32[]{:S(2)}, u32[]{:S(2)}) %collective-permute-start.8) | collective-permute-done | bytes 131104 | tf_op jit(solution)/shard_map/ppermute | solution.py:29
  58.9 1.5 %slice_add_fusion.2 = f32[128,128]{1,0:T(8,128)} fusion(f32[256,128]{1,0:T(8,128)S(1)} %collective-permute-done.8, f32[256,128]{1,0:T(8,128)S(1)} %collective-permute-done.7, f32[256,128]{1,0:T(8,128)} %get-tuple-element.64), kind=kLoop, calls=%fused_computation.19 | loop fusion | flops 32768 | bytes 262144 | tf_op jit(solution)/shard_map/add | solution.py:495
  60.4 1.6 %collective-permute-start.9 = (f32[128,128]{1,0:T(8,128)}, f32[128,128]{1,0:T(8,128)S(1)}, u32[]{:S(2)}, u32[]{:S(2)}) collective-permute-start(f32[128,128]{1,0:T(8,128)} %slice_add_fusion.2), channel_id=1, source_target_pairs={{0,1},{1,0},{2,3},{3,2},{4,5},{5,4},{6,7},{7,6},{8,9},{9,8},{10,11... | collective-permute-start | bytes 196616 | tf_op jit(solution)/shard_map/ppermute | solution.py:29
  62.0 2.0 %collective-permute-start.13 = (bf16[256,1024]{1,0:T(8,128)(2,1)}, bf16[256,1024]{1,0:T(8,128)(2,1)S(1)}, u32[]{:S(2)}, u32[]{:S(2)}) collective-permute-start(bf16[256,1024]{1,0:T(8,128)(2,1)} %get-tuple-element.75), channel_id=1, source_target_pairs={{0,2},{1,3},{2,4},{3,5},{4,6},{5,7},{6,8},{7,9},{8,10},{9,11},{10,... | collective-permute-start | bytes 1572872 | tf_op jit(solution)/shard_map/ppermute | solution.py:29
  64.0 0.9 collective-permute-done.9
  64.9 1.0 fusion.1
  65.8 0.8 broadcast_dynamic-update-slice_fusion
  66.6 4.8 %all-to-all-start.1 = ((bf16[8,128,384]{2,1,0:T(8,128)(2,1)}), bf16[8,128,384]{2,1,0:T(8,128)(2,1)S(1)}, u32[]{:S(2)}, u32[]{:S(2)}) async-start(bf16[8,128,384]{2,1,0:T(8,128)(2,1)} %broadcast_dynamic-update-slice_fusion), calls=%async_computation.1 | async-start | bytes 1572864 | tf_op jit(solution)/shard_map/all_to_all | solution.py:499
  71.4 2.4 %collective-permute-done.13 = bf16[256,1024]{1,0:T(8,128)(2,1)S(1)} collective-permute-done((bf16[256,1024]{1,0:T(8,128)(2,1)}, bf16[256,1024]{1,0:T(8,128)(2,1)S(1)}, u32[]{:S(2)}, u32[]{:S(2)}) %collective-permute-start.13) | collective-permute-done | bytes 524320 | tf_op jit(solution)/shard_map/ppermute | solution.py:29
  73.9 0.8 copy-done.10
  74.7 1.3 %add_convert_fusion.1 = bf16[256,1024]{1,0:T(8,128)(2,1)S(1)} fusion(bf16[256,1024]{1,0:T(8,128)(2,1)} %copy-done.10, bf16[256,1024]{1,0:T(8,128)(2,1)S(1)} %collective-permute-done.12, bf16[256,1024]{1,0:T(8,128)(2,1)S(1)} %copy-done.9), kind=kLoop, calls=%fused_computation.1 | loop fusion | flops 1572864 | bytes 2097152 | tf_op jit(solution)/shard_map/convert_element_type | solution.py:501
  76.0 1.7 %collective-permute-start.14 = (bf16[128,1024]{1,0:T(8,128)(2,1)S(1)}, bf16[128,1024]{1,0:T(8,128)(2,1)S(1)}, u32[]{:S(2)}, u32[]{:S(2)}) collective-permute-start(bf16[128,1024]{1,0:T(8,128)(2,1)S(1)} %slice.70), channel_id=1, source_target_pairs={{0,1},{1,0},{2,3},{3,2},{4,5},{5,4},{6,7},{7,6},{8,9},{9,8},{10,11... | collective-permute-start | bytes 786440 | tf_op jit(solution)/shard_map/ppermute | solution.py:29
  77.7 8.4 %shard_map.130 = (bf16[128,1024]{1,0:T(8,128)(2,1)}, bf16[128,1024]{1,0:T(8,128)(2,1)}, bf16[256,1024]{1,0:T(8,128)(2,1)}, bf16[256,1024]{1,0:T(8,128)(2,1)}, bf16[256,1024]{1,0:T(8,128)(2,1)}) custom-call(s32[3]{0:T(128)} %pad_add_fusion.place, bf16[128,2048]{1,0:T(8,128)(2,1)} %q_own.3, bf16[128,2048]{1,0:T(8,128)(2,1)} %copy-done.2, ...), custom_call_target="tpu_custom_call" | custom-call | flops 1677721600 | bytes 12582912 | tf_op jit(solution)/shard_map/pallas_call | solution.py:392
  86.9 1.7 %collective-permute-start.20 = (bf16[256,1024]{1,0:T(8,128)(2,1)}, bf16[256,1024]{1,0:T(8,128)(2,1)}, u32[]{:S(2)}, u32[]{:S(2)}) collective-permute-start(bf16[256,1024]{1,0:T(8,128)(2,1)} %get-tuple-element.81), channel_id=1, source_target_pairs={{0,2},{1,3},{2,4},{3,5},{4,6},{5,7},{6,8},{7,9},{8,10},{9,11},{10,... | collective-permute-start | bytes 1572872 | tf_op jit(solution)/shard_map/ppermute | solution.py:29
  88.7 0.9 copy-done.4
  89.6 2.7 %shard_map.131 = (f32[192,128]{1,0:T(8,128)}, f32[192,128]{1,0:T(8,128)}, f32[192,128]{1,0:T(8,128)}, f32[192,128]{1,0:T(8,128)}) custom-call(s32[3]{0:T(128)} %pad_add_fusion.place, bf16[8,128,512]{2,1,0:T(8,128)(2,1)} %copy-done.3, bf16[8,128,384]{2,1,0:T(8,128)(2,1)} %copy-done.4), custom_call_target="tpu_custom_call" | custom-call | tf_op jit(solution)/shard_map/pallas_call | solution.py:442
  92.3 1.6 %collective-permute-start.15 = (f32[192,128]{1,0:T(8,128)}, f32[192,128]{1,0:T(8,128)S(1)}, u32[]{:S(2)}, u32[]{:S(2)}) collective-permute-start(f32[192,128]{1,0:T(8,128)} %get-tuple-element.85), channel_id=1, source_target_pairs={{0,1},{1,0},{2,3},{3,2},{4,5},{5,4},{6,7},{7,6},{8,9},{9,8},{10,11... | collective-permute-start | bytes 294920 | tf_op jit(solution)/shard_map/ppermute | solution.py:29
  93.9 2.9 %collective-permute-start.16 = (f32[192,128]{1,0:T(8,128)}, f32[192,128]{1,0:T(8,128)S(1)}, u32[]{:S(2)}, u32[]{:S(2)}) collective-permute-start(f32[192,128]{1,0:T(8,128)} %get-tuple-element.86), channel_id=1, source_target_pairs={{0,32},{16,48},{32,0},{48,16},{64,96},{80,112},{96,64},{112,80},{1... | collective-permute-start | bytes 294920 | tf_op jit(solution)/shard_map/ppermute | solution.py:29
  97.5 1.1 broadcast_select_fusion.3
  98.6 2.1 %collective-permute-done.16 = f32[192,128]{1,0:T(8,128)S(1)} collective-permute-done((f32[192,128]{1,0:T(8,128)}, f32[192,128]{1,0:T(8,128)S(1)}, u32[]{:S(2)}, u32[]{:S(2)}) %collective-permute-start.16) | collective-permute-done | bytes 98336 | tf_op jit(solution)/shard_map/ppermute | solution.py:29
  100.6 2.2 %collective-permute-done.17 = f32[192,128]{1,0:T(8,128)S(1)} collective-permute-done((f32[192,128]{1,0:T(8,128)}, f32[192,128]{1,0:T(8,128)S(1)}, u32[]{:S(2)}, u32[]{:S(2)}) %collective-permute-start.17) | collective-permute-done | bytes 98336 | tf_op jit(solution)/shard_map/ppermute | solution.py:471
  102.8 0.9 add_convert_fusion.2
  103.7 0.8 broadcast_in_dim.2
  104.5 3.5 %all-to-all-start.2 = ((bf16[8,192,128]{2,1,0:T(8,128)(2,1)}), bf16[8,192,128]{2,1,0:T(8,128)(2,1)S(1)}, u32[]{:S(2)}, u32[]{:S(2)}) async-start(bf16[8,192,128]{2,1,0:T(8,128)(2,1)} %broadcast_in_dim.2), calls=%async_computation.2 | async-start | bytes 786432 | tf_op jit(solution)/shard_map/all_to_all | solution.py:521
  108.0 1.3 %add_convert_fusion = bf16[256,1024]{1,0:T(8,128)(2,1)S(1)} fusion(bf16[256,1024]{1,0:T(8,128)(2,1)} %collective-permute-done.20, bf16[256,1024]{1,0:T(8,128)(2,1)S(1)} %collective-permute-done.19, bf16[256,1024]{1,0:T(8,128)(2,1)S(1)} %copy-done.8), kind=kLoop, calls=%fused_computation | loop fusion | flops 1572864 | bytes 2097152 | tf_op jit(solution)/shard_map/convert_element_type | solution.py:501
  109.5 1.1 pad_maximum_fusion
  110.6 5.3 %collective-permute-done.21 = bf16[128,1024]{1,0:T(8,128)(2,1)S(1)} collective-permute-done((bf16[128,1024]{1,0:T(8,128)(2,1)S(1)}, bf16[128,1024]{1,0:T(8,128)(2,1)S(1)}, u32[]{:S(2)}, u32[]{:S(2)}) %collective-permute-start.21) | collective-permute-done | bytes 262176 | tf_op jit(solution)/shard_map/ppermute | solution.py:29
  115.9 3.9 %all-to-all-done.2 = bf16[8,192,128]{2,1,0:T(8,128)(2,1)S(1)} async-done(((bf16[8,192,128]{2,1,0:T(8,128)(2,1)}), bf16[8,192,128]{2,1,0:T(8,128)(2,1)S(1)}, u32[]{:S(2)}, u32[]{:S(2)}) %all-to-all-start.2) | async-done | bytes 393248 | tf_op jit(solution)/shard_map/all_to_all | solution.py:521
  119.9 0.8 pad_maximum_fusion.2
  120.8 3.8 %collective-permute-done.22 = f32[192,128]{1,0:T(8,128)S(1)} collective-permute-done((f32[192,128]{1,0:T(8,128)S(1)}, f32[192,128]{1,0:T(8,128)S(1)}, u32[]{:S(2)}, u32[]{:S(2)}) %collective-permute-start.22) | collective-permute-done | bytes 98336 | tf_op jit(solution)/shard_map/ppermute | solution.py:29
  124.6 0.7 pad_maximum_fusion.3
  125.3 0.6 pad_maximum_fusion.4
  (59 shorter events, 2.5 us)
Async XLA Ops:
  5.5 9.0 %collective-permute-start = (bf16[128,1152]{1,0:T(8,128)(2,1)}, bf16[128,1152]{1,0:T(8,128)(2,1)S(1)}, u32[]{:S(2)}, u32[]{:S(2)}) collective-permute-start(bf16[128,1152]{1,0:T(8,128)(2,1)} %get-tuple-element.56), channel_id=1, source_target_pairs={{0,1},{1,0},{2,3},{3,2},{4,5},{5,4},{6,7},{7,6},{8,9},{9,8},{10,11... | collective-permute-start | bytes 884744 | tf_op jit(solution)/shard_map/ppermute | solution.py:29
  7.2 26.0 %collective-permute-start.5 = (bf16[128,2176]{1,0:T(8,128)(2,1)}, bf16[128,2176]{1,0:T(8,128)(2,1)S(1)}, u32[]{:S(2)}, u32[]{:S(2)}) collective-permute-start(bf16[128,2176]{1,0:T(8,128)(2,1)} %get-tuple-element.63.l_own.v_own), channel_id=1, source_target_pairs={{0,14},{1,15},{2,0},{3,1},{4,2},{5,3},{6,4},{7,5},{8,6},{9,7},{10,... | collective-permute-start | bytes 1671176 | tf_op jit(solution)/shard_map/ppermute | solution.py:29
  13.0 20.2 %collective-permute-start.3 = (bf16[128,2176]{1,0:T(8,128)(2,1)}, bf16[128,2176]{1,0:T(8,128)(2,1)S(1)}, u32[]{:S(2)}, u32[]{:S(2)}) collective-permute-start(bf16[128,2176]{1,0:T(8,128)(2,1)} %get-tuple-element.63.l_own.v_own), channel_id=1, source_target_pairs={{0,2},{1,3},{2,4},{3,5},{4,6},{5,7},{6,8},{7,9},{8,10},{9,11},{10,... | collective-permute-start | bytes 1671176 | tf_op jit(solution)/shard_map/ppermute | solution.py:29
  14.6 22.7 %copy-start.5 = (bf16[128,1152]{1,0:T(8,128)(2,1)}, bf16[128,1152]{1,0:T(8,128)(2,1)S(1)}, u32[]{:S(2)}) copy-start(bf16[128,1152]{1,0:T(8,128)(2,1)S(1)} %collective-permute-done.k_pair.l_pair) | copy-start | bytes 884740
  14.6 12.7 %collective-permute-start.2 = (bf16[128,1024]{1,0:T(8,128)(2,1)}, bf16[128,1024]{1,0:T(8,128)(2,1)}, u32[]{:S(2)}, u32[]{:S(2)}) collective-permute-start(bf16[128,1024]{1,0:T(8,128)(2,1)} %get-tuple-element.60), channel_id=1, source_target_pairs={{0,1},{1,0},{2,3},{3,2},{4,5},{5,4},{6,7},{7,6},{8,9},{9,8},{10,11... | collective-permute-start | bytes 786440 | tf_op jit(solution)/shard_map/ppermute | solution.py:29
  16.1 17.0 %collective-permute-start.1 = (bf16[128,2048]{1,0:T(8,128)(2,1)}, bf16[128,2048]{1,0:T(8,128)(2,1)S(1)}, u32[]{:S(2)}, u32[]{:S(2)}) collective-permute-start(bf16[128,2048]{1,0:T(8,128)(2,1)} %get-tuple-element.59), channel_id=1, source_target_pairs={{0,1},{1,0},{2,3},{3,2},{4,5},{5,4},{6,7},{7,6},{8,9},{9,8},{10,11... | collective-permute-start | bytes 1572872 | tf_op jit(solution)/shard_map/ppermute | solution.py:29
  16.6 47.4 %all-to-all-start = ((bf16[8,128,512]{2,1,0:T(8,128)(2,1)}), bf16[8,128,512]{2,1,0:T(8,128)(2,1)S(1)}, u32[]{:S(2)}, u32[]{:S(2)}) async-start(bf16[8,128,512]{2,1,0:T(8,128)(2,1)} %get-tuple-element.68), calls=%async_computation | async-start | bytes 2097152 | tf_op jit(solution)/shard_map/all_to_all | solution.py:486
  21.4 12.4 %collective-permute-start.6 = (bf16[128,1152]{1,0:T(8,128)(2,1)S(1)}, bf16[128,1152]{1,0:T(8,128)(2,1)S(1)}, u32[]{:S(2)}, u32[]{:S(2)}) collective-permute-start(bf16[128,1152]{1,0:T(8,128)(2,1)S(1)} %collective-permute-done.k_pair.l_pair), channel_id=1, source_target_pairs={{0,14},{1,15},{2,0},{3,1},{4,2},{5,3},{6,4},{7,5},{8,6},{9,7},{10,... | collective-permute-start | bytes 884744 | tf_op jit(solution)/shard_map/ppermute | solution.py:29
  27.3 10.0 %collective-permute-start.4 = (bf16[128,1152]{1,0:T(8,128)(2,1)S(1)}, bf16[128,1152]{1,0:T(8,128)(2,1)S(1)}, u32[]{:S(2)}, u32[]{:S(2)}) collective-permute-start(bf16[128,1152]{1,0:T(8,128)(2,1)S(1)} %collective-permute-done.k_pair.l_pair), channel_id=1, source_target_pairs={{0,2},{1,3},{2,4},{3,5},{4,6},{5,7},{6,8},{7,9},{8,10},{9,11},{10,... | collective-permute-start | bytes 884744 | tf_op jit(solution)/shard_map/ppermute | solution.py:29
  33.2 4.1 %copy-start.2 = (bf16[128,2048]{1,0:T(8,128)(2,1)}, bf16[128,2048]{1,0:T(8,128)(2,1)S(1)}, u32[]{:S(2)}) copy-start(bf16[128,2048]{1,0:T(8,128)(2,1)S(1)} %collective-permute-done.1.q_pair.g_pair) | copy-start | bytes 1572868
  33.2 4.1 %copy-start = (bf16[128,2176]{1,0:T(8,128)(2,1)}, bf16[128,2176]{1,0:T(8,128)(2,1)S(1)}, u32[]{:S(2)}) copy-start(bf16[128,2176]{1,0:T(8,128)(2,1)S(1)} %collective-permute-done.5.k_next.l_next.v_next) | copy-start | bytes 1671172
  33.2 4.1 %copy-start.1 = (bf16[128,2176]{1,0:T(8,128)(2,1)}, bf16[128,2176]{1,0:T(8,128)(2,1)S(1)}, u32[]{:S(2)}) copy-start(bf16[128,2176]{1,0:T(8,128)(2,1)S(1)} %collective-permute-done.3.k_prev.l_prev.v_prev) | copy-start | bytes 1671172
  33.9 3.4 %copy-start.6 = (bf16[128,1152]{1,0:T(8,128)(2,1)}, bf16[128,1152]{1,0:T(8,128)(2,1)S(1)}, u32[]{:S(2)}) copy-start(bf16[128,1152]{1,0:T(8,128)(2,1)S(1)} %collective-permute-done.6.k_next2.l_next2) | copy-start | bytes 884740
  37.3 0.8 copy-start.7
  47.9 26.8 %copy-start.9 = (bf16[256,1024]{1,0:T(8,128)(2,1)S(1)}, bf16[256,1024]{1,0:T(8,128)(2,1)}, u32[]{:S(2)}) copy-start(bf16[256,1024]{1,0:T(8,128)(2,1)} %get-tuple-element.73) | copy-start | bytes 1572868
  47.9 7.5 %collective-permute-start.7 = (f32[256,128]{1,0:T(8,128)}, f32[256,128]{1,0:T(8,128)S(1)}, u32[]{:S(2)}, u32[]{:S(2)}) collective-permute-start(f32[256,128]{1,0:T(8,128)} %get-tuple-element.65), channel_id=1, source_target_pairs={{0,14},{1,15},{2,0},{3,1},{4,2},{5,3},{6,4},{7,5},{8,6},{9,7},{10,... | collective-permute-start | bytes 393224 | tf_op jit(solution)/shard_map/ppermute | solution.py:29
  51.1 7.7 %collective-permute-start.8 = (f32[256,128]{1,0:T(8,128)}, f32[256,128]{1,0:T(8,128)S(1)}, u32[]{:S(2)}, u32[]{:S(2)}) collective-permute-start(f32[256,128]{1,0:T(8,128)} %get-tuple-element.66), channel_id=1, source_target_pairs={{0,2},{1,3},{2,4},{3,5},{4,6},{5,7},{6,8},{7,9},{8,10},{9,11},{10,... | collective-permute-start | bytes 393224 | tf_op jit(solution)/shard_map/ppermute | solution.py:29
  51.2 13.7 %collective-permute-start.11 = (bf16[128,1024]{1,0:T(8,128)(2,1)}, bf16[128,1024]{1,0:T(8,128)(2,1)S(1)}, u32[]{:S(2)}, u32[]{:S(2)}) collective-permute-start(bf16[128,1024]{1,0:T(8,128)(2,1)} %collective-permute-done.2.v_pair), channel_id=1, source_target_pairs={{0,14},{1,15},{2,0},{3,1},{4,2},{5,3},{6,4},{7,5},{8,6},{9,7},{10,... | collective-permute-start | bytes 786440 | tf_op jit(solution)/shard_map/ppermute | solution.py:29
  54.4 10.5 %collective-permute-start.10 = (bf16[128,1024]{1,0:T(8,128)(2,1)}, bf16[128,1024]{1,0:T(8,128)(2,1)S(1)}, u32[]{:S(2)}, u32[]{:S(2)}) collective-permute-start(bf16[128,1024]{1,0:T(8,128)(2,1)} %collective-permute-done.2.v_pair), channel_id=1, source_target_pairs={{0,2},{1,3},{2,4},{3,5},{4,6},{5,7},{6,8},{7,9},{8,10},{9,11},{10,... | collective-permute-start | bytes 786440 | tf_op jit(solution)/shard_map/ppermute | solution.py:29
  60.4 4.5 %collective-permute-start.9 = (f32[128,128]{1,0:T(8,128)}, f32[128,128]{1,0:T(8,128)S(1)}, u32[]{:S(2)}, u32[]{:S(2)}) collective-permute-start(f32[128,128]{1,0:T(8,128)} %slice_add_fusion.2), channel_id=1, source_target_pairs={{0,1},{1,0},{2,3},{3,2},{4,5},{5,4},{6,7},{7,6},{8,9},{9,8},{10,11... | collective-permute-start | bytes 196616 | tf_op jit(solution)/shard_map/ppermute | solution.py:29
  61.9 9.5 %collective-permute-start.12 = (bf16[256,1024]{1,0:T(8,128)(2,1)}, bf16[256,1024]{1,0:T(8,128)(2,1)S(1)}, u32[]{:S(2)}, u32[]{:S(2)}) collective-permute-start(bf16[256,1024]{1,0:T(8,128)(2,1)} %get-tuple-element.74), channel_id=1, source_target_pairs={{0,14},{1,15},{2,0},{3,1},{4,2},{5,3},{6,4},{7,5},{8,6},{9,7},{10,... | collective-permute-start | bytes 1572872 | tf_op jit(solution)/shard_map/ppermute | solution.py:29
  62.0 11.9 %collective-permute-start.13 = (bf16[256,1024]{1,0:T(8,128)(2,1)}, bf16[256,1024]{1,0:T(8,128)(2,1)S(1)}, u32[]{:S(2)}, u32[]{:S(2)}) collective-permute-start(bf16[256,1024]{1,0:T(8,128)(2,1)} %get-tuple-element.75), channel_id=1, source_target_pairs={{0,2},{1,3},{2,4},{3,5},{4,6},{5,7},{6,8},{7,9},{8,10},{9,11},{10,... | collective-permute-start | bytes 1572872 | tf_op jit(solution)/shard_map/ppermute | solution.py:29
  64.0 22.1 %copy-start.3 = (bf16[8,128,512]{2,1,0:T(8,128)(2,1)}, bf16[8,128,512]{2,1,0:T(8,128)(2,1)S(1)}, u32[]{:S(2)}) copy-start(bf16[8,128,512]{2,1,0:T(8,128)(2,1)S(1)} %all-to-all-done.x_cols) | copy-start | bytes 3145732
  64.8 1.8 %copy-start.11 = (bf16[128,1024]{1,0:T(8,128)(2,1)}, bf16[128,1024]{1,0:T(8,128)(2,1)S(1)}, u32[]{:S(2)}) copy-start(bf16[128,1024]{1,0:T(8,128)(2,1)S(1)} %collective-permute-done.11.v_next2) | copy-start | bytes 786436
  64.8 1.8 %copy-start.12 = (bf16[128,1024]{1,0:T(8,128)(2,1)}, bf16[128,1024]{1,0:T(8,128)(2,1)S(1)}, u32[]{:S(2)}) copy-start(bf16[128,1024]{1,0:T(8,128)(2,1)S(1)} %collective-permute-done.10.v_prev2) | copy-start | bytes 786436
  66.6 22.1 %all-to-all-start.1 = ((bf16[8,128,384]{2,1,0:T(8,128)(2,1)}), bf16[8,128,384]{2,1,0:T(8,128)(2,1)S(1)}, u32[]{:S(2)}, u32[]{:S(2)}) async-start(bf16[8,128,384]{2,1,0:T(8,128)(2,1)} %broadcast_dynamic-update-slice_fusion), calls=%async_computation.1 | async-start | bytes 1572864 | tf_op jit(solution)/shard_map/all_to_all | solution.py:499
  73.9 0.8 copy-start.10
  76.0 12.7 %collective-permute-start.14 = (bf16[128,1024]{1,0:T(8,128)(2,1)S(1)}, bf16[128,1024]{1,0:T(8,128)(2,1)S(1)}, u32[]{:S(2)}, u32[]{:S(2)}) collective-permute-start(bf16[128,1024]{1,0:T(8,128)(2,1)S(1)} %slice.70), channel_id=1, source_target_pairs={{0,1},{1,0},{2,3},{3,2},{4,5},{5,4},{6,7},{7,6},{8,9},{9,8},{10,11... | collective-permute-start | bytes 786440 | tf_op jit(solution)/shard_map/ppermute | solution.py:29
  86.1 21.9 %copy-start.8 = (bf16[256,1024]{1,0:T(8,128)(2,1)S(1)}, bf16[256,1024]{1,0:T(8,128)(2,1)}, u32[]{:S(2)}) copy-start(bf16[256,1024]{1,0:T(8,128)(2,1)} %get-tuple-element.92) | copy-start | bytes 1572868
  86.1 10.7 %collective-permute-start.18 = (bf16[128,1024]{1,0:T(8,128)(2,1)}, bf16[128,1024]{1,0:T(8,128)(2,1)S(1)}, u32[]{:S(2)}, u32[]{:S(2)}) collective-permute-start(bf16[128,1024]{1,0:T(8,128)(2,1)} %get-tuple-element.90), channel_id=1, source_target_pairs={{0,1},{1,0},{2,3},{3,2},{4,5},{5,4},{6,7},{7,6},{8,9},{9,8},{10,11... | collective-permute-start | bytes 786440 | tf_op jit(solution)/shard_map/ppermute | solution.py:29
  86.6 21.4 %collective-permute-start.19 = (bf16[256,1024]{1,0:T(8,128)(2,1)}, bf16[256,1024]{1,0:T(8,128)(2,1)S(1)}, u32[]{:S(2)}, u32[]{:S(2)}) collective-permute-start(bf16[256,1024]{1,0:T(8,128)(2,1)} %get-tuple-element.80), channel_id=1, source_target_pairs={{0,14},{1,15},{2,0},{3,1},{4,2},{5,3},{6,4},{7,5},{8,6},{9,7},{10,... | collective-permute-start | bytes 1572872 | tf_op jit(solution)/shard_map/ppermute | solution.py:29
  86.9 21.1 %collective-permute-start.20 = (bf16[256,1024]{1,0:T(8,128)(2,1)}, bf16[256,1024]{1,0:T(8,128)(2,1)}, u32[]{:S(2)}, u32[]{:S(2)}) collective-permute-start(bf16[256,1024]{1,0:T(8,128)(2,1)} %get-tuple-element.81), channel_id=1, source_target_pairs={{0,2},{1,3},{2,4},{3,5},{4,6},{5,7},{6,8},{7,9},{8,10},{9,11},{10,... | collective-permute-start | bytes 1572872 | tf_op jit(solution)/shard_map/ppermute | solution.py:29
  88.7 0.9 copy-start.4
  92.3 6.3 %collective-permute-start.15 = (f32[192,128]{1,0:T(8,128)}, f32[192,128]{1,0:T(8,128)S(1)}, u32[]{:S(2)}, u32[]{:S(2)}) collective-permute-start(f32[192,128]{1,0:T(8,128)} %get-tuple-element.85), channel_id=1, source_target_pairs={{0,1},{1,0},{2,3},{3,2},{4,5},{5,4},{6,7},{7,6},{8,9},{9,8},{10,11... | collective-permute-start | bytes 294920 | tf_op jit(solution)/shard_map/ppermute | solution.py:29
  93.9 6.8 %collective-permute-start.16 = (f32[192,128]{1,0:T(8,128)}, f32[192,128]{1,0:T(8,128)S(1)}, u32[]{:S(2)}, u32[]{:S(2)}) collective-permute-start(f32[192,128]{1,0:T(8,128)} %get-tuple-element.86), channel_id=1, source_target_pairs={{0,32},{16,48},{32,0},{48,16},{64,96},{80,112},{96,64},{112,80},{1... | collective-permute-start | bytes 294920 | tf_op jit(solution)/shard_map/ppermute | solution.py:29
  96.8 0.7 copy-start.13
  96.8 6.0 %collective-permute-start.17 = (f32[192,128]{1,0:T(8,128)}, f32[192,128]{1,0:T(8,128)S(1)}, u32[]{:S(2)}, u32[]{:S(2)}) collective-permute-start(f32[192,128]{1,0:T(8,128)} %get-tuple-element.87), channel_id=1, source_target_pairs={{0,33},{1,32},{2,35},{3,34},{4,37},{5,36},{6,39},{7,38},{8,41},{9,... | collective-permute-start | bytes 294920 | tf_op jit(solution)/shard_map/ppermute | solution.py:471
  104.5 15.3 %all-to-all-start.2 = ((bf16[8,192,128]{2,1,0:T(8,128)(2,1)}), bf16[8,192,128]{2,1,0:T(8,128)(2,1)S(1)}, u32[]{:S(2)}, u32[]{:S(2)}) async-start(bf16[8,192,128]{2,1,0:T(8,128)(2,1)} %broadcast_in_dim.2), calls=%async_computation.2 | async-start | bytes 786432 | tf_op jit(solution)/shard_map/all_to_all | solution.py:521
  109.4 6.5 %collective-permute-start.21 = (bf16[128,1024]{1,0:T(8,128)(2,1)S(1)}, bf16[128,1024]{1,0:T(8,128)(2,1)S(1)}, u32[]{:S(2)}, u32[]{:S(2)}) collective-permute-start(bf16[128,1024]{1,0:T(8,128)(2,1)S(1)} %slice.83), channel_id=1, source_target_pairs={{0,1},{1,0},{2,3},{3,2},{4,5},{5,4},{6,7},{7,6},{8,9},{9,8},{10,11... | collective-permute-start | bytes 786440 | tf_op jit(solution)/shard_map/ppermute | solution.py:29
  119.8 4.7 %collective-permute-start.22 = (f32[192,128]{1,0:T(8,128)S(1)}, f32[192,128]{1,0:T(8,128)S(1)}, u32[]{:S(2)}, u32[]{:S(2)}) collective-permute-start(f32[192,128]{1,0:T(8,128)S(1)} %convert_reduce_fusion), channel_id=1, source_target_pairs={{0,1},{1,0},{2,3},{3,2},{4,5},{5,4},{6,7},{7,6},{8,9},{9,8},{10,11... | collective-permute-start | bytes 294920 | tf_op jit(solution)/shard_map/ppermute | solution.py:29

commit v4 on v3

--- a/solution.py
+++ b/solution.py
@@ -444,7 +444,7 @@
         out_shape=out_shape,
         in_specs=[smem] + [spec] * len(operands),
         out_specs=[spec] * len(out_shape),
-        compiler_params=pltpu.CompilerParams(vmem_limit_bytes=VMEM_LIMIT),
+        compiler_params=pltpu.CompilerParams(vmem_limit_bytes=12 * 1024 * 1024),
     )(place, *operands)
 
 
@@ -484,12 +484,12 @@
     k_prev2, k_next2 = to_next(k_pair), to_prev(k_pair)
     q_pair, v_pair = to_pair(q_send), to_pair(v_send)
     x_cols = lax.all_to_all(x_send, "dp", 0, 0, tiled=True, axis_index_groups=flat)
-    q_pair, v_pair = after(q_pair, v_pair)
 
     dv_mid, dv_prev, dv_next, back, back_prev, back_next, up_send, probs, scaled = forward(
         place, document_lengths, versions, queries, cotangent, rotated_key_rows, ring,
         adapter_up_weight, q_pair, k_pair, prev, k_prev2, nxt, k_next2,
     )
+    v_pair, back_prev = after(v_pair, back_prev)
     from_next, from_prev = to_prev(back_prev), to_next(back_next)
     v_prev2, v_next2 = to_next(v_pair), to_prev(v_pair)
     theirs = to_pair(back[rows:] + from_next[rows:] + from_prev[rows:])

time: 127 us -> 122 us (0.961)
  starting transfers between devices: 47.7 us -> 45.5 us
  Pallas kernels: 25.1 us -> 23.6 us
  waiting for transfers between devices: 36.5 us -> 35 us
    ppermute x22, starting transfers between devices: 34.4 us -> 30.3 us  [shifted(): return lax.ppermute(block, axis, route)]
    ppermute x1, starting transfers between devices: 0.23 us -> 2.05 us  [per_device(): to_both = lambda a: lax.ppermute(a, ('dp', 'seq'), crossed)]
    pallas_call x1, Pallas kernels: 2.72 us -> 1.07 us  [simple(): pl.pallas_call(kernel, out_shape=out_shape, in_specs=[smem] + [spec] * le...]
    ppermute x22, waiting for transfers between devices: 30.4 us -> 28.8 us  [shifted(): return lax.ppermute(block, axis, route)]
    unnamed x28 -> x30, local copies, waits for them, and re-layouts: 2.96 us -> 2.34 us
  transfers between devices with their start and end apart: 26 -> 26, of which waited for: 13 -> 16; matrix products, arithmetic and copies ran while one was open for 8% -> 10% of each run, Pallas kernels for 17% -> 16%
where the time goes in v4:
time: 122 us; the launch traced here: 121 us
  starting transfers between devices  45.5 us (37%)
  waiting for transfers between devices  35 us (29%)
  Pallas kernels  23.6 us (19%)
  other arithmetic  11.2 us (9%)
  local copies, waits for them, and re-layouts  4.68 us (4%)
    ppermute x22, starting transfers between devices, shifted(): return lax.ppermute(block, axis, route)  30.3 us
    ppermute x22, waiting for transfers between devices, shifted(): return lax.ppermute(block, axis, route)  28.8 us
    pallas_call x1, Pallas kernels, forward(): pl.pallas_call(forward_kernel, grid_spec=pltpu.PrefetchScalarGridSpec(num...  9.77 us
    pallas_call x1, Pallas kernels, backward(): pl.pallas_call(backward_kernel, grid_spec=pltpu.PrefetchScalarGridSpec(nu...  8.56 us
    all_to_all x1, starting transfers between devices, per_device(): lax.all_to_all(x_send, 'dp', 0, 0, tiled=True, axis_index_groups=flat)  4.83 us
    all_to_all x1, starting transfers between devices, per_device(): lax.all_to_all(payload, 'dp', 0, 0, tiled=True, axis_index_groups=flat)  4.81 us
    pallas_call x1, Pallas kernels, prepare(): pl.pallas_call(prepare_kernel, out_shape=[jax.ShapeDtypeStruct(s, kind) f...  4.2 us
    all_to_all x1, waiting for transfers between devices, per_device(): lax.all_to_all(jnp.broadcast_to(keep[None], (count,) + keep.shape), 'seq'...  3.92 us
  transfers between devices with their start and end apart: 26, of which 16 were waited for; matrix products, arithmetic and copies ran while one was open for 10% of the time, Pallas kernels for 16%

profile of v4, /device:TPU:2, one launch (start us, length us, event | category | flops | bytes accessed | tf_op | source)
XLA Modules:
  0.0 120.9 jit_solution(17994400874767373969)
XLA Ops:
  1.3 4.2 %shard_map.128 = (bf16[128,1152]{1,0:T(8,128)(2,1)}, bf16[128,2176]{1,0:T(8,128)(2,1)}, bf16[128,2048]{1,0:T(8,128)(2,1)}, bf16[128,1024]{1,0:T(8,128)(2,1)}, bf16[8,128,512]{2,1,0:T(8,128)(2,1)}) custom-call(s32[3]{0:T(128)} %pad_add_fusion.place, bf16[128,4096]{1,0:T(8,128)(2,1)} %x.1, bf16[4096,128]{1,0:T(8,128)(2,1)} %down.1, bf16[128,2048]{1,0:T(8,128)(2,1)} %up.3, ...), custom_call_target="tpu_custom_call" | custom-call | tf_op jit(solution)/shard_map/pallas_call | solution.py:106
  5.5 1.7 %collective-permute-start = (bf16[128,1152]{1,0:T(8,128)(2,1)}, bf16[128,1152]{1,0:T(8,128)(2,1)S(1)}, u32[]{:S(2)}, u32[]{:S(2)}) collective-permute-start(bf16[128,1152]{1,0:T(8,128)(2,1)} %get-tuple-element.56), channel_id=1, source_target_pairs={{0,1},{1,0},{2,3},{3,2},{4,5},{5,4},{6,7},{7,6},{8,9},{9,8},{10,11... | collective-permute-start | bytes 884744 | tf_op jit(solution)/shard_map/ppermute | solution.py:29
  7.2 5.9 %collective-permute-start.4 = (bf16[128,2176]{1,0:T(8,128)(2,1)}, bf16[128,2176]{1,0:T(8,128)(2,1)S(1)}, u32[]{:S(2)}, u32[]{:S(2)}) collective-permute-start(bf16[128,2176]{1,0:T(8,128)(2,1)} %get-tuple-element.61.l_own.v_own), channel_id=1, source_target_pairs={{0,14},{1,15},{2,0},{3,1},{4,2},{5,3},{6,4},{7,5},{8,6},{9,7},{10,... | collective-permute-start | bytes 1671176 | tf_op jit(solution)/shard_map/ppermute | solution.py:29
  13.0 1.5 %collective-permute-done.k_pair.l_pair = bf16[128,1152]{1,0:T(8,128)(2,1)S(1)} collective-permute-done((bf16[128,1152]{1,0:T(8,128)(2,1)}, bf16[128,1152]{1,0:T(8,128)(2,1)S(1)}, u32[]{:S(2)}, u32[]{:S(2)}) %collective-permute-start) | collective-permute-done | bytes 294944 | tf_op jit(solution)/shard_map/ppermute | solution.py:29
  14.5 1.6 %collective-permute-start.1 = (bf16[128,2048]{1,0:T(8,128)(2,1)}, bf16[128,2048]{1,0:T(8,128)(2,1)S(1)}, u32[]{:S(2)}, u32[]{:S(2)}) collective-permute-start(bf16[128,2048]{1,0:T(8,128)(2,1)} %get-tuple-element.59), channel_id=1, source_target_pairs={{0,1},{1,0},{2,3},{3,2},{4,5},{5,4},{6,7},{7,6},{8,9},{9,8},{10,11... | collective-permute-start | bytes 1572872 | tf_op jit(solution)/shard_map/ppermute | solution.py:29
  16.1 4.8 %all-to-all-start = ((bf16[8,128,512]{2,1,0:T(8,128)(2,1)}), bf16[8,128,512]{2,1,0:T(8,128)(2,1)S(1)}, u32[]{:S(2)}, u32[]{:S(2)}) async-start(bf16[8,128,512]{2,1,0:T(8,128)(2,1)} %get-tuple-element.68), calls=%async_computation | async-start | bytes 2097152 | tf_op jit(solution)/shard_map/all_to_all | solution.py:486
  21.0 5.9 %collective-permute-start.5 = (bf16[128,1152]{1,0:T(8,128)(2,1)S(1)}, bf16[128,1152]{1,0:T(8,128)(2,1)S(1)}, u32[]{:S(2)}, u32[]{:S(2)}) collective-permute-start(bf16[128,1152]{1,0:T(8,128)(2,1)S(1)} %collective-permute-done.k_pair.l_pair), channel_id=1, source_target_pairs={{0,14},{1,15},{2,0},{3,1},{4,2},{5,3},{6,4},{7,5},{8,6},{9,7},{10,... | collective-permute-start | bytes 884744 | tf_op jit(solution)/shard_map/ppermute | solution.py:29
  27.4 0.9 collective-permute-done.2.k_prev.l_prev.v_prev
  28.3 5.1 %collective-permute-done.5.k_next2.l_next2 = bf16[128,1152]{1,0:T(8,128)(2,1)S(1)} collective-permute-done((bf16[128,1152]{1,0:T(8,128)(2,1)S(1)}, bf16[128,1152]{1,0:T(8,128)(2,1)S(1)}, u32[]{:S(2)}, u32[]{:S(2)}) %collective-permute-start.5) | collective-permute-done | bytes 294944 | tf_op jit(solution)/shard_map/ppermute | solution.py:29
  33.4 3.4 %collective-permute-done.3.k_prev2.l_prev2 = bf16[128,1152]{1,0:T(8,128)(2,1)S(1)} collective-permute-done((bf16[128,1152]{1,0:T(8,128)(2,1)S(1)}, bf16[128,1152]{1,0:T(8,128)(2,1)S(1)}, u32[]{:S(2)}, u32[]{:S(2)}) %collective-permute-start.3) | collective-permute-done | bytes 294944 | tf_op jit(solution)/shard_map/ppermute | solution.py:29
  36.9 0.7 copy-done.6
  37.6 0.8 copy-done.3
  38.3 9.8 %shard_map.129 = (bf16[256,1024]{1,0:T(8,128)(2,1)}, bf16[256,1024]{1,0:T(8,128)(2,1)}, bf16[256,1024]{1,0:T(8,128)(2,1)}, f32[256,128]{1,0:T(8,128)}, f32[256,1...) custom-call(s32[3]{0:T(128)} %pad_add_fusion.place, ...), custom_call_target="tpu_custom_call" | custom-call | flops 1677721600 | bytes 12582912 | tf_op jit(solution)/shard_map/pallas_call | solution.py:350
  48.2 0.7 collective-permute-start.7
  48.9 1.6 %collective-permute-start.8 = (f32[256,128]{1,0:T(8,128)}, f32[256,128]{1,0:T(8,128)S(1)}, u32[]{:S(2)}, u32[]{:S(2)}) collective-permute-start(f32[256,128]{1,0:T(8,128)} %get-tuple-element.66), channel_id=1, source_target_pairs={{0,2},{1,3},{2,4},{3,5},{4,6},{5,7},{6,8},{7,9},{8,10},{9,11},{10,... | collective-permute-start | bytes 393224 | tf_op jit(solution)/shard_map/ppermute | solution.py:29
  50.4 1.6 %collective-permute-start.11 = (bf16[128,1024]{1,0:T(8,128)(2,1)S(1)}, bf16[128,1024]{1,0:T(8,128)(2,1)S(1)}, u32[]{:S(2)}, u32[]{:S(2)}) collective-permute-start(bf16[128,1024]{1,0:T(8,128)(2,1)S(1)} %collective-permute-done.6.v_pair), channel_id=1, source_target_pairs={{0,14},{1,15},{2,0},{3,1},{4,2},{5,3},{6,4},{7,5},{8,6},{9,7},{10,... | collective-permute-start | bytes 786440 | tf_op jit(solution)/shard_map/ppermute | solution.py:29
  52.5 2.6 %collective-permute-done.7 = f32[256,128]{1,0:T(8,128)S(1)} collective-permute-done((f32[256,128]{1,0:T(8,128)}, f32[256,128]{1,0:T(8,128)S(1)}, u32[]{:S(2)}, u32[]{:S(2)}) %collective-permute-start.7) | collective-permute-done | bytes 131104 | tf_op jit(solution)/shard_map/ppermute | solution.py:29
  55.1 1.1 collective-permute-done.8
  56.2 1.5 %slice_add_fusion.2 = f32[128,128]{1,0:T(8,128)} fusion(f32[256,128]{1,0:T(8,128)S(1)} %collective-permute-done.8, f32[256,128]{1,0:T(8,128)S(1)} %collective-permute-done.7, f32[256,128]{1,0:T(8,128)} %get-tuple-element.62), kind=kLoop, calls=%fused_computation.19 | loop fusion | flops 32768 | bytes 262144 | tf_op jit(solution)/shard_map/add | solution.py:495
  58.1 2.0 %collective-permute-start.13 = (bf16[256,1024]{1,0:T(8,128)(2,1)}, bf16[256,1024]{1,0:T(8,128)(2,1)S(1)}, u32[]{:S(2)}, u32[]{:S(2)}) collective-permute-start(bf16[256,1024]{1,0:T(8,128)(2,1)} %get-tuple-element.75), channel_id=1, source_target_pairs={{0,2},{1,3},{2,4},{3,5},{4,6},{5,7},{6,8},{7,9},{8,10},{9,11},{10,... | collective-permute-start | bytes 1572872 | tf_op jit(solution)/shard_map/ppermute | solution.py:29
  60.2 2.1 %collective-permute-done.9 = f32[128,128]{1,0:T(8,128)} collective-permute-done((f32[128,128]{1,0:T(8,128)}, f32[128,128]{1,0:T(8,128)}, u32[]{:S(2)}, u32[]{:S(2)}) %collective-permute-start.9) | collective-permute-done | bytes 65568 | tf_op jit(solution)/shard_map/ppermute | solution.py:29
  62.5 1.0 fusion.1
  63.6 0.8 broadcast_dynamic-update-slice_fusion
  64.4 4.8 %all-to-all-start.1 = ((bf16[8,128,384]{2,1,0:T(8,128)(2,1)}), bf16[8,128,384]{2,1,0:T(8,128)(2,1)S(1)}, u32[]{:S(2)}, u32[]{:S(2)}) async-start(bf16[8,128,384]{2,1,0:T(8,128)(2,1)} %broadcast_dynamic-update-slice_fusion), calls=%async_computation.1 | async-start | bytes 1572864 | tf_op jit(solution)/shard_map/all_to_all | solution.py:499
  69.2 0.7 collective-permute-done.12
  69.9 2.2 %collective-permute-done.13 = bf16[256,1024]{1,0:T(8,128)(2,1)S(1)} collective-permute-done((bf16[256,1024]{1,0:T(8,128)(2,1)}, bf16[256,1024]{1,0:T(8,128)(2,1)S(1)}, u32[]{:S(2)}, u32[]{:S(2)}) %collective-permute-start.13) | collective-permute-done | bytes 524320 | tf_op jit(solution)/shard_map/ppermute | solution.py:29
  72.1 0.8 copy-done.9
  72.9 1.3 %add_convert_fusion.1 = bf16[256,1024]{1,0:T(8,128)(2,1)S(1)} fusion(bf16[256,1024]{1,0:T(8,128)(2,1)} %copy-done.9, bf16[256,1024]{1,0:T(8,128)(2,1)S(1)} %collective-permute-done.12, bf16[256,1024]{1,0:T(8,128)(2,1)S(1)} %copy-done.8), kind=kLoop, calls=%fused_computation.1 | loop fusion | flops 1572864 | bytes 2097152 | tf_op jit(solution)/shard_map/convert_element_type | solution.py:501
  74.2 0.7 slice.70
  75.4 8.6 %shard_map.130 = (bf16[128,1024]{1,0:T(8,128)(2,1)}, bf16[128,1024]{1,0:T(8,128)(2,1)}, bf16[256,1024]{1,0:T(8,128)(2,1)}, bf16[256,1024]{1,0:T(8,128)(2,1)}, bf16[256,1024]{1,0:T(8,128)(2,1)}) custom-call(s32[3]{0:T(128)} %pad_add_fusion.place, bf16[128,2048]{1,0:T(8,128)(2,1)} %q_own.3, bf16[128,2048]{1,0:T(8,128)(2,1)} %copy-done.3, ...), custom_call_target="tpu_custom_call" | custom-call | flops 1677721600 | bytes 12582912 | tf_op jit(solution)/shard_map/pallas_call | solution.py:392
  84.0 1.7 %collective-permute-start.18 = (bf16[128,1024]{1,0:T(8,128)(2,1)}, bf16[128,1024]{1,0:T(8,128)(2,1)}, u32[]{:S(2)}, u32[]{:S(2)}) collective-permute-start(bf16[128,1024]{1,0:T(8,128)(2,1)} %get-tuple-element.90), channel_id=1, source_target_pairs={{0,1},{1,0},{2,3},{3,2},{4,5},{5,4},{6,7},{7,6},{8,9},{9,8},{10,11... | collective-permute-start | bytes 786440 | tf_op jit(solution)/shard_map/ppermute | solution.py:29
  85.6 2.0 %collective-permute-start.20 = (bf16[256,1024]{1,0:T(8,128)(2,1)}, bf16[256,1024]{1,0:T(8,128)(2,1)}, u32[]{:S(2)}, u32[]{:S(2)}) collective-permute-start(bf16[256,1024]{1,0:T(8,128)(2,1)} %get-tuple-element.81), channel_id=1, source_target_pairs={{0,2},{1,3},{2,4},{3,5},{4,6},{5,7},{6,8},{7,9},{8,10},{9,11},{10,... | collective-permute-start | bytes 1572872 | tf_op jit(solution)/shard_map/ppermute | solution.py:29
  87.7 1.1 shard_map.131
  89.3 3.2 %collective-permute-start.16 = (f32[192,128]{1,0:T(8,128)S(1)}, f32[192,128]{1,0:T(8,128)S(1)}, u32[]{:S(2)}, u32[]{:S(2)}) collective-permute-start(f32[192,128]{1,0:T(8,128)S(1)} %get-tuple-element.86), channel_id=1, source_target_pairs={{0,32},{16,48},{32,0},{48,16},{64,96},{80,112},{96,64},{112,80},{1... | collective-permute-start | bytes 294920 | tf_op jit(solution)/shard_map/ppermute | solution.py:29
  92.8 2.1 %collective-permute-start.17 = (f32[192,128]{1,0:T(8,128)S(1)}, f32[192,128]{1,0:T(8,128)S(1)}, u32[]{:S(2)}, u32[]{:S(2)}) collective-permute-start(f32[192,128]{1,0:T(8,128)S(1)} %get-tuple-element.87), channel_id=1, source_target_pairs={{0,33},{1,32},{2,35},{3,34},{4,37},{5,36},{6,39},{7,38},{8,41},{9,... | collective-permute-start | bytes 294920 | tf_op jit(solution)/shard_map/ppermute | solution.py:471
  94.9 1.1 broadcast_select_fusion.3
  96.3 2.3 %collective-permute-done.17 = f32[192,128]{1,0:T(8,128)S(1)} collective-permute-done((f32[192,128]{1,0:T(8,128)S(1)}, f32[192,128]{1,0:T(8,128)S(1)}, u32[]{:S(2)}, u32[]{:S(2)}) %collective-permute-start.17) | collective-permute-done | bytes 98336 | tf_op jit(solution)/shard_map/ppermute | solution.py:471
  98.7 0.8 broadcast_in_dim.2
  99.5 3.5 %all-to-all-start.2 = ((bf16[8,192,128]{2,1,0:T(8,128)(2,1)}), bf16[8,192,128]{2,1,0:T(8,128)(2,1)S(1)}, u32[]{:S(2)}, u32[]{:S(2)}) async-start(bf16[8,192,128]{2,1,0:T(8,128)(2,1)} %broadcast_in_dim.2), calls=%async_computation.2 | async-start | bytes 786432 | tf_op jit(solution)/shard_map/all_to_all | solution.py:521
  103.0 1.3 %add_convert_fusion = bf16[256,1024]{1,0:T(8,128)(2,1)S(1)} fusion(bf16[256,1024]{1,0:T(8,128)(2,1)} %collective-permute-done.20, bf16[256,1024]{1,0:T(8,128)(2,1)S(1)} %collective-permute-done.19, bf16[256,1024]{1,0:T(8,128)(2,1)S(1)} %copy-done.7), kind=kLoop, calls=%fused_computation | loop fusion | flops 1572864 | bytes 2097152 | tf_op jit(solution)/shard_map/convert_element_type | solution.py:501
  104.4 1.0 broadcast_select_fusion.5
  105.4 1.1 pad_maximum_fusion
  106.5 4.3 %collective-permute-done.21 = bf16[128,1024]{1,0:T(8,128)(2,1)S(1)} collective-permute-done((bf16[128,1024]{1,0:T(8,128)(2,1)S(1)}, bf16[128,1024]{1,0:T(8,128)(2,1)S(1)}, u32[]{:S(2)}, u32[]{:S(2)}) %collective-permute-start.21) | collective-permute-done | bytes 262176 | tf_op jit(solution)/shard_map/ppermute | solution.py:29
  110.8 3.9 %all-to-all-done.2 = bf16[8,192,128]{2,1,0:T(8,128)(2,1)S(1)} async-done(((bf16[8,192,128]{2,1,0:T(8,128)(2,1)}), bf16[8,192,128]{2,1,0:T(8,128)(2,1)S(1)}, u32[]{:S(2)}, u32[]{:S(2)}) %all-to-all-start.2) | async-done | bytes 393248 | tf_op jit(solution)/shard_map/all_to_all | solution.py:521
  114.9 0.8 pad_maximum_fusion.2
  115.7 3.8 %collective-permute-done.22 = f32[192,128]{1,0:T(8,128)S(1)} collective-permute-done((f32[192,128]{1,0:T(8,128)S(1)}, f32[192,128]{1,0:T(8,128)S(1)}, u32[]{:S(2)}, u32[]{:S(2)}) %collective-permute-start.22) | collective-permute-done | bytes 98336 | tf_op jit(solution)/shard_map/ppermute | solution.py:29
  119.6 0.7 pad_maximum_fusion.3
  120.2 0.6 pad_maximum_fusion.4
  (61 shorter events, 4.4 us)
Async XLA Ops:
  5.5 9.0 %collective-permute-start = (bf16[128,1152]{1,0:T(8,128)(2,1)}, bf16[128,1152]{1,0:T(8,128)(2,1)S(1)}, u32[]{:S(2)}, u32[]{:S(2)}) collective-permute-start(bf16[128,1152]{1,0:T(8,128)(2,1)} %get-tuple-element.56), channel_id=1, source_target_pairs={{0,1},{1,0},{2,3},{3,2},{4,5},{5,4},{6,7},{7,6},{8,9},{9,8},{10,11... | collective-permute-start | bytes 884744 | tf_op jit(solution)/shard_map/ppermute | solution.py:29
  7.2 19.7 %collective-permute-start.4 = (bf16[128,2176]{1,0:T(8,128)(2,1)}, bf16[128,2176]{1,0:T(8,128)(2,1)S(1)}, u32[]{:S(2)}, u32[]{:S(2)}) collective-permute-start(bf16[128,2176]{1,0:T(8,128)(2,1)} %get-tuple-element.61.l_own.v_own), channel_id=1, source_target_pairs={{0,14},{1,15},{2,0},{3,1},{4,2},{5,3},{6,4},{7,5},{8,6},{9,7},{10,... | collective-permute-start | bytes 1671176 | tf_op jit(solution)/shard_map/ppermute | solution.py:29
  13.0 15.2 %collective-permute-start.2 = (bf16[128,2176]{1,0:T(8,128)(2,1)}, bf16[128,2176]{1,0:T(8,128)(2,1)S(1)}, u32[]{:S(2)}, u32[]{:S(2)}) collective-permute-start(bf16[128,2176]{1,0:T(8,128)(2,1)} %get-tuple-element.61.l_own.v_own), channel_id=1, source_target_pairs={{0,2},{1,3},{2,4},{3,5},{4,6},{5,7},{6,8},{7,9},{8,10},{9,11},{10,... | collective-permute-start | bytes 1671176 | tf_op jit(solution)/shard_map/ppermute | solution.py:29
  14.5 22.3 %copy-start.4 = (bf16[128,1152]{1,0:T(8,128)(2,1)}, bf16[128,1152]{1,0:T(8,128)(2,1)S(1)}, u32[]{:S(2)}) copy-start(bf16[128,1152]{1,0:T(8,128)(2,1)S(1)} %collective-permute-done.k_pair.l_pair) | copy-start | bytes 884740
  14.5 22.3 %collective-permute-start.1 = (bf16[128,2048]{1,0:T(8,128)(2,1)}, bf16[128,2048]{1,0:T(8,128)(2,1)S(1)}, u32[]{:S(2)}, u32[]{:S(2)}) collective-permute-start(bf16[128,2048]{1,0:T(8,128)(2,1)} %get-tuple-element.59), channel_id=1, source_target_pairs={{0,1},{1,0},{2,3},{3,2},{4,5},{5,4},{6,7},{7,6},{8,9},{9,8},{10,11... | collective-permute-start | bytes 1572872 | tf_op jit(solution)/shard_map/ppermute | solution.py:29
  16.1 44.0 %all-to-all-start = ((bf16[8,128,512]{2,1,0:T(8,128)(2,1)}), bf16[8,128,512]{2,1,0:T(8,128)(2,1)S(1)}, u32[]{:S(2)}, u32[]{:S(2)}) async-start(bf16[8,128,512]{2,1,0:T(8,128)(2,1)} %get-tuple-element.68), calls=%async_computation | async-start | bytes 2097152 | tf_op jit(solution)/shard_map/all_to_all | solution.py:486
  21.0 12.4 %collective-permute-start.5 = (bf16[128,1152]{1,0:T(8,128)(2,1)S(1)}, bf16[128,1152]{1,0:T(8,128)(2,1)S(1)}, u32[]{:S(2)}, u32[]{:S(2)}) collective-permute-start(bf16[128,1152]{1,0:T(8,128)(2,1)S(1)} %collective-permute-done.k_pair.l_pair), channel_id=1, source_target_pairs={{0,14},{1,15},{2,0},{3,1},{4,2},{5,3},{6,4},{7,5},{8,6},{9,7},{10,... | collective-permute-start | bytes 884744 | tf_op jit(solution)/shard_map/ppermute | solution.py:29
  26.8 10.0 %collective-permute-start.3 = (bf16[128,1152]{1,0:T(8,128)(2,1)S(1)}, bf16[128,1152]{1,0:T(8,128)(2,1)S(1)}, u32[]{:S(2)}, u32[]{:S(2)}) collective-permute-start(bf16[128,1152]{1,0:T(8,128)(2,1)S(1)} %collective-permute-done.k_pair.l_pair), channel_id=1, source_target_pairs={{0,2},{1,3},{2,4},{3,5},{4,6},{5,7},{6,8},{7,9},{8,10},{9,11},{10,... | collective-permute-start | bytes 884744 | tf_op jit(solution)/shard_map/ppermute | solution.py:29
  26.8 10.0 %copy-start.1 = (bf16[128,2176]{1,0:T(8,128)(2,1)}, bf16[128,2176]{1,0:T(8,128)(2,1)S(1)}, u32[]{:S(2)}) copy-start(bf16[128,2176]{1,0:T(8,128)(2,1)S(1)} %collective-permute-done.4.k_next.l_next.v_next) | copy-start | bytes 1671172
  26.8 21.3 %collective-permute-start.6 = (bf16[128,1024]{1,0:T(8,128)(2,1)}, bf16[128,1024]{1,0:T(8,128)(2,1)S(1)}, u32[]{:S(2)}, u32[]{:S(2)}) collective-permute-start(bf16[128,1024]{1,0:T(8,128)(2,1)} %get-tuple-element.63), channel_id=1, source_target_pairs={{0,1},{1,0},{2,3},{3,2},{4,5},{5,4},{6,7},{7,6},{8,9},{9,8},{10,11... | collective-permute-start | bytes 786440 | tf_op jit(solution)/shard_map/ppermute | solution.py:29
  28.2 8.6 %copy-start.2 = (bf16[128,2176]{1,0:T(8,128)(2,1)}, bf16[128,2176]{1,0:T(8,128)(2,1)S(1)}, u32[]{:S(2)}) copy-start(bf16[128,2176]{1,0:T(8,128)(2,1)S(1)} %collective-permute-done.2.k_prev.l_prev.v_prev) | copy-start | bytes 1671172
  33.4 3.4 %copy-start.5 = (bf16[128,1152]{1,0:T(8,128)(2,1)}, bf16[128,1152]{1,0:T(8,128)(2,1)S(1)}, u32[]{:S(2)}) copy-start(bf16[128,1152]{1,0:T(8,128)(2,1)S(1)} %collective-permute-done.5.k_next2.l_next2) | copy-start | bytes 884740
  36.8 0.7 copy-start.6
  37.6 0.8 copy-start.3
  48.1 24.8 %copy-start.8 = (bf16[256,1024]{1,0:T(8,128)(2,1)S(1)}, bf16[256,1024]{1,0:T(8,128)(2,1)}, u32[]{:S(2)}) copy-start(bf16[256,1024]{1,0:T(8,128)(2,1)} %get-tuple-element.73) | copy-start | bytes 1572868
  48.1 16.2 %copy-start.10 = (bf16[128,1024]{1,0:T(8,128)(2,1)}, bf16[128,1024]{1,0:T(8,128)(2,1)S(1)}, u32[]{:S(2)}) copy-start(bf16[128,1024]{1,0:T(8,128)(2,1)S(1)} %collective-permute-done.6.v_pair) | copy-start | bytes 786436
  48.2 6.9 %collective-permute-start.7 = (f32[256,128]{1,0:T(8,128)}, f32[256,128]{1,0:T(8,128)S(1)}, u32[]{:S(2)}, u32[]{:S(2)}) collective-permute-start(f32[256,128]{1,0:T(8,128)} %get-tuple-element.65), channel_id=1, source_target_pairs={{0,14},{1,15},{2,0},{3,1},{4,2},{5,3},{6,4},{7,5},{8,6},{9,7},{10,... | collective-permute-start | bytes 393224 | tf_op jit(solution)/shard_map/ppermute | solution.py:29
  48.9 7.3 %collective-permute-start.8 = (f32[256,128]{1,0:T(8,128)}, f32[256,128]{1,0:T(8,128)S(1)}, u32[]{:S(2)}, u32[]{:S(2)}) collective-permute-start(f32[256,128]{1,0:T(8,128)} %get-tuple-element.66), channel_id=1, source_target_pairs={{0,2},{1,3},{2,4},{3,5},{4,6},{5,7},{6,8},{7,9},{8,10},{9,11},{10,... | collective-permute-start | bytes 393224 | tf_op jit(solution)/shard_map/ppermute | solution.py:29
  50.4 11.9 %collective-permute-start.11 = (bf16[128,1024]{1,0:T(8,128)(2,1)S(1)}, bf16[128,1024]{1,0:T(8,128)(2,1)S(1)}, u32[]{:S(2)}, u32[]{:S(2)}) collective-permute-start(bf16[128,1024]{1,0:T(8,128)(2,1)S(1)} %collective-permute-done.6.v_pair), channel_id=1, source_target_pairs={{0,14},{1,15},{2,0},{3,1},{4,2},{5,3},{6,4},{7,5},{8,6},{9,7},{10,... | collective-permute-start | bytes 786440 | tf_op jit(solution)/shard_map/ppermute | solution.py:29
  52.1 10.5 %collective-permute-start.10 = (bf16[128,1024]{1,0:T(8,128)(2,1)S(1)}, bf16[128,1024]{1,0:T(8,128)(2,1)S(1)}, u32[]{:S(2)}, u32[]{:S(2)}) collective-permute-start(bf16[128,1024]{1,0:T(8,128)(2,1)S(1)} %collective-permute-done.6.v_pair), channel_id=1, source_target_pairs={{0,2},{1,3},{2,4},{3,5},{4,6},{5,7},{6,8},{7,9},{8,10},{9,11},{10,... | collective-permute-start | bytes 786440 | tf_op jit(solution)/shard_map/ppermute | solution.py:29
  55.1 7.2 %copy-start.13 = (f32[256,128]{1,0:T(8,128)}, f32[256,128]{1,0:T(8,128)S(1)}, u32[]{:S(2)}) copy-start(f32[256,128]{1,0:T(8,128)S(1)} %collective-permute-done.7) | copy-start | bytes 393220
  56.2 2.0 %copy-start.14 = (f32[256,128]{1,0:T(8,128)}, f32[256,128]{1,0:T(8,128)S(1)}, u32[]{:S(2)}) copy-start(f32[256,128]{1,0:T(8,128)S(1)} %collective-permute-done.8) | copy-start | bytes 393220
  57.7 4.6 %collective-permute-start.9 = (f32[128,128]{1,0:T(8,128)}, f32[128,128]{1,0:T(8,128)}, u32[]{:S(2)}, u32[]{:S(2)}) collective-permute-start(f32[128,128]{1,0:T(8,128)} %slice_add_fusion.2), channel_id=1, source_target_pairs={{0,1},{1,0},{2,3},{3,2},{4,5},{5,4},{6,7},{7,6},{8,9},{9,8},{10,11... | collective-permute-start | bytes 196616 | tf_op jit(solution)/shard_map/ppermute | solution.py:29
  58.1 11.8 %collective-permute-start.12 = (bf16[256,1024]{1,0:T(8,128)(2,1)}, bf16[256,1024]{1,0:T(8,128)(2,1)S(1)}, u32[]{:S(2)}, u32[]{:S(2)}) collective-permute-start(bf16[256,1024]{1,0:T(8,128)(2,1)} %get-tuple-element.74), channel_id=1, source_target_pairs={{0,14},{1,15},{2,0},{3,1},{4,2},{5,3},{6,4},{7,5},{8,6},{9,7},{10,... | collective-permute-start | bytes 1572872 | tf_op jit(solution)/shard_map/ppermute | solution.py:29
  58.1 14.0 %collective-permute-start.13 = (bf16[256,1024]{1,0:T(8,128)(2,1)}, bf16[256,1024]{1,0:T(8,128)(2,1)S(1)}, u32[]{:S(2)}, u32[]{:S(2)}) collective-permute-start(bf16[256,1024]{1,0:T(8,128)(2,1)} %get-tuple-element.75), channel_id=1, source_target_pairs={{0,2},{1,3},{2,4},{3,5},{4,6},{5,7},{6,8},{7,9},{8,10},{9,11},{10,... | collective-permute-start | bytes 1572872 | tf_op jit(solution)/shard_map/ppermute | solution.py:29
  62.3 2.1 %copy-start.11 = (bf16[128,1024]{1,0:T(8,128)(2,1)}, bf16[128,1024]{1,0:T(8,128)(2,1)S(1)}, u32[]{:S(2)}) copy-start(bf16[128,1024]{1,0:T(8,128)(2,1)S(1)} %collective-permute-done.11.v_next2) | copy-start | bytes 786436
  62.5 1.8 %copy-start.12 = (bf16[128,1024]{1,0:T(8,128)(2,1)}, bf16[128,1024]{1,0:T(8,128)(2,1)S(1)}, u32[]{:S(2)}) copy-start(bf16[128,1024]{1,0:T(8,128)(2,1)S(1)} %collective-permute-done.10.v_prev2) | copy-start | bytes 786436
  64.4 23.3 %all-to-all-start.1 = ((bf16[8,128,384]{2,1,0:T(8,128)(2,1)}), bf16[8,128,384]{2,1,0:T(8,128)(2,1)S(1)}, u32[]{:S(2)}, u32[]{:S(2)}) async-start(bf16[8,128,384]{2,1,0:T(8,128)(2,1)} %broadcast_dynamic-update-slice_fusion), calls=%async_computation.1 | async-start | bytes 1572864 | tf_op jit(solution)/shard_map/all_to_all | solution.py:499
  72.1 0.8 copy-start.9
  74.9 12.7 %collective-permute-start.14 = (bf16[128,1024]{1,0:T(8,128)(2,1)}, bf16[128,1024]{1,0:T(8,128)(2,1)}, u32[]{:S(2)}, u32[]{:S(2)}) collective-permute-start(bf16[128,1024]{1,0:T(8,128)(2,1)} %slice.70), channel_id=1, source_target_pairs={{0,1},{1,0},{2,3},{3,2},{4,5},{5,4},{6,7},{7,6},{8,9},{9,8},{10,11... | collective-permute-start | bytes 786440 | tf_op jit(solution)/shard_map/ppermute | solution.py:29
  75.4 12.3 %copy-start = (s32[3]{0:T(128)S(1)}, s32[3]{0:T(128)}, u32[]{:S(2)}) copy-start(s32[3]{0:T(128)} %pad_add_fusion.place) | copy-start | bytes 40
  83.9 19.0 %copy-start.7 = (bf16[256,1024]{1,0:T(8,128)(2,1)S(1)}, bf16[256,1024]{1,0:T(8,128)(2,1)}, u32[]{:S(2)}) copy-start(bf16[256,1024]{1,0:T(8,128)(2,1)} %get-tuple-element.92) | copy-start | bytes 1572868
  84.0 8.9 %collective-permute-start.18 = (bf16[128,1024]{1,0:T(8,128)(2,1)}, bf16[128,1024]{1,0:T(8,128)(2,1)}, u32[]{:S(2)}, u32[]{:S(2)}) collective-permute-start(bf16[128,1024]{1,0:T(8,128)(2,1)} %get-tuple-element.90), channel_id=1, source_target_pairs={{0,1},{1,0},{2,3},{3,2},{4,5},{5,4},{6,7},{7,6},{8,9},{9,8},{10,11... | collective-permute-start | bytes 786440 | tf_op jit(solution)/shard_map/ppermute | solution.py:29
  85.6 17.3 %collective-permute-start.19 = (bf16[256,1024]{1,0:T(8,128)(2,1)}, bf16[256,1024]{1,0:T(8,128)(2,1)S(1)}, u32[]{:S(2)}, u32[]{:S(2)}) collective-permute-start(bf16[256,1024]{1,0:T(8,128)(2,1)} %get-tuple-element.80), channel_id=1, source_target_pairs={{0,14},{1,15},{2,0},{3,1},{4,2},{5,3},{6,4},{7,5},{8,6},{9,7},{10,... | collective-permute-start | bytes 1572872 | tf_op jit(solution)/shard_map/ppermute | solution.py:29
  85.6 17.3 %collective-permute-start.20 = (bf16[256,1024]{1,0:T(8,128)(2,1)}, bf16[256,1024]{1,0:T(8,128)(2,1)}, u32[]{:S(2)}, u32[]{:S(2)}) collective-permute-start(bf16[256,1024]{1,0:T(8,128)(2,1)} %get-tuple-element.81), channel_id=1, source_target_pairs={{0,2},{1,3},{2,4},{3,5},{4,6},{5,7},{6,8},{7,9},{8,10},{9,11},{10,... | collective-permute-start | bytes 1572872 | tf_op jit(solution)/shard_map/ppermute | solution.py:29
  88.7 7.2 %collective-permute-start.15 = (f32[192,128]{1,0:T(8,128)S(1)}, f32[192,128]{1,0:T(8,128)S(1)}, u32[]{:S(2)}, u32[]{:S(2)}) collective-permute-start(f32[192,128]{1,0:T(8,128)S(1)} %get-tuple-element.85), channel_id=1, source_target_pairs={{0,1},{1,0},{2,3},{3,2},{4,5},{5,4},{6,7},{7,6},{8,9},{9,8},{10,11... | collective-permute-start | bytes 294920 | tf_op jit(solution)/shard_map/ppermute | solution.py:29
  89.3 7.1 %collective-permute-start.16 = (f32[192,128]{1,0:T(8,128)S(1)}, f32[192,128]{1,0:T(8,128)S(1)}, u32[]{:S(2)}, u32[]{:S(2)}) collective-permute-start(f32[192,128]{1,0:T(8,128)S(1)} %get-tuple-element.86), channel_id=1, source_target_pairs={{0,32},{16,48},{32,0},{48,16},{64,96},{80,112},{96,64},{112,80},{1... | collective-permute-start | bytes 294920 | tf_op jit(solution)/shard_map/ppermute | solution.py:29
  92.8 5.8 %collective-permute-start.17 = (f32[192,128]{1,0:T(8,128)S(1)}, f32[192,128]{1,0:T(8,128)S(1)}, u32[]{:S(2)}, u32[]{:S(2)}) collective-permute-start(f32[192,128]{1,0:T(8,128)S(1)} %get-tuple-element.87), channel_id=1, source_target_pairs={{0,33},{1,32},{2,35},{3,34},{4,37},{5,36},{6,39},{7,38},{8,41},{9,... | collective-permute-start | bytes 294920 | tf_op jit(solution)/shard_map/ppermute | solution.py:471
  99.5 15.3 %all-to-all-start.2 = ((bf16[8,192,128]{2,1,0:T(8,128)(2,1)}), bf16[8,192,128]{2,1,0:T(8,128)(2,1)S(1)}, u32[]{:S(2)}, u32[]{:S(2)}) async-start(bf16[8,192,128]{2,1,0:T(8,128)(2,1)} %broadcast_in_dim.2), calls=%async_computation.2 | async-start | bytes 786432 | tf_op jit(solution)/shard_map/all_to_all | solution.py:521
  104.3 6.5 %collective-permute-start.21 = (bf16[128,1024]{1,0:T(8,128)(2,1)S(1)}, bf16[128,1024]{1,0:T(8,128)(2,1)S(1)}, u32[]{:S(2)}, u32[]{:S(2)}) collective-permute-start(bf16[128,1024]{1,0:T(8,128)(2,1)S(1)} %slice.83), channel_id=1, source_target_pairs={{0,1},{1,0},{2,3},{3,2},{4,5},{5,4},{6,7},{7,6},{8,9},{9,8},{10,11... | collective-permute-start | bytes 786440 | tf_op jit(solution)/shard_map/ppermute | solution.py:29
  114.8 4.7 %collective-permute-start.22 = (f32[192,128]{1,0:T(8,128)S(1)}, f32[192,128]{1,0:T(8,128)S(1)}, u32[]{:S(2)}, u32[]{:S(2)}) collective-permute-start(f32[192,128]{1,0:T(8,128)S(1)} %convert_reduce_fusion), channel_id=1, source_target_pairs={{0,1},{1,0},{2,3},{3,2},{4,5},{5,4},{6,7},{7,6},{8,9},{9,8},{10,11... | collective-permute-start | bytes 294920 | tf_op jit(solution)/shard_map/ppermute | solution.py:29
